TPU v7x, 32 devices: a whole 2x2x4 slice. The times are simulated.
32 devices in a mesh: groups: 2 (over x), expert: 8 (over z, y), replica: 2 (over core).
Axes of the slice: x: 2, y: 2, z: 4, core: 2. Of those that a mesh axis runs over, the one named last changes fastest.
Arguments:
- tiles: bfloat16 [1024, 12, 12, 128], P(('groups', 'expert', 'replica')), parts along dimension 0, may hold values from -6 to 6
- route: int32 [1024], P(('groups', 'expert', 'replica')), parts along dimension 0, may hold values from 0 to 7, as said below
- gate: float32 [1024], P(('groups', 'expert', 'replica')), parts along dimension 0, may hold values from 0.25 to 1
- conv_first: bfloat16 [8, 3, 3, 128, 128], P('expert'), may hold values from -0.1875 to 0.1875
- conv_second: bfloat16 [8, 3, 3, 128, 128], P('expert'), may hold values from -0.1875 to 0.1875
- cotangent: bfloat16 [1024, 8, 8, 128], P(('groups', 'expert', 'replica')), parts along dimension 0, may hold values from -6 to 6
Outputs:
- output: bfloat16 [1024, 8, 8, 128], P(('groups', 'expert', 'replica')), parts along dimension 0
- tiles_grad: bfloat16 [1024, 12, 12, 128], P(('groups', 'expert', 'replica')), parts along dimension 0
- first_grad: float32 [16, 3, 3, 128, 128], P(('groups', 'expert')), parts along dimension 0
- second_grad: float32 [16, 3, 3, 128, 128], P(('groups', 'expert')), parts along dimension 0
- gate_grad: float32 [1024], P(('groups', 'expert', 'replica')), parts along dimension 0
There are 2 independent parts, one for each index of `groups`. A program takes and returns all parts, laid end to end along the dimension named above; an argument that names none is the same for every part. Nothing has to cross between parts.
Inputs may be any that keep to these rules, and one draw needn't show every extreme that they name: `route`: the 32 patches of one device name each expert at most 4 times, and one expert is named exactly 4 times by every device's patches.
All inputs are finite; a program needn't handle non-finite values.
Results may differ from a plain program's by a relative error of at most 0.0057.
Values may be sent and summed in bfloat16 or wider, within the bound.
No kernel may reach another device: no remote copies, remote signals or barrier semaphores. Data moves between devices by JAX's collectives and lax.ppermute only.
A program may use at most 64 MiB of HBM per device.

v0:
```python
import jax
import jax.numpy as jnp
from jax import lax
from jax.sharding import PartitionSpec as P

LAYOUT = ("NHWC", "HWIO", "NHWC")


def as_sent(shard):

    def short(part):
        return part.astype(jnp.bfloat16) if part.dtype == jnp.float32 else part

    return jax.tree.map(short, shard)


def convolve(inputs, kernel):
    return lax.conv_general_dilated(
        inputs,
        kernel,
        (1, 1),
        "VALID",
        dimension_numbers=LAYOUT,
        preferred_element_type=jnp.float32,
    )


def transpose_conv(gradient, kernel):
    padded = jnp.pad(gradient, ((0, 0), (2, 2), (2, 2), (0, 0)))
    flipped = jnp.transpose(kernel[::-1, ::-1], (0, 1, 3, 2))
    return convolve(padded, flipped)


def kernel_grad(inputs, gradient):
    height_out = gradient.shape[1]
    width_out = gradient.shape[2]
    pieces = []
    for row_shift in range(3):
        for col_shift in range(3):
            window = inputs[
                :, row_shift : row_shift + height_out, col_shift : col_shift + width_out, :
            ]
            pieces.append(
                jnp.einsum("nijc,nijd->cd", window, gradient, preferred_element_type=jnp.float32)
            )
    stacked = jnp.stack(pieces)
    return stacked.reshape((3, 3) + stacked.shape[1:])


def silu_slope(pre_act):
    sigma_val = jax.nn.sigmoid(pre_act)
    return sigma_val * (1.0 + pre_act * (1.0 - sigma_val))


def flatten_two(values):
    return values.reshape((values.shape[0] * values.shape[1],) + values.shape[2:])


def unflatten_two(values, leading, items):
    return values.reshape((leading, items) + values.shape[1:])


def shards(tiles, route, gate, conv_first, conv_second, cotangent):
    owners = lax.axis_size("expert")
    patch_count = tiles.shape[0]
    capacity = max(2, (patch_count + owners - 1) // owners)
    onehot = (route[:, None] == jnp.arange(owners, dtype=jnp.int32)[None, :]).astype(jnp.int32)
    rank_within = jnp.cumsum(onehot, axis=0) - 1
    slot_index = jnp.sum(onehot * rank_within, axis=1)
    target = route * capacity + slot_index
    kernel_one = conv_first[0]
    kernel_two = conv_second[0]
    gate_column = gate[:, None, None, None]
    scaled = (gate_column * cotangent.astype(jnp.float32)).astype(jnp.bfloat16)

    def to_slots(values):
        blank_slots = jnp.zeros((owners * capacity,) + values.shape[1:], values.dtype)
        filled = blank_slots.at[target].set(values)
        return filled.reshape((owners, capacity) + values.shape[1:])

    received = lax.all_to_all(to_slots(tiles), "expert", split_axis=0, concat_axis=0, tiled=True)
    leading = received.shape[0]
    items = received.shape[1]
    pre_act = convolve(flatten_two(received), kernel_one)
    hidden = jax.nn.silu(pre_act).astype(jnp.bfloat16)
    result = convolve(hidden, kernel_two).astype(jnp.bfloat16)
    pre_act, hidden, result = (
        unflatten_two(pre_act, leading, items),
        unflatten_two(hidden, leading, items),
        unflatten_two(result, leading, items),
    )
    back_result = lax.all_to_all(
        as_sent(result), "expert", split_axis=0, concat_axis=0, tiled=True
    ).astype(result.dtype)
    back_result, pre_act, hidden, received = (back_result, pre_act, hidden, received)
    grads_in = lax.all_to_all(to_slots(scaled), "expert", split_axis=0, concat_axis=0, tiled=True)
    leading = grads_in.shape[0]
    items = grads_in.shape[1]
    grad_hidden = transpose_conv(flatten_two(grads_in), kernel_two)
    grad_mid = (grad_hidden * silu_slope(flatten_two(pre_act))).astype(jnp.bfloat16)
    tile_grad = transpose_conv(grad_mid, kernel_one).astype(jnp.bfloat16)
    grad_mid, tile_grad = (
        unflatten_two(grad_mid, leading, items),
        unflatten_two(tile_grad, leading, items),
    )
    back_grad = lax.all_to_all(
        as_sent(tile_grad), "expert", split_axis=0, concat_axis=0, tiled=True
    ).astype(tile_grad.dtype)
    first_local = kernel_grad(flatten_two(received), flatten_two(grad_mid))
    second_local = kernel_grad(flatten_two(hidden), flatten_two(grads_in))
    first_grad, second_grad = lax.psum((first_local, second_local), "replica")
    result_patch = flatten_two(back_result)[target]
    tiles_grad = flatten_two(back_grad)[target]
    output = (gate_column * result_patch.astype(jnp.float32)).astype(jnp.bfloat16)
    gate_grad = jnp.sum(
        cotangent.astype(jnp.float32) * result_patch.astype(jnp.float32), axis=(1, 2, 3)
    )
    return (output, tiles_grad, first_grad[None], second_grad[None], gate_grad)


def solution(mesh):
    placed = (
        P(("groups", "expert", "replica"), None, None, None),
        P(("groups", "expert", "replica")),
        P(("groups", "expert", "replica")),
        P("expert", None, None, None, None),
        P("expert", None, None, None, None),
        P(("groups", "expert", "replica"), None, None, None),
    )
    return jax.shard_map(
        shards,
        mesh=mesh,
        in_specs=placed,
        out_specs=(
            P(("groups", "expert", "replica"), None, None, None),
            P(("groups", "expert", "replica"), None, None, None),
            P(("groups", "expert"), None, None, None, None),
            P(("groups", "expert"), None, None, None, None),
            P(("groups", "expert", "replica")),
        ),
        check_vma=False,
    )
```

profile of v0, /device:TPU:0, one launch (start us, length us, event | category | flops | bytes accessed | tf_op | source)
XLA Modules:
  0.0 155.3 jit_solution(3513916115597740346)
XLA Ops:
  7.2 0.8 fusion.26
  8.0 0.8 select_reduce_fusion
  8.8 0.7 compare_select_fusion
  9.5 1.8 %copy.17 = bf16[32,12,12,128]{3,2,1,0:T(8,128)(2,1)S(1)} copy(bf16[32,12,12,128]{3,0,2,1:T(8,128)(2,1)} %param.6) | data formatting | bytes 2359296 | tf_op args[0]
  11.3 0.3 broadcast_in_dim.10
  11.6 1.9 %scatter_fusion = bf16[32,12,12,128]{3,2,1,0:T(8,128)(2,1)S(1)} fusion(bf16[32,12,12,128]{3,2,1,0:T(8,128)(2,1)S(1)} %broadcast_in_dim.10, s32[32]{0:T(128)S(1)} %compare_select_fusion, bf16[32,12,12,128]{3,2,1,0:T(8,128)(2,1)S(1)} %copy.17), kind=kCustom, calls=%fused_computation.2 | custom fusion | bytes 3539072 | tf_op jit(solution)/shard_map/scatter | solution.py:78
  13.6 1.5 copy.18
  15.1 36.0 %all_to_all.20 = bf16[8,4,12,12,128]{4,1,3,2,0:T(4,128)(2,1)S(1)} all-to-all(bf16[8,4,12,12,128]{4,1,3,2,0:T(4,128)(2,1)S(1)} %copy.18), channel_id=1, replica_groups=mesh['groups'=2,'expert'=8,'replica'=2] {'expert'}, dimensions={0} | all-to-all | bytes 2359296 | tf_op jit(solution)/shard_map/all_to_all | solution.py:81
  51.1 0.5 copy.19
  51.7 3.3 %multiply_convert_fusion.1 = (bf16[32,10,10,128]{3,0,2,1:T(8,128)(2,1)S(1)}, f32[32,10,10,128]{3,0,2,1:T(8,128)}) fusion(bf16[32,12,12,128]{3,0,2,1:T(8,128)(2,1)S(1)} %bitcast.213, bf16[1,3,3,128,128]{4,3,2,1,0:T(8,128)(2,1)S(1)} %copy-done), kind=kOutput, calls=%fused_computation.5 | convolution fusion | flops 945766400 | bytes 3932160 | tf_op jit(solution)/shard_map/conv_general_dilated | solution.py:18
  55.0 0.9 copy-done.12
  55.9 1.4 convolution_convert_fusion.1
  57.3 1.0 copy.20
  58.3 3.5 %all-to-all-start.1 = ((bf16[8,4,8,8,128]{4,1,3,2,0:T(4,128)(2,1)}), bf16[8,4,8,8,128]{4,1,3,2,0:T(4,128)(2,1)S(1)}, u32[]{:S(2)}, u32[]{:S(2)}) async-start(bf16[8,4,8,8,128]{4,1,3,2,0:T(4,128)(2,1)} %copy.20), calls=%async_computation.1 | async-start | bytes 1048576 | tf_op jit(solution)/shard_map/all_to_all | solution.py:92
  61.8 14.0 %all-to-all-done.1 = bf16[8,4,8,8,128]{4,1,3,2,0:T(4,128)(2,1)S(1)} async-done(((bf16[8,4,8,8,128]{4,1,3,2,0:T(4,128)(2,1)}), bf16[8,4,8,8,128]{4,1,3,2,0:T(4,128)(2,1)S(1)}, u32[]{:S(2)}, u32[]{:S(2)}) %all-to-all-start.1) | async-done | bytes 524320 | tf_op jit(solution)/shard_map/all_to_all | solution.py:92
  76.0 0.7 gather_fusion
  76.6 2.2 %fusion.20 = (f32[32]{0:T(128)}, bf16[32,8,8,128]{3,2,1,0:T(8,128)(2,1)S(1)}, bf16[32,8,8,128]{3,2,1,0:T(8,128)(2,1)}) fusion(bf16[32,8,8,128]{3,2,1,0:T(8,128)(2,1)S(1)} %gather_fusion, bf16[32,8,8,128]{3,2,1,0:T(8,128)(2,1)S(1)} %copy-done.9, f32[32]{0:T(128)S(1)} %copy-done.10), kind=kLoop, calls=%fused_computation.50 | loop fusion | flops 2097120 | bytes 2097408 | tf_op jit(solution)/shard_map/reduce_sum | solution.py:115
  79.0 1.6 %scatter_fusion.1 = bf16[32,8,8,128]{3,2,1,0:T(8,128)(2,1)S(1)} fusion(bf16[32,8,8,128]{3,2,1,0:T(8,128)(2,1)S(1)} %broadcast_in_dim.23, s32[32]{0:T(128)S(1)} %compare_select_fusion, bf16[32,8,8,128]{3,2,1,0:T(8,128)(2,1)S(1)} %get-tuple-element.18), kind=kCustom, calls=%fused_computation.3 | custom fusion | bytes 1572992 | tf_op jit(solution)/shard_map/scatter | solution.py:78
  80.6 0.7 copy.22
  81.3 18.0 %all_to_all.21 = bf16[8,4,8,8,128]{4,1,3,2,0:T(4,128)(2,1)S(1)} all-to-all(bf16[8,4,8,8,128]{4,1,3,2,0:T(4,128)(2,1)S(1)} %copy.22), channel_id=1, replica_groups=mesh['groups'=2,'expert'=8,'replica'=2] {'expert'}, dimensions={0} | all-to-all | bytes 1048576 | tf_op jit(solution)/shard_map/all_to_all | solution.py:96
  99.6 2.3 %multiply_convert_fusion = bf16[32,10,10,128]{3,0,2,1:T(8,128)(2,1)S(1)} fusion(f32[32,10,10,128]{3,0,2,1:T(8,128)S(1)} %copy-done.15, bf16[32,8,8,128]{3,0,2,1:T(8,128)(2,1)S(1)} %bitcast.225, bf16[1,3,3,128,128]{4,3,2,1,0:T(8,128)(2,1)S(1)} %copy-done.11), kind=kOutput, calls=%fused_computation.4 | convolution fusion | flops 607666176 | bytes 3276800 | tf_op jit(solution)/shard_map/conv_general_dilated | solution.py:18
  101.8 0.4 fusion.17
  102.3 2.9 %convolution_convert_fusion = bf16[32,12,12,128]{3,0,2,1:T(8,128)(2,1)S(1)} fusion(bf16[32,10,10,128]{3,0,2,1:T(8,128)(2,1)S(1)} %multiply_convert_fusion, bf16[1,3,3,128,128]{4,3,2,1,0:T(8,128)(2,1)S(1)} %copy-done), kind=kOutput, calls=%fused_computation.7 | convolution fusion | flops 944308224 | bytes 2293760 | tf_op jit(solution)/shard_map/conv_general_dilated | solution.py:18
  105.2 1.0 fusion.8
  106.2 0.4 fusion.16
  106.6 0.4 fusion.15
  107.0 0.4 fusion.14
  107.5 0.4 fusion.13
  107.9 0.4 fusion.12
  108.4 0.8 copy-done.6
  109.2 1.5 copy.24
  110.6 3.7 %all-to-all-start.3 = ((bf16[8,4,12,12,128]{4,1,3,2,0:T(4,128)(2,1)}), bf16[8,4,12,12,128]{4,1,3,2,0:T(4,128)(2,1)S(1)}, u32[]{:S(2)}, u32[]{:S(2)}) async-start(bf16[8,4,12,12,128]{4,1,3,2,0:T(4,128)(2,1)} %copy.24), calls=%async_computation.3 | async-start | bytes 2359296 | tf_op jit(solution)/shard_map/all_to_all | solution.py:106
  114.7 1.6 %fusion.7 = f32[9,128,128]{2,1,0:T(8,128)S(1)} fusion(f32[9,128,128]{2,1,0:T(8,128)S(1)} %copy-done.4, bf16[32,10,10,128]{3,0,2,1:T(8,128)(2,1)} %copy-done.12, bf16[32,8,8,128]{3,0,2,1:T(8,128)(2,1)} %bitcast.227), kind=kOutput, calls=%fused_computation.27 | convolution fusion | flops 67108864 | bytes 1409024 | tf_op jit(solution)/shard_map/nijc,nijd->cd/dot_general | solution.py:44
  116.3 0.3 fusion.6
  116.7 0.3 fusion.5
  117.0 0.3 fusion.4
  117.4 0.3 fusion.3
  117.7 0.3 fusion.2
  118.7 0.9 copy-done.2
  119.7 1.0 fusion.11
  120.7 1.1 fusion.10
  121.8 1.1 fusion.9
  122.9 19.8 %all-to-all-done.3 = bf16[8,4,12,12,128]{4,1,3,2,0:T(4,128)(2,1)S(1)} async-done(((bf16[8,4,12,12,128]{4,1,3,2,0:T(4,128)(2,1)}), bf16[8,4,12,12,128]{4,1,3,2,0:T(4,128)(2,1)S(1)}, u32[]{:S(2)}, u32[]{:S(2)}) %all-to-all-start.3) | async-done | bytes 1179680 | tf_op jit(solution)/shard_map/all_to_all | solution.py:106
  142.7 0.4 copy.25
  143.1 0.9 gather_fusion.1
  143.9 1.8 %copy.26 = bf16[32,12,12,128]{3,0,2,1:T(8,128)(2,1)} copy(bf16[32,12,12,128]{3,2,1,0:T(8,128)(2,1)S(1)} %gather_fusion.1) | data formatting | bytes 2359296
  145.7 2.0 %copy.65 = f32[1,3,3,128,128]{4,3,2,1,0:T(8,128)} copy(f32[1,3,3,128,128]{4,3,2,1,0:T(8,128)} %get-tuple-element.24) | data formatting | bytes 1179648
  147.7 0.8 copy.66
  (39 shorter events, 1.5 us)
Async XLA Ops:
  7.2 44.5 %copy-start = (bf16[1,3,3,128,128]{4,3,2,1,0:T(8,128)(2,1)S(1)}, bf16[1,3,3,128,128]{4,3,2,1,0:T(8,128)(2,1)}, u32[]{:S(2)}) copy-start(bf16[1,3,3,128,128]{4,3,2,1,0:T(8,128)(2,1)} %param.9) | copy-start | bytes 884740
  51.6 56.3 %copy-start.1 = (bf16[8,4,12,12,128]{4,1,0,3,2:T(4,128)(2,1)}, bf16[8,4,12,12,128]{4,1,0,3,2:T(4,128)(2,1)S(1)}, u32[]{:S(2)}) copy-start(bf16[8,4,12,12,128]{4,1,0,3,2:T(4,128)(2,1)S(1)} %copy.19) | copy-start | bytes 3538948
  51.6 4.2 %copy-start.11 = (bf16[1,3,3,128,128]{4,3,2,1,0:T(8,128)(2,1)S(1)}, bf16[1,3,3,128,128]{4,3,2,1,0:T(8,128)(2,1)}, u32[]{:S(2)}) copy-start(bf16[1,3,3,128,128]{4,3,2,1,0:T(8,128)(2,1)} %param.10) | copy-start | bytes 884740
  55.0 0.9 copy-start.12
  58.3 17.6 %all-to-all-start.1 = ((bf16[8,4,8,8,128]{4,1,3,2,0:T(4,128)(2,1)}), bf16[8,4,8,8,128]{4,1,3,2,0:T(4,128)(2,1)S(1)}, u32[]{:S(2)}, u32[]{:S(2)}) async-start(bf16[8,4,8,8,128]{4,1,3,2,0:T(4,128)(2,1)} %copy.20), calls=%async_computation.1 | async-start | bytes 1048576 | tf_op jit(solution)/shard_map/all_to_all | solution.py:92
  61.8 14.9 %copy-start.9 = (bf16[32,8,8,128]{3,2,1,0:T(8,128)(2,1)S(1)}, bf16[32,8,8,128]{3,2,1,0:T(8,128)(2,1)}, u32[]{:S(2)}) copy-start(bf16[32,8,8,128]{3,2,1,0:T(8,128)(2,1)} %param.11) | copy-start | bytes 1572868
  61.8 14.9 %copy-start.10 = (f32[32]{0:T(128)S(1)}, f32[32]{0:T(128)}, u32[]{:S(2)}) copy-start(f32[32]{0:T(128)} %param.8) | copy-start | bytes 388
  81.3 18.3 %copy-start.15 = (f32[32,10,10,128]{3,0,2,1:T(8,128)S(1)}, f32[32,10,10,128]{3,0,2,1:T(8,128)}, u32[]{:S(2)}) copy-start(f32[32,10,10,128]{3,0,2,1:T(8,128)} %get-tuple-element.21) | copy-start | bytes 4915204
  99.5 5.7 %copy-start.7 = (bf16[8,4,8,8,128]{4,1,0,3,2:T(4,128)(2,1)}, bf16[8,4,8,8,128]{4,1,0,3,2:T(4,128)(2,1)S(1)}, u32[]{:S(2)}) copy-start(bf16[8,4,8,8,128]{4,1,0,3,2:T(4,128)(2,1)S(1)} %copy.23) | copy-start | bytes 1572868
  102.2 3.0 %copy-start.13 = (bf16[32,10,10,128]{3,0,2,1:T(8,128)(2,1)S(1)}, bf16[32,10,10,128]{3,0,2,1:T(8,128)(2,1)}, u32[]{:S(2)}) copy-start(bf16[32,10,10,128]{3,0,2,1:T(8,128)(2,1)} %copy-done.12) | copy-start | bytes 2457604
  108.4 0.8 copy-start.6
  110.6 4.0 %copy-start.4 = (f32[9,128,128]{2,1,0:T(8,128)S(1)}, f32[9,128,128]{2,1,0:T(8,128)}, u32[]{:S(2)}) copy-start(f32[9,128,128]{2,1,0:T(8,128)} %fusion.8) | copy-start | bytes 1769476
  110.6 32.0 %all-to-all-start.3 = ((bf16[8,4,12,12,128]{4,1,3,2,0:T(4,128)(2,1)}), bf16[8,4,12,12,128]{4,1,3,2,0:T(4,128)(2,1)S(1)}, u32[]{:S(2)}, u32[]{:S(2)}) async-start(bf16[8,4,12,12,128]{4,1,3,2,0:T(4,128)(2,1)} %copy.24), calls=%async_computation.3 | async-start | bytes 2359296 | tf_op jit(solution)/shard_map/all_to_all | solution.py:106
  114.4 31.3 %all-reduce.3.cloned.1.call-start = ((), (), s32[]{:S(2)}) async-start(), calls=%async_computation.4 | async-start | bytes 2359296 | tf_op jit(solution)/shard_map/psum | solution.py:111
  114.6 1.7 %copy-start.8 = (bf16[8,4,8,8,128]{4,1,0,3,2:T(4,128)(2,1)S(1)}, bf16[8,4,8,8,128]{4,1,0,3,2:T(4,128)(2,1)}, u32[]{:S(2)}) copy-start(bf16[8,4,8,8,128]{4,1,0,3,2:T(4,128)(2,1)} %copy-done.7) | copy-start | bytes 1572868
  114.6 1.7 %copy-start.14 = (bf16[32,10,10,128]{3,0,2,1:T(8,128)(2,1)S(1)}, bf16[32,10,10,128]{3,0,2,1:T(8,128)(2,1)}, u32[]{:S(2)}) copy-start(bf16[32,10,10,128]{3,0,2,1:T(8,128)(2,1)} %copy-done.12) | copy-start | bytes 2457604
  118.4 1.3 copy-start.2
  119.7 1.0 copy-start.5
  145.7 2.0 %copy-start.3 = (f32[1,3,3,128,128]{4,3,2,1,0:T(8,128)S(1)}, f32[1,3,3,128,128]{4,3,2,1,0:T(8,128)}, u32[]{:S(2)}) copy-start(f32[1,3,3,128,128]{4,3,2,1,0:T(8,128)} %get-tuple-element.25) | copy-start | bytes 1769476
Sparse Core Ops, SparseCore 0:
  123.0 21.0 all-reduce.2
where the time goes:
time: 156 us; the launch traced here: 155 us
  blocking collectives  54.1 us (35%)
  waiting for transfers between devices  33.9 us (22%)
  matrix products  20.6 us (13%)
  local copies, waits for them, and re-layouts  20.4 us (13%)
  between operations  14.4 us (9%)
  starting transfers between devices  7.47 us (5%)
  other arithmetic  4.54 us (3%)
    all_to_all x1, blocking collectives, shards(): lax.all_to_all(to_slots(tiles), 'expert', split_axis=0, concat_axis=0, ti...  36 us
    all_to_all x1, waiting for transfers between devices, shards(): lax.all_to_all(as_sent(tile_grad), 'expert', split_axis=0, concat_axis=0,...  19.8 us
    all_to_all x1, blocking collectives, shards(): lax.all_to_all(to_slots(scaled), 'expert', split_axis=0, concat_axis=0, t...  18 us
    all_to_all x1, waiting for transfers between devices, shards(): lax.all_to_all(as_sent(result), 'expert', split_axis=0, concat_axis=0, ti...  14 us
    dot_general x18, matrix products, kernel_grad(): jnp.einsum('nijc,nijd->cd', window, gradient, preferred_element_type=jnp....  10.7 us
    conv_general_dilated x4, matrix products, convolve(): lax.conv_general_dilated(inputs, kernel, (1, 1), 'VALID', dimension_numbe...  9.88 us
    unnamed x36, local copies, waits for them, and re-layouts  9.04 us
    all_to_all x1, starting transfers between devices, shards(): lax.all_to_all(as_sent(tile_grad), 'expert', split_axis=0, concat_axis=0,...  3.72 us
  transfers between devices with their start and end apart: 3, of which 2 were waited for; matrix products, arithmetic and copies ran while one was open for 7% of the time, Pallas kernels for 0%

commit v1 on v0

--- a/solution.py
+++ b/solution.py
@@ -1,8 +1,11 @@
 import jax
 import jax.numpy as jnp
 from jax import lax
+from jax.sharding import Mesh
 from jax.sharding import PartitionSpec as P
 
+SWAP = [(0, 3), (2, 1)]
+SWAP_HOME = [(3, 0), (1, 2)]
 LAYOUT = ("NHWC", "HWIO", "NHWC")
 
 
@@ -61,15 +64,22 @@
 
 
 def shards(tiles, route, gate, conv_first, conv_second, cotangent):
-    owners = lax.axis_size("expert")
+    halves = lax.axis_size("half")
+    per_half = lax.axis_size("owner")
+    cores = lax.axis_size("replica")
+    half = lax.axis_index("half")
+    core = lax.axis_index("replica")
+    owners = halves * per_half
     patch_count = tiles.shape[0]
     capacity = max(2, (patch_count + owners - 1) // owners)
     onehot = (route[:, None] == jnp.arange(owners, dtype=jnp.int32)[None, :]).astype(jnp.int32)
     rank_within = jnp.cumsum(onehot, axis=0) - 1
     slot_index = jnp.sum(onehot * rank_within, axis=1)
-    target = route * capacity + slot_index
-    kernel_one = conv_first[0]
-    kernel_two = conv_second[0]
+    route_core = (route // per_half - half + halves) % halves
+    target = ((route % per_half) * cores + route_core) * capacity + slot_index
+    other_one, other_two = lax.ppermute((conv_first[0], conv_second[0]), ("half", "replica"), SWAP)
+    kernel_one = jnp.where(core == 0, conv_first[0], other_one)
+    kernel_two = jnp.where(core == 0, conv_second[0], other_two)
     gate_column = gate[:, None, None, None]
     scaled = (gate_column * cotangent.astype(jnp.float32)).astype(jnp.bfloat16)
 
@@ -78,7 +88,7 @@
         filled = blank_slots.at[target].set(values)
         return filled.reshape((owners, capacity) + values.shape[1:])
 
-    received = lax.all_to_all(to_slots(tiles), "expert", split_axis=0, concat_axis=0, tiled=True)
+    received = lax.all_to_all(to_slots(tiles), ("owner", "replica"), split_axis=0, concat_axis=0, tiled=True)
     leading = received.shape[0]
     items = received.shape[1]
     pre_act = convolve(flatten_two(received), kernel_one)
@@ -90,10 +100,10 @@
         unflatten_two(result, leading, items),
     )
     back_result = lax.all_to_all(
-        as_sent(result), "expert", split_axis=0, concat_axis=0, tiled=True
+        as_sent(result), ("owner", "replica"), split_axis=0, concat_axis=0, tiled=True
     ).astype(result.dtype)
     back_result, pre_act, hidden, received = (back_result, pre_act, hidden, received)
-    grads_in = lax.all_to_all(to_slots(scaled), "expert", split_axis=0, concat_axis=0, tiled=True)
+    grads_in = lax.all_to_all(to_slots(scaled), ("owner", "replica"), split_axis=0, concat_axis=0, tiled=True)
     leading = grads_in.shape[0]
     items = grads_in.shape[1]
     grad_hidden = transpose_conv(flatten_two(grads_in), kernel_two)
@@ -104,11 +114,20 @@
         unflatten_two(tile_grad, leading, items),
     )
     back_grad = lax.all_to_all(
-        as_sent(tile_grad), "expert", split_axis=0, concat_axis=0, tiled=True
+        as_sent(tile_grad), ("owner", "replica"), split_axis=0, concat_axis=0, tiled=True
     ).astype(tile_grad.dtype)
     first_local = kernel_grad(flatten_two(received), flatten_two(grad_mid))
     second_local = kernel_grad(flatten_two(hidden), flatten_two(grads_in))
-    first_grad, second_grad = lax.psum((first_local, second_local), "replica")
+
+    def combine(local):
+        away = lax.ppermute(local.astype(jnp.bfloat16), ("half", "replica"), SWAP_HOME)
+        beside = lax.ppermute(local, "replica", [(0, 1)])
+        own = jnp.where(core == 0, local, beside)
+        passed = lax.ppermute(away, "replica", [(0, 1)])
+        return own + jnp.where(core == 0, away, passed).astype(jnp.float32)
+
+    first_grad = combine(first_local)
+    second_grad = combine(second_local)
     result_patch = flatten_two(back_result)[target]
     tiles_grad = flatten_two(back_grad)[target]
     output = (gate_column * result_patch.astype(jnp.float32)).astype(jnp.bfloat16)
@@ -119,24 +138,29 @@
 
 
 def solution(mesh):
+    groups, experts, cores = (mesh.shape[a] for a in ("groups", "expert", "replica"))
+    mesh = Mesh(
+        mesh.devices.reshape(groups, cores, experts // cores, cores),
+        ("groups", "half", "owner", "replica"),
+    )
     placed = (
-        P(("groups", "expert", "replica"), None, None, None),
-        P(("groups", "expert", "replica")),
-        P(("groups", "expert", "replica")),
-        P("expert", None, None, None, None),
-        P("expert", None, None, None, None),
-        P(("groups", "expert", "replica"), None, None, None),
+        P(("groups", "half", "owner", "replica"), None, None, None),
+        P(("groups", "half", "owner", "replica")),
+        P(("groups", "half", "owner", "replica")),
+        P(("half", "owner"), None, None, None, None),
+        P(("half", "owner"), None, None, None, None),
+        P(("groups", "half", "owner", "replica"), None, None, None),
     )
     return jax.shard_map(
         shards,
         mesh=mesh,
         in_specs=placed,
         out_specs=(
-            P(("groups", "expert", "replica"), None, None, None),
-            P(("groups", "expert", "replica"), None, None, None),
-            P(("groups", "expert"), None, None, None, None),
-            P(("groups", "expert"), None, None, None, None),
-            P(("groups", "expert", "replica")),
+            P(("groups", "half", "owner", "replica"), None, None, None),
+            P(("groups", "half", "owner", "replica"), None, None, None),
+            P(("groups", "half", "owner"), None, None, None, None),
+            P(("groups", "half", "owner"), None, None, None, None),
+            P(("groups", "half", "owner", "replica")),
         ),
         check_vma=False,
     )

time: 156 us -> 120 us (0.77)
  blocking collectives: 54.1 us -> 11.6 us
  starting transfers between devices: 7.47 us -> 33.5 us
  between operations: 14.4 us -> 1.19 us
  waiting for transfers between devices: 33.9 us -> 30.8 us
  local copies, waits for them, and re-layouts: 20.4 us -> 17.9 us
  matrix products: 20.6 us -> 18.2 us
    all_to_all x2 -> x1, blocking collectives: 54.1 us -> 11.6 us  [shards(): lax.all_to_all(to_slots(scaled), ('owner', 'replica'), split_axis=0, conc...]
    ppermute x0 -> x8, starting transfers between devices: none -> 21 us  [the longest x2 7.55 us: combine(): beside = lax.ppermute(local, 'replica', [(0, 1)])]
    all_to_all x2 -> x3, waiting for transfers between devices: 33.9 us -> 24.4 us  [the longest x1 15.5 us: shards(): lax.all_to_all(to_slots(tiles), ('owner', 'replica'), split_axis=0, conca...]
    ppermute x0 -> x8, waiting for transfers between devices: none -> 6.47 us  [the longest x2 6.23 us: combine(): lax.ppermute(local.astype(jnp.bfloat16), ('half', 'replica'), SWAP_HOME)]
    all_to_all x2 -> x3, starting transfers between devices: 7.21 us -> 12.4 us  [the longest x1 5.39 us: shards(): lax.all_to_all(to_slots(tiles), ('owner', 'replica'), split_axis=0, conca...]
    unnamed x36, local copies, waits for them, and re-layouts: 9.04 us -> 5.58 us
    dot_general x18, matrix products: 10.7 us -> 8.19 us  [kernel_grad(): jnp.einsum('nijc,nijd->cd', window, gradient, preferred_element_type=jnp....]
    broadcast_in_dim x0 -> x2, other arithmetic: none -> 1.85 us  [shards(): return (output, tiles_grad, first_grad[None], second_grad[None], gate_grad)]
  transfers between devices with their start and end apart: 3 -> 11, of which waited for: 2 -> 4; matrix products, arithmetic and copies ran while one was open for 7% -> 10% of each run, Pallas kernels for 0% -> 0%
where the time goes in v1:
time: 120 us; the launch traced here: 119 us
  starting transfers between devices  33.5 us (28%)
  waiting for transfers between devices  30.8 us (26%)
  matrix products  18.2 us (15%)
  local copies, waits for them, and re-layouts  17.9 us (15%)
  blocking collectives  11.6 us (10%)
  other arithmetic  5.78 us (5%)
    all_to_all x1, waiting for transfers between devices, shards(): lax.all_to_all(to_slots(tiles), ('owner', 'replica'), split_axis=0, conca...  15.5 us
    all_to_all x1, blocking collectives, shards(): lax.all_to_all(to_slots(scaled), ('owner', 'replica'), split_axis=0, conc...  11.6 us
    conv_general_dilated x4, matrix products, convolve(): lax.conv_general_dilated(inputs, kernel, (1, 1), 'VALID', dimension_numbe...  9.97 us
    all_to_all x1, waiting for transfers between devices, shards(): lax.all_to_all(as_sent(result), ('owner', 'replica'), split_axis=0, conca...  8.82 us
    dot_general x18, matrix products, kernel_grad(): jnp.einsum('nijc,nijd->cd', window, gradient, preferred_element_type=jnp....  8.19 us
    ppermute x2, starting transfers between devices, combine(): beside = lax.ppermute(local, 'replica', [(0, 1)])  7.55 us
    ppermute x2, starting transfers between devices, shards(): lax.ppermute((conv_first[0], conv_second[0]), ('half', 'replica'), SWAP)  6.62 us
    ppermute x2, waiting for transfers between devices, combine(): lax.ppermute(local.astype(jnp.bfloat16), ('half', 'replica'), SWAP_HOME)  6.23 us
  transfers between devices with their start and end apart: 11, of which 4 were waited for; matrix products, arithmetic and copies ran while one was open for 10% of the time, Pallas kernels for 0%

profile of v1, /device:TPU:0, one launch (start us, length us, event | category | flops | bytes accessed | tf_op | source)
XLA Modules:
  0.0 119.0 jit_solution(7853953223417285552)
XLA Ops:
  0.6 0.7 fusion.22
  1.4 0.8 select_reduce_fusion
  2.3 1.8 %copy.17 = bf16[32,12,12,128]{3,2,1,0:T(8,128)(2,1)S(1)} copy(bf16[32,12,12,128]{3,0,2,1:T(8,128)(2,1)} %param.6) | data formatting | bytes 2359296 | tf_op args[0]
  4.4 1.9 %scatter_fusion = bf16[32,12,12,128]{3,2,1,0:T(8,128)(2,1)S(1)} fusion(bf16[32,12,12,128]{3,2,1,0:T(8,128)(2,1)S(1)} %broadcast_in_dim.10, s32[32]{0:T(128)S(1)} %compare_select_fusion, bf16[32,12,12,128]{3,2,1,0:T(8,128)(2,1)S(1)} %copy.17), kind=kCustom, calls=%fused_computation.2 | custom fusion | bytes 3539072 | tf_op jit(solution)/shard_map/scatter | solution.py:88
  6.4 2.5 %copy.18 = bf16[8,4,12,12,128]{4,1,3,2,0:T(4,128)(2,1)} copy(bf16[8,4,12,12,128]{4,3,2,1,0:T(8,128)(2,1)S(1)} %bitcast.220) | data formatting | bytes 2359296 | tf_op jit(solution)/shard_map/reshape | solution.py:89
  8.9 5.4 %all-to-all-start = ((bf16[8,4,12,12,128]{4,1,3,2,0:T(4,128)(2,1)}), bf16[8,4,12,12,128]{4,1,3,2,0:T(4,128)(2,1)S(1)}, u32[]{:S(2)}, u32[]{:S(2)}) async-start(bf16[8,4,12,12,128]{4,1,3,2,0:T(4,128)(2,1)} %copy.18), calls=%async_computation | async-start | bytes 2359296 | tf_op jit(solution)/shard_map/all_to_all | solution.py:91
  14.3 4.6 %collective-permute-start = (bf16[3,3,128,128]{3,2,1,0:T(8,128)(2,1)S(1)}, bf16[3,3,128,128]{3,2,1,0:T(8,128)(2,1)S(1)}, u32[]{:S(2)}, u32[]{:S(2)}) collective-permute-start(bf16[3,3,128,128]{3,2,1,0:T(8,128)(2,1)S(1)} %bitcast.252), channel_id=1, source_target_pairs={{0,9},{8,1},{2,11},{10,3},{4,13},{12,5},{6,15},{14,7},{16,25},{24,... | collective-permute-start | bytes 884744 | tf_op jit(solution)/shard_map/ppermute | solution.py:80
  18.9 2.0 %collective-permute-start.1 = (bf16[3,3,128,128]{3,2,1,0:T(8,128)(2,1)S(1)}, bf16[3,3,128,128]{3,2,1,0:T(8,128)(2,1)}, u32[]{:S(2)}, u32[]{:S(2)}) collective-permute-start(bf16[3,3,128,128]{3,2,1,0:T(8,128)(2,1)S(1)} %bitcast.253), channel_id=1, source_target_pairs={{0,9},{8,1},{2,11},{10,3},{4,13},{12,5},{6,15},{14,7},{16,25},{24,... | collective-permute-start | bytes 884744 | tf_op jit(solution)/shard_map/ppermute | solution.py:80
  20.9 15.5 %all-to-all-done = bf16[8,4,12,12,128]{4,1,3,2,0:T(4,128)(2,1)S(1)} async-done(((bf16[8,4,12,12,128]{4,1,3,2,0:T(4,128)(2,1)}), bf16[8,4,12,12,128]{4,1,3,2,0:T(4,128)(2,1)S(1)}, u32[]{:S(2)}, u32[]{:S(2)}) %all-to-all-start) | async-done | bytes 1179680 | tf_op jit(solution)/shard_map/all_to_all | solution.py:91
  36.5 0.5 copy.19
  37.0 3.3 %multiply_convert_fusion.1 = (bf16[32,10,10,128]{3,0,2,1:T(8,128)(2,1)S(1)}, f32[32,10,10,128]{3,0,2,1:T(8,128)}) fusion(bf16[32,12,12,128]{3,0,2,1:T(8,128)(2,1)S(1)} %bitcast.231, bf16[3,3,128,128]{3,2,1,0:T(8,128)(2,1)S(1)} %collective-permute-done, pred[]{:T(512)S(6)} %eq.14, bf16[1,3,3,128,128]{4,3,2,1,0:T(8,128)(2,1)S(1)} %copy-done.5), kind=kOutput, calls=%fused_computation.5 | convolution fusion | flops 945913856 | bytes 4227073 | tf_op jit(solution)/shard_map/conv_general_dilated | solution.py:21
  40.3 1.4 %convolution_convert_fusion.1 = bf16[32,8,8,128]{3,0,2,1:T(8,128)(2,1)S(1)} fusion(bf16[32,10,10,128]{3,0,2,1:T(8,128)(2,1)S(1)} %get-tuple-element.18, bf16[3,3,128,128]{3,2,1,0:T(8,128)(2,1)} %collective-permute-done.1, pred[]{:T(512)S(6)} %eq.14, bf16[1,3,3,128,128]{4,3,2,1,0:T(8,128)(2,1)S(1)} %copy-done.11), kind=kOutput, calls=%fused_computation.11 | convolution fusion | flops 604389376 | bytes 1933313 | tf_op jit(solution)/shard_map/conv_general_dilated | solution.py:21
  41.7 1.0 copy.20
  42.7 3.5 %all-to-all-start.1 = ((bf16[8,4,8,8,128]{4,1,3,2,0:T(4,128)(2,1)}), bf16[8,4,8,8,128]{4,1,3,2,0:T(4,128)(2,1)S(1)}, u32[]{:S(2)}, u32[]{:S(2)}) async-start(bf16[8,4,8,8,128]{4,1,3,2,0:T(4,128)(2,1)} %copy.20), calls=%async_computation.1 | async-start | bytes 1048576 | tf_op jit(solution)/shard_map/all_to_all | solution.py:102
  46.3 8.8 %all-to-all-done.1 = bf16[8,4,8,8,128]{4,1,3,2,0:T(4,128)(2,1)S(1)} async-done(((bf16[8,4,8,8,128]{4,1,3,2,0:T(4,128)(2,1)}), bf16[8,4,8,8,128]{4,1,3,2,0:T(4,128)(2,1)S(1)}, u32[]{:S(2)}, u32[]{:S(2)}) %all-to-all-start.1) | async-done | bytes 524320 | tf_op jit(solution)/shard_map/all_to_all | solution.py:102
  55.2 0.7 gather_fusion
  55.9 2.2 %fusion.20 = (f32[32]{0:T(128)}, bf16[32,8,8,128]{3,2,1,0:T(8,128)(2,1)S(1)}, bf16[32,8,8,128]{3,2,1,0:T(8,128)(2,1)}) fusion(bf16[32,8,8,128]{3,2,1,0:T(8,128)(2,1)S(1)} %gather_fusion, bf16[32,8,8,128]{3,2,1,0:T(8,128)(2,1)S(1)} %copy-done.4, f32[32]{0:T(128)S(1)} %copy-done.10), kind=kLoop, calls=%fused_computation.50 | loop fusion | flops 2097120 | bytes 2097408 | tf_op jit(solution)/shard_map/reduce_sum | solution.py:134
  58.2 1.6 %scatter_fusion.1 = bf16[32,8,8,128]{3,2,1,0:T(8,128)(2,1)S(1)} fusion(bf16[32,8,8,128]{3,2,1,0:T(8,128)(2,1)S(1)} %broadcast_in_dim.23, s32[32]{0:T(128)S(1)} %compare_select_fusion, bf16[32,8,8,128]{3,2,1,0:T(8,128)(2,1)S(1)} %get-tuple-element.16), kind=kCustom, calls=%fused_computation.3 | custom fusion | bytes 1572992 | tf_op jit(solution)/shard_map/scatter | solution.py:88
  59.9 0.7 copy.22
  60.5 11.6 %all_to_all.20 = bf16[8,4,8,8,128]{4,1,3,2,0:T(4,128)(2,1)S(1)} all-to-all(bf16[8,4,8,8,128]{4,1,3,2,0:T(4,128)(2,1)S(1)} %copy.22), channel_id=1, replica_groups=mesh['groups'=2,'half'=2,'owner'=4,'replica'=2] {'owner','replica'}, dimensions={0} | all-to-all | bytes 1048576 | tf_op jit(solution)/shard_map/all_to_all | solution.py:106
  72.7 0.8 copy-done.12
  73.5 0.6 copy-done.16
  74.0 2.3 %multiply_convert_fusion = bf16[32,10,10,128]{3,0,2,1:T(8,128)(2,1)S(1)} fusion(f32[32,10,10,128]{3,0,2,1:T(8,128)S(1)} %copy-done.16, bf16[32,8,8,128]{3,0,2,1:T(8,128)(2,1)S(1)} %bitcast.242, bf16[3,3,128,128]{3,2,1,0:T(8,128)(2,1)} %collective-permute-done.1, pred[]{:T(512)S(6)} %eq.14, bf16[1,3,3,128,128]{4,3,2,1,0:T(8,128)(2,1)S(1)} %copy-done.12), kind=kOutput, calls=%fused_computation.4 | convolution fusion | flops 607813632 | bytes 3571713 | tf_op jit(solution)/shard_map/conv_general_dilated | solution.py:21
  76.4 0.4 fusion.17
  76.8 0.4 fusion.16
  77.3 0.4 fusion.15
  77.7 0.4 fusion.14
  78.1 0.4 fusion.13
  78.6 0.5 copy-done.6
  79.2 2.9 %convolution_convert_fusion = bf16[32,12,12,128]{3,0,2,1:T(8,128)(2,1)S(1)} fusion(bf16[32,10,10,128]{3,0,2,1:T(8,128)(2,1)S(1)} %multiply_convert_fusion, bf16[3,3,128,128]{3,2,1,0:T(8,128)(2,1)S(1)} %copy-done.8, pred[]{:T(512)S(6)} %eq.14, bf16[1,3,3,128,128]{4,3,2,1,0:T(8,128)(2,1)S(1)} %copy-done.6), kind=kOutput, calls=%fused_computation.7 | convolution fusion | flops 944455680 | bytes 2588673 | tf_op jit(solution)/shard_map/conv_general_dilated | solution.py:21
  82.1 1.5 %copy.24 = bf16[8,4,12,12,128]{4,1,3,2,0:T(4,128)(2,1)} copy(bf16[8,4,12,12,128]{4,1,0,3,2:T(4,128)(2,1)S(1)} %bitcast.221) | data formatting | bytes 2359296 | tf_op jit(solution)/shard_map/reshape | solution.py:63
  83.6 3.6 %all-to-all-start.3 = ((bf16[8,4,12,12,128]{4,1,3,2,0:T(4,128)(2,1)}), bf16[8,4,12,12,128]{4,1,3,2,0:T(4,128)(2,1)S(1)}, u32[]{:S(2)}, u32[]{:S(2)}) async-start(bf16[8,4,12,12,128]{4,1,3,2,0:T(4,128)(2,1)} %copy.24), calls=%async_computation.3 | async-start | bytes 2359296 | tf_op jit(solution)/shard_map/all_to_all | solution.py:116
  87.2 1.6 %fusion.7 = f32[9,128,128]{2,1,0:T(8,128)S(1)} fusion(f32[9,128,128]{2,1,0:T(8,128)S(1)} %fusion.8, bf16[32,10,10,128]{3,0,2,1:T(8,128)(2,1)} %copy-done.13, bf16[32,8,8,128]{3,0,2,1:T(8,128)(2,1)} %bitcast.243), kind=kOutput, calls=%fused_computation.27 | convolution fusion | flops 67108864 | bytes 1409024 | tf_op jit(solution)/shard_map/nijc,nijd->cd/dot_general | solution.py:47
  91.3 2.6 %collective-permute-start.5 = (f32[3,3,128,128]{3,2,1,0:T(8,128)S(1)}, f32[3,3,128,128]{3,2,1,0:T(8,128)S(1)}, u32[]{:S(2)}, u32[]{:S(2)}) collective-permute-start(f32[3,3,128,128]{3,2,1,0:T(8,128)S(1)} %bitcast.224), channel_id=1, source_target_pairs={{0,1},{2,3},{4,5},{6,7},{8,9},{10,11},{12,13},{14,15},{16,17},{18,... | collective-permute-start | bytes 1769480 | tf_op jit(solution)/shard_map/ppermute | solution.py:124
  93.9 1.5 %collective-permute-start.6 = (bf16[3,3,128,128]{3,2,1,0:T(8,128)(2,1)S(1)}, bf16[3,3,128,128]{3,2,1,0:T(8,128)(2,1)S(1)}, u32[]{:S(2)}, u32[]{:S(2)}) collective-permute-start(bf16[3,3,128,128]{3,2,1,0:T(8,128)(2,1)S(1)} %convert_element_type.56), channel_id=1, source_target_pairs={{9,0},{1,8},{11,2},{3,10},{13,4},{5,12},{15,6},{7,14},{25,16},{17,... | collective-permute-start | bytes 884744 | tf_op jit(solution)/shard_map/ppermute | solution.py:123
  95.5 0.4 fusion.12
  95.9 0.4 fusion.11
  96.3 0.4 fusion.10
  96.8 0.4 fusion.9
  97.3 1.3 %collective-permute-start.3 = (bf16[3,3,128,128]{3,2,1,0:T(8,128)(2,1)S(1)}, bf16[3,3,128,128]{3,2,1,0:T(8,128)(2,1)S(1)}, u32[]{:S(2)}, u32[]{:S(2)}) collective-permute-start(bf16[3,3,128,128]{3,2,1,0:T(8,128)(2,1)S(1)} %convert_element_type.54), channel_id=1, source_target_pairs={{9,0},{1,8},{11,2},{3,10},{13,4},{5,12},{15,6},{7,14},{25,16},{17,... | collective-permute-start | bytes 884744 | tf_op jit(solution)/shard_map/ppermute | solution.py:123
  98.6 4.9 %collective-permute-start.2 = (f32[3,3,128,128]{3,2,1,0:T(8,128)S(1)}, f32[3,3,128,128]{3,2,1,0:T(8,128)S(1)}, u32[]{:S(2)}, u32[]{:S(2)}) collective-permute-start(f32[3,3,128,128]{3,2,1,0:T(8,128)S(1)} %bitcast.228), channel_id=1, source_target_pairs={{0,1},{2,3},{4,5},{6,7},{8,9},{10,11},{12,13},{14,15},{16,17},{18,... | collective-permute-start | bytes 1769480 | tf_op jit(solution)/shard_map/ppermute | solution.py:124
  103.5 2.8 %collective-permute-start.7 = (bf16[3,3,128,128]{3,2,1,0:T(8,128)(2,1)S(1)}, bf16[3,3,128,128]{3,2,1,0:T(8,128)(2,1)S(1)}, u32[]{:S(2)}, u32[]{:S(2)}) collective-permute-start(bf16[3,3,128,128]{3,2,1,0:T(8,128)(2,1)S(1)} %collective-permute-done.6), channel_id=1, source_target_pairs={{0,1},{2,3},{4,5},{6,7},{8,9},{10,11},{12,13},{14,15},{16,17},{18,... | collective-permute-start | bytes 884744 | tf_op jit(solution)/shard_map/ppermute | solution.py:126
  106.3 6.2 %collective-permute-done.3 = bf16[3,3,128,128]{3,2,1,0:T(8,128)(2,1)S(1)} collective-permute-done((bf16[3,3,128,128]{3,2,1,0:T(8,128)(2,1)S(1)}, bf16[3,3,128,128]{3,2,1,0:T(8,128)(2,1)S(1)}, u32[]{:S(2)}, u32[]{:S(2)}) %collective-permute-start.3) | collective-permute-done | bytes 294944 | tf_op jit(solution)/shard_map/ppermute | solution.py:123
  112.5 1.3 %collective-permute-start.4 = (bf16[3,3,128,128]{3,2,1,0:T(8,128)(2,1)S(1)}, bf16[3,3,128,128]{3,2,1,0:T(8,128)(2,1)S(1)}, u32[]{:S(2)}, u32[]{:S(2)}) collective-permute-start(bf16[3,3,128,128]{3,2,1,0:T(8,128)(2,1)S(1)} %collective-permute-done.3), channel_id=1, source_target_pairs={{0,1},{2,3},{4,5},{6,7},{8,9},{10,11},{12,13},{14,15},{16,17},{18,... | collective-permute-start | bytes 884744 | tf_op jit(solution)/shard_map/ppermute | solution.py:126
  113.9 0.9 add_bitcast_fusion
  115.0 0.9 add_bitcast_fusion.1
  116.3 0.9 gather_fusion.1
  117.2 1.8 %copy.26 = bf16[32,12,12,128]{3,0,2,1:T(8,128)(2,1)} copy(bf16[32,12,12,128]{3,2,1,0:T(8,128)(2,1)S(1)} %gather_fusion.1) | data formatting | bytes 2359296
  (57 shorter events, 4.4 us)
Async XLA Ops:
  2.3 1.8 %copy-start.9 = (s32[32]{0:T(128)S(1)}, s32[32]{0:T(128)}, u32[]{:S(2)}) copy-start(s32[32]{0:T(128)} %param.7) | copy-start | bytes 388
  8.9 5.4 %copy-start.5 = (bf16[1,3,3,128,128]{4,3,2,1,0:T(8,128)(2,1)S(1)}, bf16[1,3,3,128,128]{4,3,2,1,0:T(8,128)(2,1)}, u32[]{:S(2)}) copy-start(bf16[1,3,3,128,128]{4,3,2,1,0:T(8,128)(2,1)} %param.9) | copy-start | bytes 884740
  8.9 10.0 %copy-start.11 = (bf16[1,3,3,128,128]{4,3,2,1,0:T(8,128)(2,1)S(1)}, bf16[1,3,3,128,128]{4,3,2,1,0:T(8,128)(2,1)}, u32[]{:S(2)}) copy-start(bf16[1,3,3,128,128]{4,3,2,1,0:T(8,128)(2,1)} %param.10) | copy-start | bytes 884740
  8.9 27.6 %all-to-all-start = ((bf16[8,4,12,12,128]{4,1,3,2,0:T(4,128)(2,1)}), bf16[8,4,12,12,128]{4,1,3,2,0:T(4,128)(2,1)S(1)}, u32[]{:S(2)}, u32[]{:S(2)}) async-start(bf16[8,4,12,12,128]{4,1,3,2,0:T(4,128)(2,1)} %copy.18), calls=%async_computation | async-start | bytes 2359296 | tf_op jit(solution)/shard_map/all_to_all | solution.py:91
  14.3 22.7 %collective-permute-start = (bf16[3,3,128,128]{3,2,1,0:T(8,128)(2,1)S(1)}, bf16[3,3,128,128]{3,2,1,0:T(8,128)(2,1)S(1)}, u32[]{:S(2)}, u32[]{:S(2)}) collective-permute-start(bf16[3,3,128,128]{3,2,1,0:T(8,128)(2,1)S(1)} %bitcast.252), channel_id=1, source_target_pairs={{0,9},{8,1},{2,11},{10,3},{4,13},{12,5},{6,15},{14,7},{16,25},{24,... | collective-permute-start | bytes 884744 | tf_op jit(solution)/shard_map/ppermute | solution.py:80
  18.9 21.4 %collective-permute-start.1 = (bf16[3,3,128,128]{3,2,1,0:T(8,128)(2,1)S(1)}, bf16[3,3,128,128]{3,2,1,0:T(8,128)(2,1)}, u32[]{:S(2)}, u32[]{:S(2)}) collective-permute-start(bf16[3,3,128,128]{3,2,1,0:T(8,128)(2,1)S(1)} %bitcast.253), channel_id=1, source_target_pairs={{0,9},{8,1},{2,11},{10,3},{4,13},{12,5},{6,15},{14,7},{16,25},{24,... | collective-permute-start | bytes 884744 | tf_op jit(solution)/shard_map/ppermute | solution.py:80
  37.0 41.1 %copy-start = (bf16[8,4,12,12,128]{4,1,0,3,2:T(4,128)(2,1)}, bf16[8,4,12,12,128]{4,1,0,3,2:T(4,128)(2,1)S(1)}, u32[]{:S(2)}) copy-start(bf16[8,4,12,12,128]{4,1,0,3,2:T(4,128)(2,1)S(1)} %copy.19) | copy-start | bytes 3538948
  37.0 3.3 %copy-start.7 = (bf16[3,3,128,128]{3,2,1,0:T(8,128)(2,1)}, bf16[3,3,128,128]{3,2,1,0:T(8,128)(2,1)S(1)}, u32[]{:S(2)}) copy-start(bf16[3,3,128,128]{3,2,1,0:T(8,128)(2,1)S(1)} %collective-permute-done) | copy-start | bytes 884740
  40.3 1.4 %copy-start.13 = (bf16[32,10,10,128]{3,0,2,1:T(8,128)(2,1)}, bf16[32,10,10,128]{3,0,2,1:T(8,128)(2,1)S(1)}, u32[]{:S(2)}) copy-start(bf16[32,10,10,128]{3,0,2,1:T(8,128)(2,1)S(1)} %get-tuple-element.18) | copy-start | bytes 2457604
  42.7 12.4 %all-to-all-start.1 = ((bf16[8,4,8,8,128]{4,1,3,2,0:T(4,128)(2,1)}), bf16[8,4,8,8,128]{4,1,3,2,0:T(4,128)(2,1)S(1)}, u32[]{:S(2)}, u32[]{:S(2)}) async-start(bf16[8,4,8,8,128]{4,1,3,2,0:T(4,128)(2,1)} %copy.20), calls=%async_computation.1 | async-start | bytes 1048576 | tf_op jit(solution)/shard_map/all_to_all | solution.py:102
  46.2 9.6 %copy-start.4 = (bf16[32,8,8,128]{3,2,1,0:T(8,128)(2,1)S(1)}, bf16[32,8,8,128]{3,2,1,0:T(8,128)(2,1)}, u32[]{:S(2)}) copy-start(bf16[32,8,8,128]{3,2,1,0:T(8,128)(2,1)} %param.11) | copy-start | bytes 1572868
  46.3 9.6 %copy-start.10 = (f32[32]{0:T(128)S(1)}, f32[32]{0:T(128)}, u32[]{:S(2)}) copy-start(f32[32]{0:T(128)} %param.8) | copy-start | bytes 388
  60.5 11.8 %copy-start.14 = (bf16[32,10,10,128]{3,0,2,1:T(8,128)(2,1)S(1)}, bf16[32,10,10,128]{3,0,2,1:T(8,128)(2,1)}, u32[]{:S(2)}) copy-start(bf16[32,10,10,128]{3,0,2,1:T(8,128)(2,1)} %copy-done.13) | copy-start | bytes 2457604
  72.3 4.1 %copy-start.2 = (bf16[8,4,8,8,128]{4,1,0,3,2:T(4,128)(2,1)}, bf16[8,4,8,8,128]{4,1,0,3,2:T(4,128)(2,1)S(1)}, u32[]{:S(2)}) copy-start(bf16[8,4,8,8,128]{4,1,0,3,2:T(4,128)(2,1)S(1)} %copy.23) | copy-start | bytes 1572868
  72.3 1.2 copy-start.12
  72.3 1.7 %copy-start.16 = (f32[32,10,10,128]{3,0,2,1:T(8,128)S(1)}, f32[32,10,10,128]{3,0,2,1:T(8,128)}, u32[]{:S(2)}) copy-start(f32[32,10,10,128]{3,0,2,1:T(8,128)} %get-tuple-element.19) | copy-start | bytes 4915204
  78.1 1.0 copy-start.6
  78.1 1.0 copy-start.8
  83.6 32.4 %all-to-all-start.3 = ((bf16[8,4,12,12,128]{4,1,3,2,0:T(4,128)(2,1)}), bf16[8,4,12,12,128]{4,1,3,2,0:T(4,128)(2,1)S(1)}, u32[]{:S(2)}, u32[]{:S(2)}) async-start(bf16[8,4,12,12,128]{4,1,3,2,0:T(4,128)(2,1)} %copy.24), calls=%async_computation.3 | async-start | bytes 2359296 | tf_op jit(solution)/shard_map/all_to_all | solution.py:116
  87.2 1.7 %copy-start.3 = (bf16[8,4,8,8,128]{4,1,0,3,2:T(4,128)(2,1)S(1)}, bf16[8,4,8,8,128]{4,1,0,3,2:T(4,128)(2,1)}, u32[]{:S(2)}) copy-start(bf16[8,4,8,8,128]{4,1,0,3,2:T(4,128)(2,1)} %copy-done.2) | copy-start | bytes 1572868
  87.2 1.7 %copy-start.15 = (bf16[32,10,10,128]{3,0,2,1:T(8,128)(2,1)S(1)}, bf16[32,10,10,128]{3,0,2,1:T(8,128)(2,1)}, u32[]{:S(2)}) copy-start(bf16[32,10,10,128]{3,0,2,1:T(8,128)(2,1)} %copy-done.13) | copy-start | bytes 2457604
  90.9 4.5 %copy-start.1 = (bf16[8,4,12,12,128]{4,1,0,3,2:T(4,128)(2,1)S(1)}, bf16[8,4,12,12,128]{4,1,0,3,2:T(4,128)(2,1)}, u32[]{:S(2)}) copy-start(bf16[8,4,12,12,128]{4,1,0,3,2:T(4,128)(2,1)} %copy-done) | copy-start | bytes 3538948
  91.3 22.6 %collective-permute-start.5 = (f32[3,3,128,128]{3,2,1,0:T(8,128)S(1)}, f32[3,3,128,128]{3,2,1,0:T(8,128)S(1)}, u32[]{:S(2)}, u32[]{:S(2)}) collective-permute-start(f32[3,3,128,128]{3,2,1,0:T(8,128)S(1)} %bitcast.224), channel_id=1, source_target_pairs={{0,1},{2,3},{4,5},{6,7},{8,9},{10,11},{12,13},{14,15},{16,17},{18,... | collective-permute-start | bytes 1769480 | tf_op jit(solution)/shard_map/ppermute | solution.py:124
  93.9 9.6 %collective-permute-start.6 = (bf16[3,3,128,128]{3,2,1,0:T(8,128)(2,1)S(1)}, bf16[3,3,128,128]{3,2,1,0:T(8,128)(2,1)S(1)}, u32[]{:S(2)}, u32[]{:S(2)}) collective-permute-start(bf16[3,3,128,128]{3,2,1,0:T(8,128)(2,1)S(1)} %convert_element_type.56), channel_id=1, source_target_pairs={{9,0},{1,8},{11,2},{3,10},{13,4},{5,12},{15,6},{7,14},{25,16},{17,... | collective-permute-start | bytes 884744 | tf_op jit(solution)/shard_map/ppermute | solution.py:123
  97.3 15.3 %collective-permute-start.3 = (bf16[3,3,128,128]{3,2,1,0:T(8,128)(2,1)S(1)}, bf16[3,3,128,128]{3,2,1,0:T(8,128)(2,1)S(1)}, u32[]{:S(2)}, u32[]{:S(2)}) collective-permute-start(bf16[3,3,128,128]{3,2,1,0:T(8,128)(2,1)S(1)} %convert_element_type.54), channel_id=1, source_target_pairs={{9,0},{1,8},{11,2},{3,10},{13,4},{5,12},{15,6},{7,14},{25,16},{17,... | collective-permute-start | bytes 884744 | tf_op jit(solution)/shard_map/ppermute | solution.py:123
  98.6 16.2 %collective-permute-start.2 = (f32[3,3,128,128]{3,2,1,0:T(8,128)S(1)}, f32[3,3,128,128]{3,2,1,0:T(8,128)S(1)}, u32[]{:S(2)}, u32[]{:S(2)}) collective-permute-start(f32[3,3,128,128]{3,2,1,0:T(8,128)S(1)} %bitcast.228), channel_id=1, source_target_pairs={{0,1},{2,3},{4,5},{6,7},{8,9},{10,11},{12,13},{14,15},{16,17},{18,... | collective-permute-start | bytes 1769480 | tf_op jit(solution)/shard_map/ppermute | solution.py:124
  103.5 10.3 %collective-permute-start.7 = (bf16[3,3,128,128]{3,2,1,0:T(8,128)(2,1)S(1)}, bf16[3,3,128,128]{3,2,1,0:T(8,128)(2,1)S(1)}, u32[]{:S(2)}, u32[]{:S(2)}) collective-permute-start(bf16[3,3,128,128]{3,2,1,0:T(8,128)(2,1)S(1)} %collective-permute-done.6), channel_id=1, source_target_pairs={{0,1},{2,3},{4,5},{6,7},{8,9},{10,11},{12,13},{14,15},{16,17},{18,... | collective-permute-start | bytes 884744 | tf_op jit(solution)/shard_map/ppermute | solution.py:126
  112.5 2.5 %collective-permute-start.4 = (bf16[3,3,128,128]{3,2,1,0:T(8,128)(2,1)S(1)}, bf16[3,3,128,128]{3,2,1,0:T(8,128)(2,1)S(1)}, u32[]{:S(2)}, u32[]{:S(2)}) collective-permute-start(bf16[3,3,128,128]{3,2,1,0:T(8,128)(2,1)S(1)} %collective-permute-done.3), channel_id=1, source_target_pairs={{0,1},{2,3},{4,5},{6,7},{8,9},{10,11},{12,13},{14,15},{16,17},{18,... | collective-permute-start | bytes 884744 | tf_op jit(solution)/shard_map/ppermute | solution.py:126

commit v2 on v1

v2 whole, which is shorter than its diff:
```python
import functools

import jax
import jax.numpy as jnp
from jax import lax
from jax.experimental import pallas as pl
from jax.experimental.pallas import tpu as pltpu
from jax.sharding import Mesh
from jax.sharding import PartitionSpec as P

SWAP = [(0, 3), (2, 1)]
SWAP_HOME = [(3, 0), (1, 2)]
TAPS = 3
BLOCK = 8
SLOTS = 2
PARAMS = pltpu.CompilerParams(vmem_limit_bytes=40 * 1024 * 1024)


def dot(left, right):
    return jnp.dot(left, right, preferred_element_type=jnp.float32)


def iota(shape, dim):
    return lax.broadcasted_iota(jnp.int32, shape, dim)


def onto_rows(row):
    count = row.shape[1]
    eye = iota((count, count), 0) == iota((count, count), 1)
    return jnp.sum(jnp.where(eye, row, 0.0), axis=1, keepdims=True)


def slot_matrix(key, chunk, peers, cells_first):
    patches = key.shape[1]
    earlier = iota((patches, patches), 0) < iota((patches, patches), 1)
    same = onto_rows(key) == key
    rank = jnp.sum(jnp.where(same & earlier, 1.0, 0.0), axis=0, keepdims=True)
    code = key * 8.0 + rank
    columns = BLOCK * patches
    spread_row = iota((patches, columns), 0)
    spread_col = iota((patches, columns), 1)
    hit = (spread_col % patches) == spread_row if cells_first else (spread_col // BLOCK) == spread_row
    spread = jnp.where(hit, 1.0, 0.0)
    code_wide = jnp.sum(onto_rows(code) * spread, axis=0, keepdims=True)
    rows = peers * BLOCK * SLOTS
    row = iota((rows, columns), 0)
    col = iota((rows, columns), 1)
    row_code = (row // (BLOCK * SLOTS)) * 8 + (row % SLOTS + chunk * SLOTS)
    row_cell = (row // SLOTS) % BLOCK
    col_cell = col // patches if cells_first else col % BLOCK
    match = (row_code.astype(jnp.float32) == code_wide) & (row_cell == col_cell)
    return jnp.where(match, 1.0, 0.0).astype(jnp.bfloat16)


def pack_kernel(chunk, key_ref, gate_ref, tiles_ref, cot_ref, *out_refs):
    peers = len(out_refs)
    step = BLOCK * SLOTS
    key = key_ref[...]
    pick = slot_matrix(key, chunk, peers, True)
    blocks = tiles_ref.shape[0]

    def put(at, values):
        values = values.astype(jnp.bfloat16)
        for peer in range(peers):
            out_refs[peer][at : at + step, :] = values[peer * step : (peer + 1) * step, :]

    for block in range(blocks):
        put(block * step, dot(pick, tiles_ref[block]))
    pick = slot_matrix(key, chunk, peers, False)
    gate = onto_rows(gate_ref[...])[:, :, None]
    patches, rows, cols, channels = cot_ref.shape
    for i in range(rows):
        scaled = cot_ref[:, i, :, :].astype(jnp.float32) * gate
        scaled = scaled.reshape(patches * cols, channels).astype(jnp.bfloat16)
        put((blocks + i) * step, dot(pick, scaled))


def unpack_kernel(peers, key_ref, gate_ref, cot_ref, *refs):
    chunks = (len(refs) - 3) // peers
    msgs, (out_ref, tiles_ref, gate_grad_ref) = refs[: chunks * peers], refs[chunks * peers :]
    step = BLOCK * SLOTS
    key = key_ref[...]

    def spread(cells_first):
        picks = [slot_matrix(key, chunk, peers, cells_first) for chunk in range(chunks)]
        return jnp.concatenate(picks, axis=0).T

    def gather(block):
        return jnp.concatenate([m[block * step : (block + 1) * step, :] for m in msgs], axis=0)

    blocks = tiles_ref.shape[0]
    pick = spread(True)
    for block in range(blocks):
        tiles_ref[block] = dot(pick, gather(block)).astype(jnp.bfloat16)
    pick = spread(False)
    gate = onto_rows(gate_ref[...])[:, :, None]
    patches, rows, cols, channels = cot_ref.shape
    total = jnp.zeros((patches, cols, channels), jnp.float32)
    for i in range(rows):
        result = dot(pick, gather(blocks + i)).reshape(patches, cols, channels)
        out_ref[:, i, :, :] = (result * gate).astype(jnp.bfloat16)
        total = total + result * cot_ref[:, i, :, :].astype(jnp.float32)
    sums = jnp.sum(jnp.sum(total, axis=1), axis=1, keepdims=True)
    eye = iota((patches, patches), 0) == iota((patches, patches), 1)
    gate_grad_ref[...] = jnp.sum(jnp.where(eye, sums, 0.0), axis=0, keepdims=True)


def mix_matrix(peers, inverse):
    size = peers * BLOCK * SLOTS
    mixed, apart = (1, 0) if inverse else (0, 1)
    a = iota((size, size), mixed)
    b = iota((size, size), apart)
    cell_a, rest = a // (peers * SLOTS), a % (peers * SLOTS)
    from_b = (rest // SLOTS) * (BLOCK * SLOTS) + cell_a * SLOTS + rest % SLOTS
    return jnp.where(from_b == b, 1.0, 0.0).astype(jnp.bfloat16)


def expert_kernel(peers, side, *refs):
    msgs = refs[:peers]
    one_ref, two_ref, one_t_ref, two_t_ref = refs[peers : peers + 4]
    backs = refs[peers + 4 : 2 * peers + 4]
    x_ref, h_ref, g_ref, m_ref, slope_ref, t_ref = refs[2 * peers + 4 :]
    step = BLOCK * SLOTS
    wide = peers * SLOTS
    mid, out = side - 2, side - 4
    blocks = side * side // BLOCK
    size = BLOCK * wide

    def gather(block):
        return jnp.concatenate([m[block * step : (block + 1) * step, :] for m in msgs], axis=0)

    def window(ref, cols, row, col, count):
        at = (row * cols + col) * wide
        return ref[at : at + count * wide, :]

    mix = mix_matrix(peers, False)
    for block in range(blocks):
        x_ref[block * size : (block + 1) * size, :] = dot(mix, gather(block)).astype(jnp.bfloat16)
    for i in range(mid):
        lhs = jnp.concatenate(
            [window(x_ref, side, i + a, b, mid) for a in range(TAPS) for b in range(TAPS)], axis=1
        )
        pre = dot(lhs, one_ref[...])
        sigma = jax.nn.sigmoid(pre)
        rows = slice(i * mid * wide, (i + 1) * mid * wide)
        h_ref[rows, :] = (pre * sigma).astype(jnp.bfloat16)
        slope_ref[rows, :] = sigma * (1.0 + pre * (1.0 - sigma))

    apart = mix_matrix(peers, True)

    def put(block, values):
        values = dot(apart, values).astype(jnp.bfloat16)
        for peer in range(peers):
            backs[peer][block * step : (block + 1) * step, :] = values[peer * step : (peer + 1) * step, :]

    for i in range(out):
        lhs = jnp.concatenate(
            [window(h_ref, mid, i + a, b, out) for a in range(TAPS) for b in range(TAPS)], axis=1
        )
        put(blocks + i, dot(lhs, two_ref[...]).astype(jnp.bfloat16))

    blank = jnp.zeros((2 * wide, x_ref.shape[1]), jnp.bfloat16)
    for i in range(out):
        at = i * (out + 4) * wide
        g_ref[at : at + 2 * wide, :] = blank
        g_ref[at + 2 * wide : at + 2 * wide + size, :] = dot(mix, gather(blocks + i)).astype(jnp.bfloat16)
        g_ref[at + 2 * wide + size : at + 4 * wide + size, :] = blank

    def transposed(ref, kernel_ref, rows, i):
        taps = [a for a in range(TAPS) if 0 <= i - a < rows]
        lhs = jnp.concatenate(
            [window(ref, rows + 4, i - a, 2 - b, rows + 2) for a in taps for b in range(TAPS)], axis=1
        )
        per = TAPS * x_ref.shape[1]
        return dot(lhs, kernel_ref[taps[0] * per : (taps[-1] + 1) * per, :])

    for i in range(mid):
        at = i * (mid + 4) * wide
        grad_mid = transposed(g_ref, two_t_ref, out, i) * slope_ref[i * mid * wide : (i + 1) * mid * wide, :]
        m_ref[at : at + 2 * wide, :] = blank
        m_ref[at + 2 * wide : at + (mid + 2) * wide, :] = grad_mid.astype(jnp.bfloat16)
        m_ref[at + (mid + 2) * wide : at + (mid + 4) * wide, :] = blank
    for i in range(side):
        t_ref[i * side * wide : (i + 1) * side * wide, :] = transposed(m_ref, one_t_ref, mid, i).astype(
            jnp.bfloat16
        )
    for block in range(blocks):
        put(block, t_ref[block * size : (block + 1) * size, :])


def sums_kernel(side, wide, last, *refs):
    x_ref, h_ref, g_ref, m_ref = refs[:4]
    refs = refs[4:]
    before = None
    if last:
        before, refs = refs[:2], refs[2:]
    mid, out = side - 2, side - 4

    def one(in_ref, cols, grad_ref, rows, k):
        grads = [
            grad_ref[(i * (rows + 4) + 2) * wide : (i * (rows + 4) + 2 + rows) * wide, :] for i in range(rows)
        ]
        grad_t = jnp.concatenate(grads, axis=0).T
        for tap in range(TAPS * TAPS):
            a, b = divmod(tap, TAPS)
            window = jnp.concatenate(
                [
                    in_ref[((i + a) * cols + b) * wide : ((i + a) * cols + b + rows) * wide, :]
                    for i in range(rows)
                ],
                axis=0,
            )
            total = dot(grad_t, window)
            if last:
                total = (total + before[k][tap]).T
                refs[2 + k][tap] = total.astype(jnp.bfloat16)
            refs[k][tap] = total

    one(h_ref, mid, g_ref, out, 1)
    one(x_ref, side, m_ref, mid, 0)


def shards(tiles, route, gate, conv_first, conv_second, cotangent):
    halves = lax.axis_size("half")
    per_half = lax.axis_size("owner")
    cores = lax.axis_size("replica")
    half = lax.axis_index("half")
    core = lax.axis_index("replica")
    me = lax.axis_index("owner") * cores + core
    peers = per_half * cores
    patches, side, _, channels = tiles.shape
    out_side = cotangent.shape[1]
    capacity = max(2, (patches + peers - 1) // peers)
    chunks = capacity // SLOTS
    blocks = side * side // BLOCK
    message = (side * side + out_side * out_side) * SLOTS
    wide = peers * SLOTS

    other_one, other_two = (
        lax.ppermute(k[0], ("half", "replica"), SWAP) for k in (conv_first, conv_second)
    )
    route_core = (route // per_half - half + halves) % halves
    key = ((((route % per_half) * cores + route_core) ^ me).astype(jnp.float32))[None, :]
    gate_row = gate[None, :]
    tiles_rows = jnp.transpose(tiles, (1, 2, 0, 3)).reshape(blocks, BLOCK * patches, channels)

    bf16 = functools.partial(jax.ShapeDtypeStruct, dtype=jnp.bfloat16)
    f32 = functools.partial(jax.ShapeDtypeStruct, dtype=jnp.float32)

    def exchange(messages):
        got = [messages[0]]
        for mask in range(1, peers):
            pairs = [(i, i ^ mask) for i in range(peers)]
            got.append(lax.ppermute(messages[mask], ("owner", "replica"), pairs))
        return got

    def pack(chunk):
        return pl.pallas_call(
            functools.partial(pack_kernel, chunk),
            out_shape=[bf16((message, channels))] * peers,
            compiler_params=PARAMS,
            name="pack",
        )(key, gate_row, tiles_rows, cotangent)

    arrived = [exchange(pack(chunk)) for chunk in range(chunks)]

    kernel_one = jnp.where(core == 0, conv_first[0], other_one)
    kernel_two = jnp.where(core == 0, conv_second[0], other_two)
    flat = (TAPS * TAPS * channels, channels)
    weights = (
        kernel_one.reshape(flat),
        kernel_two.reshape(flat),
        jnp.swapaxes(kernel_one, 2, 3).reshape(flat),
        jnp.swapaxes(kernel_two, 2, 3).reshape(flat),
    )
    mid = side - 2
    kept = [
        bf16((side * side * wide, channels)),
        bf16((mid * mid * wide, channels)),
        bf16((out_side * side * wide, channels)),
        bf16((mid * (mid + 4) * wide, channels)),
    ]

    def expert(messages):
        result = pl.pallas_call(
            functools.partial(expert_kernel, peers, side),
            out_shape=[bf16((message, channels))] * peers + kept,
            scratch_shapes=[
                pltpu.VMEM((mid * mid * wide, channels), jnp.float32),
                pltpu.VMEM((side * side * wide, channels), jnp.bfloat16),
            ],
            compiler_params=PARAMS,
            name="expert",
        )(*messages, *weights)
        return result[:peers], result[peers:]

    def sums(held, before):
        last = before is not None or chunks == 1
        shape = (TAPS * TAPS, channels, channels)
        return pl.pallas_call(
            functools.partial(sums_kernel, side, wide, before is not None),
            out_shape=[f32(shape)] * 2 + ([bf16(shape)] * 2 if before is not None else []),
            compiler_params=PARAMS,
            name="sums",
        )(*held, *(before or []))

    backs, total = [], None
    for messages in arrived:
        back, held = expert(messages)
        backs.append(exchange(back))
        if total is None:
            shape = (TAPS * TAPS, channels, channels)
            total = [jnp.zeros(shape, jnp.float32)] * 2 if chunks == 1 else None
        total = sums(held, total)

    def combine(local, short):
        away = lax.ppermute(short, ("half", "replica"), SWAP_HOME)
        beside = lax.ppermute(local, "replica", [(0, 1)])
        own = jnp.where(core == 0, local, beside)
        passed = lax.ppermute(away, "replica", [(0, 1)])
        total = own + jnp.where(core == 0, away, passed).astype(jnp.float32)
        return total.reshape((1, TAPS, TAPS) + total.shape[1:])

    first_grad = combine(total[0], total[2])
    second_grad = combine(total[1], total[3])
    output, tiles_out, gate_grad = pl.pallas_call(
        functools.partial(unpack_kernel, peers),
        out_shape=[
            bf16(cotangent.shape),
            bf16(tiles_rows.shape),
            f32((1, patches)),
        ],
        compiler_params=PARAMS,
        name="unpack",
    )(key, gate_row, cotangent, *[m for back in backs for m in back])
    tiles_grad = jnp.transpose(tiles_out.reshape(side, side, patches, channels), (2, 0, 1, 3))
    return (output, tiles_grad, first_grad, second_grad, gate_grad[0])


def solution(mesh):
    groups, experts, cores = (mesh.shape[a] for a in ("groups", "expert", "replica"))
    mesh = Mesh(
        mesh.devices.reshape(groups, cores, experts // cores, cores),
        ("groups", "half", "owner", "replica"),
    )
    every = ("groups", "half", "owner", "replica")
    placed = (
        P(every, None, None, None),
        P(every),
        P(every),
        P(("half", "owner"), None, None, None, None),
        P(("half", "owner"), None, None, None, None),
        P(every, None, None, None),
    )
    return jax.shard_map(
        shards,
        mesh=mesh,
        in_specs=placed,
        out_specs=(
            P(every, None, None, None),
            P(every, None, None, None),
            P(("groups", "half", "owner"), None, None, None, None),
            P(("groups", "half", "owner"), None, None, None, None),
            P(every),
        ),
        check_vma=False,
    )
```

time: 120 us -> 98.4 us (0.82)
  Pallas kernels: 0 us -> 18.3 us
  matrix products: 18.2 us -> 0 us
  local copies, waits for them, and re-layouts: 17.9 us -> 3.43 us
  blocking collectives: 11.6 us -> 0 us
  starting transfers between devices: 33.5 us -> 44.9 us
  other arithmetic: 5.78 us -> 2.64 us
  waiting for transfers between devices: 30.8 us -> 27.8 us
    ppermute x4 -> x32, starting transfers between devices: 9.42 us -> 34.4 us  [the longest x28 24.3 us: exchange(): got.append(lax.ppermute(messages[mask], ('owner', 'replica'), pairs))]
    all_to_all x3 -> x0, waiting for transfers between devices: 24.4 us -> none  [the longest x1 15.5 us: shards(): lax.all_to_all(to_slots(tiles), ('owner', 'replica'), split_axis=0, conca...]
    ppermute x4 -> x32, waiting for transfers between devices: 6.24 us -> 27.8 us  [the longest x28 27.8 us: exchange(): got.append(lax.ppermute(messages[mask], ('owner', 'replica'), pairs))]
    pallas_call x0 -> x7, Pallas kernels: none -> 18.3 us  [the longest x2 10.4 us: expert(): pl.pallas_call(functools.partial(expert_kernel, peers, side), out_shape=[...]
    all_to_all x3 -> x0, starting transfers between devices: 12.4 us -> none  [the longest x1 5.39 us: shards(): lax.all_to_all(to_slots(tiles), ('owner', 'replica'), split_axis=0, conca...]
    all_to_all x1 -> x0, blocking collectives: 11.6 us -> none  [shards(): lax.all_to_all(to_slots(scaled), ('owner', 'replica'), split_axis=0, conc...]
    conv_general_dilated x4 -> x0, matrix products: 9.97 us -> none  [convolve(): lax.conv_general_dilated(inputs, kernel, (1, 1), 'VALID', dimension_numbe...]
    dot_general x18 -> x0, matrix products: 8.19 us -> none  [kernel_grad(): jnp.einsum('nijc,nijd->cd', window, gradient, preferred_element_type=jnp....]
  transfers between devices with their start and end apart: 11 -> 36, of which waited for: 4 -> 12; matrix products, arithmetic and copies ran while one was open for 10% -> 2% of each run, Pallas kernels for 0% -> 19%
where the time goes in v2:
time: 98.4 us; the launch traced here: 98 us
  starting transfers between devices  44.9 us (46%)
  waiting for transfers between devices  27.8 us (28%)
  Pallas kernels  18.3 us (19%)
  local copies, waits for them, and re-layouts  3.43 us (3%)
  other arithmetic  2.64 us (3%)
    ppermute x28, waiting for transfers between devices, exchange(): got.append(lax.ppermute(messages[mask], ('owner', 'replica'), pairs))  27.8 us
    ppermute x28, starting transfers between devices, exchange(): got.append(lax.ppermute(messages[mask], ('owner', 'replica'), pairs))  24.3 us
    pallas_call x2, Pallas kernels, expert(): pl.pallas_call(functools.partial(expert_kernel, peers, side), out_shape=[...  10.4 us
    ppermute x2, starting transfers between devices, shards(): lax.ppermute(k[0], ('half', 'replica'), SWAP)  7.53 us
    ppermute x2, starting transfers between devices, combine(): beside = lax.ppermute(local, 'replica', [(0, 1)])  6.9 us
    pallas_call x2, Pallas kernels, sums(): pl.pallas_call(functools.partial(sums_kernel, side, wide, before is not N...  3.93 us
    ppermute x2, starting transfers between devices, combine(): passed = lax.ppermute(away, 'replica', [(0, 1)])  3.61 us
    unnamed x14, local copies, waits for them, and re-layouts  2.98 us
  transfers between devices with their start and end apart: 36, of which 12 were waited for; matrix products, arithmetic and copies ran while one was open for 2% of the time, Pallas kernels for 19%

profile of v2, /device:TPU:0, one launch (start us, length us, event | category | flops | bytes accessed | tf_op | source)
XLA Modules:
  0.0 98.0 jit_solution(10999642919115688784)
XLA Ops:
  0.6 5.4 %collective-permute-start.8 = (bf16[3,3,128,128]{3,2,1,0:T(8,128)(2,1)}, bf16[3,3,128,128]{3,2,1,0:T(8,128)(2,1)S(1)}, u32[]{:S(2)}, u32[]{:S(2)}) collective-permute-start(bf16[3,3,128,128]{3,2,1,0:T(8,128)(2,1)} %bitcast.39), channel_id=1, source_target_pairs={{0,9},{8,1},{2,11},{10,3},{4,13},{12,5},{6,15},{14,7},{16,25},{24,... | collective-permute-start | bytes 884744 | tf_op jit(solution)/shard_map/ppermute | solution.py:240
  6.0 0.7 convert_bitcast_fusion.key_ref
  6.7 1.0 %copy-done = bf16[32,8,8,128]{3,2,1,0:T(8,128)(2,1)S(1)} copy-done((bf16[32,8,8,128]{3,2,1,0:T(8,128)(2,1)S(1)}, bf16[32,8,8,128]{3,2,1,0:T(8,128)(2,1)}, u32[]{:S(2)}) %copy-start) | copy-done | bytes 524312
  7.8 1.3 %copy-done.2 = bf16[32,12,12,128]{3,0,2,1:T(8,128)(2,1)S(1)} copy-done((bf16[32,12,12,128]{3,0,2,1:T(8,128)(2,1)S(1)}, bf16[32,12,12,128]{3,0,2,1:T(8,128)(2,1)}, u32[]{:S(2)}) %copy-start.2) | copy-done | bytes 1179672
  9.0 0.7 copy-done.3
  9.7 0.8 pack.2
  10.6 1.6 %collective-permute-start.1 = (bf16[416,128]{1,0:T(8,128)(2,1)S(1)}, bf16[416,128]{1,0:T(8,128)(2,1)S(1)}, u32[]{:S(2)}, u32[]{:S(2)}) collective-permute-start(bf16[416,128]{1,0:T(8,128)(2,1)S(1)} %get-tuple-element.56), channel_id=1, source_target_pairs={{0,2},{1,3},{2,0},{3,1},{4,6},{5,7},{6,4},{7,5},{8,10},{9,11},{10,... | collective-permute-start | bytes 319496 | tf_op jit(solution)/shard_map/ppermute | solution.py:254
  12.2 0.8 pack.3
  13.2 0.5 collective-permute-start.17
  13.7 1.2 %collective-permute-start.18 = (bf16[416,128]{1,0:T(8,128)(2,1)S(1)}, bf16[416,128]{1,0:T(8,128)(2,1)S(1)}, u32[]{:S(2)}, u32[]{:S(2)}) collective-permute-start(bf16[416,128]{1,0:T(8,128)(2,1)S(1)} %get-tuple-element.73), channel_id=1, source_target_pairs={{0,3},{1,2},{2,1},{3,0},{4,7},{5,6},{6,5},{7,4},{8,11},{9,10},{10,... | collective-permute-start | bytes 319496 | tf_op jit(solution)/shard_map/ppermute | solution.py:254
  14.9 1.1 %collective-permute-done.1.refs_2_ = bf16[416,128]{1,0:T(8,128)(2,1)S(1)} collective-permute-done((bf16[416,128]{1,0:T(8,128)(2,1)S(1)}, bf16[416,128]{1,0:T(8,128)(2,1)S(1)}, u32[]{:S(2)}, u32[]{:S(2)}) %collective-permute-start.1) | collective-permute-done | bytes 106528 | tf_op jit(solution)/shard_map/ppermute | solution.py:254
  16.0 2.1 %collective-permute-start.7 = (bf16[3,3,128,128]{3,2,1,0:T(8,128)(2,1)S(1)}, bf16[3,3,128,128]{3,2,1,0:T(8,128)(2,1)}, u32[]{:S(2)}, u32[]{:S(2)}) collective-permute-start(bf16[3,3,128,128]{3,2,1,0:T(8,128)(2,1)S(1)} %bitcast.40), channel_id=1, source_target_pairs={{0,9},{8,1},{2,11},{10,3},{4,13},{12,5},{6,15},{14,7},{16,25},{24,... | collective-permute-start | bytes 884744 | tf_op jit(solution)/shard_map/ppermute | solution.py:240
  18.1 1.7 %collective-permute-start.19 = (bf16[416,128]{1,0:T(8,128)(2,1)S(1)}, bf16[416,128]{1,0:T(8,128)(2,1)S(1)}, u32[]{:S(2)}, u32[]{:S(2)}) collective-permute-start(bf16[416,128]{1,0:T(8,128)(2,1)S(1)} %get-tuple-element.74), channel_id=1, source_target_pairs={{0,4},{1,5},{2,6},{3,7},{4,0},{5,1},{6,2},{7,3},{8,12},{9,13},{10,... | collective-permute-start | bytes 319496 | tf_op jit(solution)/shard_map/ppermute | solution.py:254
  20.1 2.5 %collective-permute-start.21 = (bf16[416,128]{1,0:T(8,128)(2,1)S(1)}, bf16[416,128]{1,0:T(8,128)(2,1)S(1)}, u32[]{:S(2)}, u32[]{:S(2)}) collective-permute-start(bf16[416,128]{1,0:T(8,128)(2,1)S(1)} %get-tuple-element.76), channel_id=1, source_target_pairs={{0,6},{1,7},{2,4},{3,5},{4,2},{5,3},{6,0},{7,1},{8,14},{9,15},{10,... | collective-permute-start | bytes 319496 | tf_op jit(solution)/shard_map/ppermute | solution.py:254
  22.9 3.7 %collective-permute-done.19.refs_4_ = bf16[416,128]{1,0:T(8,128)(2,1)S(1)} collective-permute-done((bf16[416,128]{1,0:T(8,128)(2,1)S(1)}, bf16[416,128]{1,0:T(8,128)(2,1)S(1)}, u32[]{:S(2)}, u32[]{:S(2)}) %collective-permute-start.19) | collective-permute-done | bytes 106528 | tf_op jit(solution)/shard_map/ppermute | solution.py:254
  26.7 1.8 %collective-permute-done.20.refs_5_ = bf16[416,128]{1,0:T(8,128)(2,1)S(1)} collective-permute-done((bf16[416,128]{1,0:T(8,128)(2,1)S(1)}, bf16[416,128]{1,0:T(8,128)(2,1)S(1)}, u32[]{:S(2)}, u32[]{:S(2)}) %collective-permute-start.20) | collective-permute-done | bytes 106528 | tf_op jit(solution)/shard_map/ppermute | solution.py:254
  28.5 0.7 collective-permute-start.3
  29.2 3.2 %collective-permute-done.21.refs_6_ = bf16[416,128]{1,0:T(8,128)(2,1)S(1)} collective-permute-done((bf16[416,128]{1,0:T(8,128)(2,1)S(1)}, bf16[416,128]{1,0:T(8,128)(2,1)S(1)}, u32[]{:S(2)}, u32[]{:S(2)}) %collective-permute-start.21) | collective-permute-done | bytes 106528 | tf_op jit(solution)/shard_map/ppermute | solution.py:254
  32.3 0.6 collective-permute-done.22.refs_7_
  32.9 0.9 collective-permute-start.5
  33.8 2.5 %collective-permute-start.6 = (bf16[416,128]{1,0:T(8,128)(2,1)S(1)}, bf16[416,128]{1,0:T(8,128)(2,1)S(1)}, u32[]{:S(2)}, u32[]{:S(2)}) collective-permute-start(bf16[416,128]{1,0:T(8,128)(2,1)S(1)} %get-tuple-element.61), channel_id=1, source_target_pairs={{0,7},{1,6},{2,5},{3,4},{4,3},{5,2},{6,1},{7,0},{8,15},{9,14},{10,... | collective-permute-start | bytes 319496 | tf_op jit(solution)/shard_map/ppermute | solution.py:254
  36.8 5.2 %expert.3 = (bf16[416,128]{1,0:T(8,128)(2,1)S(1)}, bf16[416,128]{1,0:T(8,128)(2,1)S(1)}, bf16[416,128]{1,0:T(8,128)(2,1)S(1)}, bf16[416,128]{1,0:T(8,128)(2,1)S(...) custom-call(bf16[416,128]{1,0:T(8,128)(2,1)S(1)} %get-tuple-element., ...), custom_call_target="tpu_custom_call" | custom-call | tf_op jit(solution)/shard_map/expert/pallas_call | solution.py:285
  42.0 0.6 collective-permute-start.23
  43.0 1.1 %collective-permute-start.25 = (bf16[416,128]{1,0:T(8,128)(2,1)S(1)}, bf16[416,128]{1,0:T(8,128)(2,1)S(1)}, u32[]{:S(2)}, u32[]{:S(2)}) collective-permute-start(bf16[416,128]{1,0:T(8,128)(2,1)S(1)} %get-tuple-element.81), channel_id=1, source_target_pairs={{0,3},{1,2},{2,1},{3,0},{4,7},{5,6},{6,5},{7,4},{8,11},{9,10},{10,... | collective-permute-start | bytes 319496 | tf_op jit(solution)/shard_map/ppermute | solution.py:254
  44.1 0.5 collective-permute-start.26
  44.6 1.6 %collective-permute-start.27 = (bf16[416,128]{1,0:T(8,128)(2,1)S(1)}, bf16[416,128]{1,0:T(8,128)(2,1)S(1)}, u32[]{:S(2)}, u32[]{:S(2)}) collective-permute-start(bf16[416,128]{1,0:T(8,128)(2,1)S(1)} %get-tuple-element.83), channel_id=1, source_target_pairs={{0,5},{1,4},{2,7},{3,6},{4,1},{5,0},{6,3},{7,2},{8,13},{9,12},{10,... | collective-permute-start | bytes 319496 | tf_op jit(solution)/shard_map/ppermute | solution.py:254
  46.2 5.2 %expert.2 = (bf16[416,128]{1,0:T(8,128)(2,1)S(1)}, bf16[416,128]{1,0:T(8,128)(2,1)S(1)}, bf16[416,128]{1,0:T(8,128)(2,1)S(1)}, bf16[416,128]{1,0:T(8,128)(2,1)S(...) custom-call(bf16[416,128]{1,0:T(8,128)(2,1)S(1)} %get-tuple-element., ...), custom_call_target="tpu_custom_call" | custom-call | tf_op jit(solution)/shard_map/expert/pallas_call | solution.py:285
  51.4 2.0 %sums.2 = (f32[9,128,128]{2,1,0:T(8,128)S(1)}, f32[9,128,128]{2,1,0:T(8,128)S(1)}) custom-call(bf16[2304,128]{1,0:T(8,128)(2,1)S(1)} %get-tuple-element.92.refs_0_, bf16[1600,128]{1,0:T(8,128)(2,1)S(1)} %get-tuple-element.93.refs_1_, bf16[1536,128]{1,0:T(8,128)(2,1)S(1)} %get-tuple-element.94.refs_2_, bf16[2240,128]{1,0:T(8,128)(2,1)S(1)} %get-tuple-element.95.refs_3_), custom_call_target="tpu_custom_call" | custom-call | tf_op jit(solution)/shard_map/sums/pallas_call | solution.py:300
  53.5 1.9 %sums.3 = (f32[9,128,128]{2,1,0:T(8,128)S(1)}, f32[9,128,128]{2,1,0:T(8,128)S(1)}, bf16[9,128,128]{2,1,0:T(8,128)(2,1)S(1)}, bf16[9,128,128]{2,1,0:T(8,128)(2,1)S(1)}) custom-call(bf16[2304,128]{1,0:T(8,128)(2,1)S(1)} %get-tuple-element.88.refs_0_, bf16[1600,128]{1,0:T(8,128)(2,1)S(1)} %get-tuple-element.89.refs_1_, ...), custom_call_target="tpu_custom_call" | custom-call | tf_op jit(solution)/shard_map/sums/pallas_call | solution.py:300
  55.4 1.3 %collective-permute-start.34 = (bf16[9,128,128]{2,1,0:T(8,128)(2,1)S(1)}, bf16[9,128,128]{2,1,0:T(8,128)(2,1)S(1)}, u32[]{:S(2)}, u32[]{:S(2)}) collective-permute-start(bf16[9,128,128]{2,1,0:T(8,128)(2,1)S(1)} %get-tuple-element.101), channel_id=1, source_target_pairs={{9,0},{1,8},{11,2},{3,10},{13,4},{5,12},{15,6},{7,14},{25,16},{17,... | collective-permute-start | bytes 884744 | tf_op jit(solution)/shard_map/ppermute | solution.py:317
  56.7 4.0 %collective-permute-start.33 = (f32[9,128,128]{2,1,0:T(8,128)S(1)}, f32[9,128,128]{2,1,0:T(8,128)S(1)}, u32[]{:S(2)}, u32[]{:S(2)}) collective-permute-start(f32[9,128,128]{2,1,0:T(8,128)S(1)} %get-tuple-element.100), channel_id=1, source_target_pairs={{0,1},{2,3},{4,5},{6,7},{8,9},{10,11},{12,13},{14,15},{16,17},{18,... | collective-permute-start | bytes 1769480 | tf_op jit(solution)/shard_map/ppermute | solution.py:318
  60.7 1.6 %collective-permute-start.28 = (bf16[416,128]{1,0:T(8,128)(2,1)S(1)}, bf16[416,128]{1,0:T(8,128)(2,1)S(1)}, u32[]{:S(2)}, u32[]{:S(2)}) collective-permute-start(bf16[416,128]{1,0:T(8,128)(2,1)S(1)} %get-tuple-element.84), channel_id=1, source_target_pairs={{0,6},{1,7},{2,4},{3,5},{4,2},{5,3},{6,0},{7,1},{8,14},{9,15},{10,... | collective-permute-start | bytes 319496 | tf_op jit(solution)/shard_map/ppermute | solution.py:254
  62.4 1.5 %collective-permute-start.10 = (bf16[416,128]{1,0:T(8,128)(2,1)S(1)}, bf16[416,128]{1,0:T(8,128)(2,1)S(1)}, u32[]{:S(2)}, u32[]{:S(2)}) collective-permute-start(bf16[416,128]{1,0:T(8,128)(2,1)S(1)} %get-tuple-element.64), channel_id=1, source_target_pairs={{0,2},{1,3},{2,0},{3,1},{4,6},{5,7},{6,4},{7,5},{8,10},{9,11},{10,... | collective-permute-start | bytes 319496 | tf_op jit(solution)/shard_map/ppermute | solution.py:254
  63.9 5.6 %collective-permute-done.28.refs_14_ = bf16[416,128]{1,0:T(8,128)(2,1)S(1)} collective-permute-done((bf16[416,128]{1,0:T(8,128)(2,1)S(1)}, bf16[416,128]{1,0:T(8,128)(2,1)S(1)}, u32[]{:S(2)}, u32[]{:S(2)}) %collective-permute-start.28) | collective-permute-done | bytes 106528 | tf_op jit(solution)/shard_map/ppermute | solution.py:254
  69.7 1.0 %collective-permute-start.12 = (bf16[416,128]{1,0:T(8,128)(2,1)S(1)}, bf16[416,128]{1,0:T(8,128)(2,1)S(1)}, u32[]{:S(2)}, u32[]{:S(2)}) collective-permute-start(bf16[416,128]{1,0:T(8,128)(2,1)S(1)} %get-tuple-element.66), channel_id=1, source_target_pairs={{0,4},{1,5},{2,6},{3,7},{4,0},{5,1},{6,2},{7,3},{8,12},{9,13},{10,... | collective-permute-start | bytes 319496 | tf_op jit(solution)/shard_map/ppermute | solution.py:254
  70.7 0.5 collective-permute-done.10.refs_2_
  71.2 1.6 %collective-permute-start.13 = (bf16[416,128]{1,0:T(8,128)(2,1)S(1)}, bf16[416,128]{1,0:T(8,128)(2,1)S(1)}, u32[]{:S(2)}, u32[]{:S(2)}) collective-permute-start(bf16[416,128]{1,0:T(8,128)(2,1)S(1)} %get-tuple-element.67), channel_id=1, source_target_pairs={{0,5},{1,4},{2,7},{3,6},{4,1},{5,0},{6,3},{7,2},{8,13},{9,12},{10,... | collective-permute-start | bytes 319496 | tf_op jit(solution)/shard_map/ppermute | solution.py:254
  72.9 1.6 %collective-permute-done.11.refs_3_ = bf16[416,128]{1,0:T(8,128)(2,1)S(1)} collective-permute-done((bf16[416,128]{1,0:T(8,128)(2,1)S(1)}, bf16[416,128]{1,0:T(8,128)(2,1)S(1)}, u32[]{:S(2)}, u32[]{:S(2)}) %collective-permute-start.11) | collective-permute-done | bytes 106528 | tf_op jit(solution)/shard_map/ppermute | solution.py:254
  74.8 1.3 %collective-permute-start.31 = (bf16[9,128,128]{2,1,0:T(8,128)(2,1)S(1)}, bf16[9,128,128]{2,1,0:T(8,128)(2,1)S(1)}, u32[]{:S(2)}, u32[]{:S(2)}) collective-permute-start(bf16[9,128,128]{2,1,0:T(8,128)(2,1)S(1)} %get-tuple-element.99), channel_id=1, source_target_pairs={{9,0},{1,8},{11,2},{3,10},{13,4},{5,12},{15,6},{7,14},{25,16},{17,... | collective-permute-start | bytes 884744 | tf_op jit(solution)/shard_map/ppermute | solution.py:317
  76.1 1.7 %collective-permute-done.13.refs_5_ = bf16[416,128]{1,0:T(8,128)(2,1)S(1)} collective-permute-done((bf16[416,128]{1,0:T(8,128)(2,1)S(1)}, bf16[416,128]{1,0:T(8,128)(2,1)S(1)}, u32[]{:S(2)}, u32[]{:S(2)}) %collective-permute-start.13) | collective-permute-done | bytes 106528 | tf_op jit(solution)/shard_map/ppermute | solution.py:254
  77.8 2.9 %collective-permute-start.30 = (f32[9,128,128]{2,1,0:T(8,128)S(1)}, f32[9,128,128]{2,1,0:T(8,128)S(1)}, u32[]{:S(2)}, u32[]{:S(2)}) collective-permute-start(f32[9,128,128]{2,1,0:T(8,128)S(1)} %get-tuple-element.98), channel_id=1, source_target_pairs={{0,1},{2,3},{4,5},{6,7},{8,9},{10,11},{12,13},{14,15},{16,17},{18,... | collective-permute-start | bytes 1769480 | tf_op jit(solution)/shard_map/ppermute | solution.py:318
  80.7 1.3 %collective-permute-start.35 = (bf16[9,128,128]{2,1,0:T(8,128)(2,1)S(1)}, bf16[9,128,128]{2,1,0:T(8,128)(2,1)S(1)}, u32[]{:S(2)}, u32[]{:S(2)}) collective-permute-start(bf16[9,128,128]{2,1,0:T(8,128)(2,1)S(1)} %collective-permute-done.34), channel_id=1, source_target_pairs={{0,1},{2,3},{4,5},{6,7},{8,9},{10,11},{12,13},{14,15},{16,17},{18,... | collective-permute-start | bytes 884744 | tf_op jit(solution)/shard_map/ppermute | solution.py:320
  82.0 1.7 %collective-permute-start.15 = (bf16[416,128]{1,0:T(8,128)(2,1)S(1)}, bf16[416,128]{1,0:T(8,128)(2,1)S(1)}, u32[]{:S(2)}, u32[]{:S(2)}) collective-permute-start(bf16[416,128]{1,0:T(8,128)(2,1)S(1)} %get-tuple-element.69), channel_id=1, source_target_pairs={{0,7},{1,6},{2,5},{3,4},{4,3},{5,2},{6,1},{7,0},{8,15},{9,14},{10,... | collective-permute-start | bytes 319496 | tf_op jit(solution)/shard_map/ppermute | solution.py:254
  83.7 7.4 %collective-permute-done.15.refs_7_ = bf16[416,128]{1,0:T(8,128)(2,1)S(1)} collective-permute-done((bf16[416,128]{1,0:T(8,128)(2,1)S(1)}, bf16[416,128]{1,0:T(8,128)(2,1)S(1)}, u32[]{:S(2)}, u32[]{:S(2)}) %collective-permute-start.15) | collective-permute-done | bytes 106528 | tf_op jit(solution)/shard_map/ppermute | solution.py:254
  91.3 2.3 %collective-permute-start.32 = (bf16[9,128,128]{2,1,0:T(8,128)(2,1)S(1)}, bf16[9,128,128]{2,1,0:T(8,128)(2,1)S(1)}, u32[]{:S(2)}, u32[]{:S(2)}) collective-permute-start(bf16[9,128,128]{2,1,0:T(8,128)(2,1)S(1)} %collective-permute-done.31), channel_id=1, source_target_pairs={{0,1},{2,3},{4,5},{6,7},{8,9},{10,11},{12,13},{14,15},{16,17},{18,... | collective-permute-start | bytes 884744 | tf_op jit(solution)/shard_map/ppermute | solution.py:320
  93.6 2.5 %unpack.1 = (bf16[32,8,8,128]{3,2,1,0:T(8,128)(2,1)}, bf16[18,256,128]{2,1,0:T(8,128)(2,1)}, f32[1,32]{1,0:T(1,128)}) custom-call(f32[1,32]{1,0:T(1,128)S(1)} %convert_bitcast_fusion.key_ref, f32[1,32]{1,0:T(1,128)S(1)} %bitcast.36, bf16[32,8,8,128]{3,2,1,0:T(8,128)(2,1)S(1)} %copy-done.1, bf16[416,128]{1,0:T(8,128)(2,1)S(1)} %get-tuple-element.62.refs_0_, ...), custom_call_target="tpu_custom_call" | custom-call | tf_op jit(solution)/shard_map/unpack/pallas_call | solution.py:326
  96.1 0.9 convert_add_fusion
  97.0 0.9 convert_add_fusion.1
  (52 shorter events, 2.6 us)
Async XLA Ops:
  0.6 22.0 %collective-permute-start.8 = (bf16[3,3,128,128]{3,2,1,0:T(8,128)(2,1)}, bf16[3,3,128,128]{3,2,1,0:T(8,128)(2,1)S(1)}, u32[]{:S(2)}, u32[]{:S(2)}) collective-permute-start(bf16[3,3,128,128]{3,2,1,0:T(8,128)(2,1)} %bitcast.39), channel_id=1, source_target_pairs={{0,9},{8,1},{2,11},{10,3},{4,13},{12,5},{6,15},{14,7},{16,25},{24,... | collective-permute-start | bytes 884744 | tf_op jit(solution)/shard_map/ppermute | solution.py:240
  6.7 1.0 %copy-start = (bf16[32,8,8,128]{3,2,1,0:T(8,128)(2,1)S(1)}, bf16[32,8,8,128]{3,2,1,0:T(8,128)(2,1)}, u32[]{:S(2)}) copy-start(bf16[32,8,8,128]{3,2,1,0:T(8,128)(2,1)} %cot_ref.5) | copy-start | bytes 1572868
  7.8 1.3 %copy-start.2 = (bf16[32,12,12,128]{3,0,2,1:T(8,128)(2,1)S(1)}, bf16[32,12,12,128]{3,0,2,1:T(8,128)(2,1)}, u32[]{:S(2)}) copy-start(bf16[32,12,12,128]{3,0,2,1:T(8,128)(2,1)} %param.6) | copy-start | bytes 3538948
  9.0 0.7 copy-start.3
  10.5 5.5 %copy-start.6 = (bf16[1,3,3,128,128]{4,3,2,1,0:T(8,128)(2,1)S(1)}, bf16[1,3,3,128,128]{4,3,2,1,0:T(8,128)(2,1)}, u32[]{:S(2)}) copy-start(bf16[1,3,3,128,128]{4,3,2,1,0:T(8,128)(2,1)} %param.9) | copy-start | bytes 884740
  10.5 12.4 %copy-start.5 = (bf16[1,3,3,128,128]{4,3,2,1,0:T(8,128)(2,1)S(1)}, bf16[1,3,3,128,128]{4,3,2,1,0:T(8,128)(2,1)}, u32[]{:S(2)}) copy-start(bf16[1,3,3,128,128]{4,3,2,1,0:T(8,128)(2,1)} %param.10) | copy-start | bytes 884740
  10.5 3.2 %collective-permute-start = (bf16[416,128]{1,0:T(8,128)(2,1)S(1)}, bf16[416,128]{1,0:T(8,128)(2,1)S(1)}, u32[]{:S(2)}, u32[]{:S(2)}) collective-permute-start(bf16[416,128]{1,0:T(8,128)(2,1)S(1)} %get-tuple-element.55), channel_id=1, source_target_pairs={{0,1},{1,0},{2,3},{3,2},{4,5},{5,4},{6,7},{7,6},{8,9},{9,8},{10,11... | collective-permute-start | bytes 319496 | tf_op jit(solution)/shard_map/ppermute | solution.py:254
  10.6 5.4 %collective-permute-start.1 = (bf16[416,128]{1,0:T(8,128)(2,1)S(1)}, bf16[416,128]{1,0:T(8,128)(2,1)S(1)}, u32[]{:S(2)}, u32[]{:S(2)}) collective-permute-start(bf16[416,128]{1,0:T(8,128)(2,1)S(1)} %get-tuple-element.56), channel_id=1, source_target_pairs={{0,2},{1,3},{2,0},{3,1},{4,6},{5,7},{6,4},{7,5},{8,10},{9,11},{10,... | collective-permute-start | bytes 319496 | tf_op jit(solution)/shard_map/ppermute | solution.py:254
  12.9 5.2 %collective-permute-start.16 = (bf16[416,128]{1,0:T(8,128)(2,1)S(1)}, bf16[416,128]{1,0:T(8,128)(2,1)S(1)}, u32[]{:S(2)}, u32[]{:S(2)}) collective-permute-start(bf16[416,128]{1,0:T(8,128)(2,1)S(1)} %get-tuple-element.71), channel_id=1, source_target_pairs={{0,1},{1,0},{2,3},{3,2},{4,5},{5,4},{6,7},{7,6},{8,9},{9,8},{10,11... | collective-permute-start | bytes 319496 | tf_op jit(solution)/shard_map/ppermute | solution.py:254
  13.2 6.6 %collective-permute-start.17 = (bf16[416,128]{1,0:T(8,128)(2,1)S(1)}, bf16[416,128]{1,0:T(8,128)(2,1)S(1)}, u32[]{:S(2)}, u32[]{:S(2)}) collective-permute-start(bf16[416,128]{1,0:T(8,128)(2,1)S(1)} %get-tuple-element.72), channel_id=1, source_target_pairs={{0,2},{1,3},{2,0},{3,1},{4,6},{5,7},{6,4},{7,5},{8,10},{9,11},{10,... | collective-permute-start | bytes 319496 | tf_op jit(solution)/shard_map/ppermute | solution.py:254
  13.7 6.4 %collective-permute-start.18 = (bf16[416,128]{1,0:T(8,128)(2,1)S(1)}, bf16[416,128]{1,0:T(8,128)(2,1)S(1)}, u32[]{:S(2)}, u32[]{:S(2)}) collective-permute-start(bf16[416,128]{1,0:T(8,128)(2,1)S(1)} %get-tuple-element.73), channel_id=1, source_target_pairs={{0,3},{1,2},{2,1},{3,0},{4,7},{5,6},{6,5},{7,4},{8,11},{9,10},{10,... | collective-permute-start | bytes 319496 | tf_op jit(solution)/shard_map/ppermute | solution.py:254
  16.0 17.9 %collective-permute-start.7 = (bf16[3,3,128,128]{3,2,1,0:T(8,128)(2,1)S(1)}, bf16[3,3,128,128]{3,2,1,0:T(8,128)(2,1)}, u32[]{:S(2)}, u32[]{:S(2)}) collective-permute-start(bf16[3,3,128,128]{3,2,1,0:T(8,128)(2,1)S(1)} %bitcast.40), channel_id=1, source_target_pairs={{0,9},{8,1},{2,11},{10,3},{4,13},{12,5},{6,15},{14,7},{16,25},{24,... | collective-permute-start | bytes 884744 | tf_op jit(solution)/shard_map/ppermute | solution.py:240
  18.1 8.6 %collective-permute-start.19 = (bf16[416,128]{1,0:T(8,128)(2,1)S(1)}, bf16[416,128]{1,0:T(8,128)(2,1)S(1)}, u32[]{:S(2)}, u32[]{:S(2)}) collective-permute-start(bf16[416,128]{1,0:T(8,128)(2,1)S(1)} %get-tuple-element.74), channel_id=1, source_target_pairs={{0,4},{1,5},{2,6},{3,7},{4,0},{5,1},{6,2},{7,3},{8,12},{9,13},{10,... | collective-permute-start | bytes 319496 | tf_op jit(solution)/shard_map/ppermute | solution.py:254
  19.8 8.7 %collective-permute-start.20 = (bf16[416,128]{1,0:T(8,128)(2,1)S(1)}, bf16[416,128]{1,0:T(8,128)(2,1)S(1)}, u32[]{:S(2)}, u32[]{:S(2)}) collective-permute-start(bf16[416,128]{1,0:T(8,128)(2,1)S(1)} %get-tuple-element.75), channel_id=1, source_target_pairs={{0,5},{1,4},{2,7},{3,6},{4,1},{5,0},{6,3},{7,2},{8,13},{9,12},{10,... | collective-permute-start | bytes 319496 | tf_op jit(solution)/shard_map/ppermute | solution.py:254
  20.1 12.2 %collective-permute-start.21 = (bf16[416,128]{1,0:T(8,128)(2,1)S(1)}, bf16[416,128]{1,0:T(8,128)(2,1)S(1)}, u32[]{:S(2)}, u32[]{:S(2)}) collective-permute-start(bf16[416,128]{1,0:T(8,128)(2,1)S(1)} %get-tuple-element.76), channel_id=1, source_target_pairs={{0,6},{1,7},{2,4},{3,5},{4,2},{5,3},{6,0},{7,1},{8,14},{9,15},{10,... | collective-permute-start | bytes 319496 | tf_op jit(solution)/shard_map/ppermute | solution.py:254
  22.6 10.3 %collective-permute-start.22 = (bf16[416,128]{1,0:T(8,128)(2,1)S(1)}, bf16[416,128]{1,0:T(8,128)(2,1)S(1)}, u32[]{:S(2)}, u32[]{:S(2)}) collective-permute-start(bf16[416,128]{1,0:T(8,128)(2,1)S(1)} %get-tuple-element.77), channel_id=1, source_target_pairs={{0,7},{1,6},{2,5},{3,4},{4,3},{5,2},{6,1},{7,0},{8,15},{9,14},{10,... | collective-permute-start | bytes 319496 | tf_op jit(solution)/shard_map/ppermute | solution.py:254
  26.7 15.4 %collective-permute-start.2 = (bf16[416,128]{1,0:T(8,128)(2,1)S(1)}, bf16[416,128]{1,0:T(8,128)(2,1)S(1)}, u32[]{:S(2)}, u32[]{:S(2)}) collective-permute-start(bf16[416,128]{1,0:T(8,128)(2,1)S(1)} %get-tuple-element.57), channel_id=1, source_target_pairs={{0,3},{1,2},{2,1},{3,0},{4,7},{5,6},{6,5},{7,4},{8,11},{9,10},{10,... | collective-permute-start | bytes 319496 | tf_op jit(solution)/shard_map/ppermute | solution.py:254
  28.5 14.2 %collective-permute-start.3 = (bf16[416,128]{1,0:T(8,128)(2,1)S(1)}, bf16[416,128]{1,0:T(8,128)(2,1)S(1)}, u32[]{:S(2)}, u32[]{:S(2)}) collective-permute-start(bf16[416,128]{1,0:T(8,128)(2,1)S(1)} %get-tuple-element.58), channel_id=1, source_target_pairs={{0,4},{1,5},{2,6},{3,7},{4,0},{5,1},{6,2},{7,3},{8,12},{9,13},{10,... | collective-permute-start | bytes 319496 | tf_op jit(solution)/shard_map/ppermute | solution.py:254
  32.3 10.7 %collective-permute-start.4 = (bf16[416,128]{1,0:T(8,128)(2,1)S(1)}, bf16[416,128]{1,0:T(8,128)(2,1)S(1)}, u32[]{:S(2)}, u32[]{:S(2)}) collective-permute-start(bf16[416,128]{1,0:T(8,128)(2,1)S(1)} %get-tuple-element.59), channel_id=1, source_target_pairs={{0,5},{1,4},{2,7},{3,6},{4,1},{5,0},{6,3},{7,2},{8,13},{9,12},{10,... | collective-permute-start | bytes 319496 | tf_op jit(solution)/shard_map/ppermute | solution.py:254
  32.9 11.2 %collective-permute-start.5 = (bf16[416,128]{1,0:T(8,128)(2,1)S(1)}, bf16[416,128]{1,0:T(8,128)(2,1)S(1)}, u32[]{:S(2)}, u32[]{:S(2)}) collective-permute-start(bf16[416,128]{1,0:T(8,128)(2,1)S(1)} %get-tuple-element.60), channel_id=1, source_target_pairs={{0,6},{1,7},{2,4},{3,5},{4,2},{5,3},{6,0},{7,1},{8,14},{9,15},{10,... | collective-permute-start | bytes 319496 | tf_op jit(solution)/shard_map/ppermute | solution.py:254
  33.8 10.8 %collective-permute-start.6 = (bf16[416,128]{1,0:T(8,128)(2,1)S(1)}, bf16[416,128]{1,0:T(8,128)(2,1)S(1)}, u32[]{:S(2)}, u32[]{:S(2)}) collective-permute-start(bf16[416,128]{1,0:T(8,128)(2,1)S(1)} %get-tuple-element.61), channel_id=1, source_target_pairs={{0,7},{1,6},{2,5},{3,4},{4,3},{5,2},{6,1},{7,0},{8,15},{9,14},{10,... | collective-permute-start | bytes 319496 | tf_op jit(solution)/shard_map/ppermute | solution.py:254
  42.0 13.3 %collective-permute-start.23 = (bf16[416,128]{1,0:T(8,128)(2,1)S(1)}, bf16[416,128]{1,0:T(8,128)(2,1)S(1)}, u32[]{:S(2)}, u32[]{:S(2)}) collective-permute-start(bf16[416,128]{1,0:T(8,128)(2,1)S(1)} %get-tuple-element.79), channel_id=1, source_target_pairs={{0,1},{1,0},{2,3},{3,2},{4,5},{5,4},{6,7},{7,6},{8,9},{9,8},{10,11... | collective-permute-start | bytes 319496 | tf_op jit(solution)/shard_map/ppermute | solution.py:254
  42.7 14.0 %collective-permute-start.24 = (bf16[416,128]{1,0:T(8,128)(2,1)S(1)}, bf16[416,128]{1,0:T(8,128)(2,1)S(1)}, u32[]{:S(2)}, u32[]{:S(2)}) collective-permute-start(bf16[416,128]{1,0:T(8,128)(2,1)S(1)} %get-tuple-element.80), channel_id=1, source_target_pairs={{0,2},{1,3},{2,0},{3,1},{4,6},{5,7},{6,4},{7,5},{8,10},{9,11},{10,... | collective-permute-start | bytes 319496 | tf_op jit(solution)/shard_map/ppermute | solution.py:254
  43.0 17.7 %collective-permute-start.25 = (bf16[416,128]{1,0:T(8,128)(2,1)S(1)}, bf16[416,128]{1,0:T(8,128)(2,1)S(1)}, u32[]{:S(2)}, u32[]{:S(2)}) collective-permute-start(bf16[416,128]{1,0:T(8,128)(2,1)S(1)} %get-tuple-element.81), channel_id=1, source_target_pairs={{0,3},{1,2},{2,1},{3,0},{4,7},{5,6},{6,5},{7,4},{8,11},{9,10},{10,... | collective-permute-start | bytes 319496 | tf_op jit(solution)/shard_map/ppermute | solution.py:254
  44.1 18.2 %collective-permute-start.26 = (bf16[416,128]{1,0:T(8,128)(2,1)S(1)}, bf16[416,128]{1,0:T(8,128)(2,1)S(1)}, u32[]{:S(2)}, u32[]{:S(2)}) collective-permute-start(bf16[416,128]{1,0:T(8,128)(2,1)S(1)} %get-tuple-element.82), channel_id=1, source_target_pairs={{0,4},{1,5},{2,6},{3,7},{4,0},{5,1},{6,2},{7,3},{8,12},{9,13},{10,... | collective-permute-start | bytes 319496 | tf_op jit(solution)/shard_map/ppermute | solution.py:254
  44.6 17.8 %collective-permute-start.27 = (bf16[416,128]{1,0:T(8,128)(2,1)S(1)}, bf16[416,128]{1,0:T(8,128)(2,1)S(1)}, u32[]{:S(2)}, u32[]{:S(2)}) collective-permute-start(bf16[416,128]{1,0:T(8,128)(2,1)S(1)} %get-tuple-element.83), channel_id=1, source_target_pairs={{0,5},{1,4},{2,7},{3,6},{4,1},{5,0},{6,3},{7,2},{8,13},{9,12},{10,... | collective-permute-start | bytes 319496 | tf_op jit(solution)/shard_map/ppermute | solution.py:254
  53.4 40.2 %copy-start.1 = (bf16[32,8,8,128]{3,2,1,0:T(8,128)(2,1)S(1)}, bf16[32,8,8,128]{3,2,1,0:T(8,128)(2,1)}, u32[]{:S(2)}) copy-start(bf16[32,8,8,128]{3,2,1,0:T(8,128)(2,1)} %cot_ref.5) | copy-start | bytes 1572868
  53.4 40.2 %copy-start.4 = (f32[32]{0:T(128)S(1)}, f32[32]{0:T(128)}, u32[]{:S(2)}) copy-start(f32[32]{0:T(128)} %param.8) | copy-start | bytes 388
  55.4 25.3 %collective-permute-start.34 = (bf16[9,128,128]{2,1,0:T(8,128)(2,1)S(1)}, bf16[9,128,128]{2,1,0:T(8,128)(2,1)S(1)}, u32[]{:S(2)}, u32[]{:S(2)}) collective-permute-start(bf16[9,128,128]{2,1,0:T(8,128)(2,1)S(1)} %get-tuple-element.101), channel_id=1, source_target_pairs={{9,0},{1,8},{11,2},{3,10},{13,4},{5,12},{15,6},{7,14},{25,16},{17,... | collective-permute-start | bytes 884744 | tf_op jit(solution)/shard_map/ppermute | solution.py:317
  56.7 39.4 %collective-permute-start.33 = (f32[9,128,128]{2,1,0:T(8,128)S(1)}, f32[9,128,128]{2,1,0:T(8,128)S(1)}, u32[]{:S(2)}, u32[]{:S(2)}) collective-permute-start(f32[9,128,128]{2,1,0:T(8,128)S(1)} %get-tuple-element.100), channel_id=1, source_target_pairs={{0,1},{2,3},{4,5},{6,7},{8,9},{10,11},{12,13},{14,15},{16,17},{18,... | collective-permute-start | bytes 1769480 | tf_op jit(solution)/shard_map/ppermute | solution.py:318
  60.7 8.8 %collective-permute-start.28 = (bf16[416,128]{1,0:T(8,128)(2,1)S(1)}, bf16[416,128]{1,0:T(8,128)(2,1)S(1)}, u32[]{:S(2)}, u32[]{:S(2)}) collective-permute-start(bf16[416,128]{1,0:T(8,128)(2,1)S(1)} %get-tuple-element.84), channel_id=1, source_target_pairs={{0,6},{1,7},{2,4},{3,5},{4,2},{5,3},{6,0},{7,1},{8,14},{9,15},{10,... | collective-permute-start | bytes 319496 | tf_op jit(solution)/shard_map/ppermute | solution.py:254
  62.3 7.4 %collective-permute-start.29 = (bf16[416,128]{1,0:T(8,128)(2,1)S(1)}, bf16[416,128]{1,0:T(8,128)(2,1)S(1)}, u32[]{:S(2)}, u32[]{:S(2)}) collective-permute-start(bf16[416,128]{1,0:T(8,128)(2,1)S(1)} %get-tuple-element.85), channel_id=1, source_target_pairs={{0,7},{1,6},{2,5},{3,4},{4,3},{5,2},{6,1},{7,0},{8,15},{9,14},{10,... | collective-permute-start | bytes 319496 | tf_op jit(solution)/shard_map/ppermute | solution.py:254
  62.4 8.8 %collective-permute-start.10 = (bf16[416,128]{1,0:T(8,128)(2,1)S(1)}, bf16[416,128]{1,0:T(8,128)(2,1)S(1)}, u32[]{:S(2)}, u32[]{:S(2)}) collective-permute-start(bf16[416,128]{1,0:T(8,128)(2,1)S(1)} %get-tuple-element.64), channel_id=1, source_target_pairs={{0,2},{1,3},{2,0},{3,1},{4,6},{5,7},{6,4},{7,5},{8,10},{9,11},{10,... | collective-permute-start | bytes 319496 | tf_op jit(solution)/shard_map/ppermute | solution.py:254
  69.5 4.9 %collective-permute-start.11 = (bf16[416,128]{1,0:T(8,128)(2,1)S(1)}, bf16[416,128]{1,0:T(8,128)(2,1)S(1)}, u32[]{:S(2)}, u32[]{:S(2)}) collective-permute-start(bf16[416,128]{1,0:T(8,128)(2,1)S(1)} %get-tuple-element.65), channel_id=1, source_target_pairs={{0,3},{1,2},{2,1},{3,0},{4,7},{5,6},{6,5},{7,4},{8,11},{9,10},{10,... | collective-permute-start | bytes 319496 | tf_op jit(solution)/shard_map/ppermute | solution.py:254
  69.7 5.1 %collective-permute-start.12 = (bf16[416,128]{1,0:T(8,128)(2,1)S(1)}, bf16[416,128]{1,0:T(8,128)(2,1)S(1)}, u32[]{:S(2)}, u32[]{:S(2)}) collective-permute-start(bf16[416,128]{1,0:T(8,128)(2,1)S(1)} %get-tuple-element.66), channel_id=1, source_target_pairs={{0,4},{1,5},{2,6},{3,7},{4,0},{5,1},{6,2},{7,3},{8,12},{9,13},{10,... | collective-permute-start | bytes 319496 | tf_op jit(solution)/shard_map/ppermute | solution.py:254
  71.2 6.6 %collective-permute-start.13 = (bf16[416,128]{1,0:T(8,128)(2,1)S(1)}, bf16[416,128]{1,0:T(8,128)(2,1)S(1)}, u32[]{:S(2)}, u32[]{:S(2)}) collective-permute-start(bf16[416,128]{1,0:T(8,128)(2,1)S(1)} %get-tuple-element.67), channel_id=1, source_target_pairs={{0,5},{1,4},{2,7},{3,6},{4,1},{5,0},{6,3},{7,2},{8,13},{9,12},{10,... | collective-permute-start | bytes 319496 | tf_op jit(solution)/shard_map/ppermute | solution.py:254
  74.4 7.6 %collective-permute-start.14 = (bf16[416,128]{1,0:T(8,128)(2,1)S(1)}, bf16[416,128]{1,0:T(8,128)(2,1)S(1)}, u32[]{:S(2)}, u32[]{:S(2)}) collective-permute-start(bf16[416,128]{1,0:T(8,128)(2,1)S(1)} %get-tuple-element.68), channel_id=1, source_target_pairs={{0,6},{1,7},{2,4},{3,5},{4,2},{5,3},{6,0},{7,1},{8,14},{9,15},{10,... | collective-permute-start | bytes 319496 | tf_op jit(solution)/shard_map/ppermute | solution.py:254
  74.8 16.5 %collective-permute-start.31 = (bf16[9,128,128]{2,1,0:T(8,128)(2,1)S(1)}, bf16[9,128,128]{2,1,0:T(8,128)(2,1)S(1)}, u32[]{:S(2)}, u32[]{:S(2)}) collective-permute-start(bf16[9,128,128]{2,1,0:T(8,128)(2,1)S(1)} %get-tuple-element.99), channel_id=1, source_target_pairs={{9,0},{1,8},{11,2},{3,10},{13,4},{5,12},{15,6},{7,14},{25,16},{17,... | collective-permute-start | bytes 884744 | tf_op jit(solution)/shard_map/ppermute | solution.py:317
  77.8 19.2 %collective-permute-start.30 = (f32[9,128,128]{2,1,0:T(8,128)S(1)}, f32[9,128,128]{2,1,0:T(8,128)S(1)}, u32[]{:S(2)}, u32[]{:S(2)}) collective-permute-start(f32[9,128,128]{2,1,0:T(8,128)S(1)} %get-tuple-element.98), channel_id=1, source_target_pairs={{0,1},{2,3},{4,5},{6,7},{8,9},{10,11},{12,13},{14,15},{16,17},{18,... | collective-permute-start | bytes 1769480 | tf_op jit(solution)/shard_map/ppermute | solution.py:318
  80.7 15.4 %collective-permute-start.35 = (bf16[9,128,128]{2,1,0:T(8,128)(2,1)S(1)}, bf16[9,128,128]{2,1,0:T(8,128)(2,1)S(1)}, u32[]{:S(2)}, u32[]{:S(2)}) collective-permute-start(bf16[9,128,128]{2,1,0:T(8,128)(2,1)S(1)} %collective-permute-done.34), channel_id=1, source_target_pairs={{0,1},{2,3},{4,5},{6,7},{8,9},{10,11},{12,13},{14,15},{16,17},{18,... | collective-permute-start | bytes 884744 | tf_op jit(solution)/shard_map/ppermute | solution.py:320
  82.0 9.1 %collective-permute-start.15 = (bf16[416,128]{1,0:T(8,128)(2,1)S(1)}, bf16[416,128]{1,0:T(8,128)(2,1)S(1)}, u32[]{:S(2)}, u32[]{:S(2)}) collective-permute-start(bf16[416,128]{1,0:T(8,128)(2,1)S(1)} %get-tuple-element.69), channel_id=1, source_target_pairs={{0,7},{1,6},{2,5},{3,4},{4,3},{5,2},{6,1},{7,0},{8,15},{9,14},{10,... | collective-permute-start | bytes 319496 | tf_op jit(solution)/shard_map/ppermute | solution.py:254
  91.2 2.4 %collective-permute-start.9 = (bf16[416,128]{1,0:T(8,128)(2,1)S(1)}, bf16[416,128]{1,0:T(8,128)(2,1)S(1)}, u32[]{:S(2)}, u32[]{:S(2)}) collective-permute-start(bf16[416,128]{1,0:T(8,128)(2,1)S(1)} %get-tuple-element.63), channel_id=1, source_target_pairs={{0,1},{1,0},{2,3},{3,2},{4,5},{5,4},{6,7},{7,6},{8,9},{9,8},{10,11... | collective-permute-start | bytes 319496 | tf_op jit(solution)/shard_map/ppermute | solution.py:254
  91.3 5.8 %collective-permute-start.32 = (bf16[9,128,128]{2,1,0:T(8,128)(2,1)S(1)}, bf16[9,128,128]{2,1,0:T(8,128)(2,1)S(1)}, u32[]{:S(2)}, u32[]{:S(2)}) collective-permute-start(bf16[9,128,128]{2,1,0:T(8,128)(2,1)S(1)} %collective-permute-done.31), channel_id=1, source_target_pairs={{0,1},{2,3},{4,5},{6,7},{8,9},{10,11},{12,13},{14,15},{16,17},{18,... | collective-permute-start | bytes 884744 | tf_op jit(solution)/shard_map/ppermute | solution.py:320

commit v3 on v2

--- a/solution.py
+++ b/solution.py
@@ -9,10 +9,9 @@
 from jax.sharding import PartitionSpec as P
 
 SWAP = [(0, 3), (2, 1)]
-SWAP_HOME = [(3, 0), (1, 2)]
+SWAP_HOME = [(1, 3), (3, 1)]
 TAPS = 3
 BLOCK = 8
-SLOTS = 2
 PARAMS = pltpu.CompilerParams(vmem_limit_bytes=40 * 1024 * 1024)
 
 
@@ -30,7 +29,7 @@
     return jnp.sum(jnp.where(eye, row, 0.0), axis=1, keepdims=True)
 
 
-def slot_matrix(key, chunk, peers, cells_first):
+def slot_matrix(key, slots, peers, cells_first):
     patches = key.shape[1]
     earlier = iota((patches, patches), 0) < iota((patches, patches), 1)
     same = onto_rows(key) == key
@@ -42,21 +41,21 @@
     hit = (spread_col % patches) == spread_row if cells_first else (spread_col // BLOCK) == spread_row
     spread = jnp.where(hit, 1.0, 0.0)
     code_wide = jnp.sum(onto_rows(code) * spread, axis=0, keepdims=True)
-    rows = peers * BLOCK * SLOTS
+    rows = peers * BLOCK * slots
     row = iota((rows, columns), 0)
     col = iota((rows, columns), 1)
-    row_code = (row // (BLOCK * SLOTS)) * 8 + (row % SLOTS + chunk * SLOTS)
-    row_cell = (row // SLOTS) % BLOCK
+    row_code = (row // (BLOCK * slots)) * 8 + row % slots
+    row_cell = (row // slots) % BLOCK
     col_cell = col // patches if cells_first else col % BLOCK
     match = (row_code.astype(jnp.float32) == code_wide) & (row_cell == col_cell)
     return jnp.where(match, 1.0, 0.0).astype(jnp.bfloat16)
 
 
-def pack_kernel(chunk, key_ref, gate_ref, tiles_ref, cot_ref, *out_refs):
+def pack_kernel(slots, key_ref, gate_ref, tiles_ref, cot_ref, *out_refs):
     peers = len(out_refs)
-    step = BLOCK * SLOTS
+    step = BLOCK * slots
     key = key_ref[...]
-    pick = slot_matrix(key, chunk, peers, True)
+    pick = slot_matrix(key, slots, peers, True)
     blocks = tiles_ref.shape[0]
 
     def put(at, values):
@@ -66,7 +65,7 @@
 
     for block in range(blocks):
         put(block * step, dot(pick, tiles_ref[block]))
-    pick = slot_matrix(key, chunk, peers, False)
+    pick = slot_matrix(key, slots, peers, False)
     gate = onto_rows(gate_ref[...])[:, :, None]
     patches, rows, cols, channels = cot_ref.shape
     for i in range(rows):
@@ -75,24 +74,20 @@
         put((blocks + i) * step, dot(pick, scaled))
 
 
-def unpack_kernel(peers, key_ref, gate_ref, cot_ref, *refs):
-    chunks = (len(refs) - 3) // peers
-    msgs, (out_ref, tiles_ref, gate_grad_ref) = refs[: chunks * peers], refs[chunks * peers :]
-    step = BLOCK * SLOTS
+def unpack_kernel(slots, key_ref, gate_ref, cot_ref, *refs):
+    msgs, (out_ref, tiles_ref, gate_grad_ref) = refs[:-3], refs[-3:]
+    peers = len(msgs)
+    step = BLOCK * slots
     key = key_ref[...]
-
-    def spread(cells_first):
-        picks = [slot_matrix(key, chunk, peers, cells_first) for chunk in range(chunks)]
-        return jnp.concatenate(picks, axis=0).T
 
     def gather(block):
         return jnp.concatenate([m[block * step : (block + 1) * step, :] for m in msgs], axis=0)
 
     blocks = tiles_ref.shape[0]
-    pick = spread(True)
+    pick = slot_matrix(key, slots, peers, True).T
     for block in range(blocks):
         tiles_ref[block] = dot(pick, gather(block)).astype(jnp.bfloat16)
-    pick = spread(False)
+    pick = slot_matrix(key, slots, peers, False).T
     gate = onto_rows(gate_ref[...])[:, :, None]
     patches, rows, cols, channels = cot_ref.shape
     total = jnp.zeros((patches, cols, channels), jnp.float32)
@@ -105,23 +100,23 @@
     gate_grad_ref[...] = jnp.sum(jnp.where(eye, sums, 0.0), axis=0, keepdims=True)
 
 
-def mix_matrix(peers, inverse):
-    size = peers * BLOCK * SLOTS
+def mix_matrix(peers, slots, inverse):
+    size = peers * BLOCK * slots
     mixed, apart = (1, 0) if inverse else (0, 1)
     a = iota((size, size), mixed)
     b = iota((size, size), apart)
-    cell_a, rest = a // (peers * SLOTS), a % (peers * SLOTS)
-    from_b = (rest // SLOTS) * (BLOCK * SLOTS) + cell_a * SLOTS + rest % SLOTS
+    cell_a, rest = a // (peers * slots), a % (peers * slots)
+    from_b = (rest // slots) * (BLOCK * slots) + cell_a * slots + rest % slots
     return jnp.where(from_b == b, 1.0, 0.0).astype(jnp.bfloat16)
 
 
-def expert_kernel(peers, side, *refs):
+def expert_kernel(peers, slots, side, *refs):
     msgs = refs[:peers]
     one_ref, two_ref, one_t_ref, two_t_ref = refs[peers : peers + 4]
-    backs = refs[peers + 4 : 2 * peers + 4]
-    x_ref, h_ref, g_ref, m_ref, slope_ref, t_ref = refs[2 * peers + 4 :]
-    step = BLOCK * SLOTS
-    wide = peers * SLOTS
+    backs = refs[-peers - 6 : -6]
+    x_ref, h_ref, g_ref, m_ref, slope_ref, t_ref = refs[-6:]
+    step = BLOCK * slots
+    wide = peers * slots
     mid, out = side - 2, side - 4
     blocks = side * side // BLOCK
     size = BLOCK * wide
@@ -133,7 +128,7 @@
         at = (row * cols + col) * wide
         return ref[at : at + count * wide, :]
 
-    mix = mix_matrix(peers, False)
+    mix = mix_matrix(peers, slots, False)
     for block in range(blocks):
         x_ref[block * size : (block + 1) * size, :] = dot(mix, gather(block)).astype(jnp.bfloat16)
     for i in range(mid):
@@ -146,7 +141,7 @@
         h_ref[rows, :] = (pre * sigma).astype(jnp.bfloat16)
         slope_ref[rows, :] = sigma * (1.0 + pre * (1.0 - sigma))
 
-    apart = mix_matrix(peers, True)
+    apart = mix_matrix(peers, slots, True)
 
     def put(block, values):
         values = dot(apart, values).astype(jnp.bfloat16)
@@ -188,12 +183,10 @@
         put(block, t_ref[block * size : (block + 1) * size, :])
 
 
-def sums_kernel(side, wide, last, *refs):
+def sums_kernel(side, wide, first, last, *refs):
     x_ref, h_ref, g_ref, m_ref = refs[:4]
-    refs = refs[4:]
-    before = None
-    if last:
-        before, refs = refs[:2], refs[2:]
+    before_ref = None if first else refs[4]
+    out_ref = refs[-1]
     mid, out = side - 2, side - 4
 
     def one(in_ref, cols, grad_ref, rows, k):
@@ -210,11 +203,11 @@
                 ],
                 axis=0,
             )
+            at = k * TAPS * TAPS + tap
             total = dot(grad_t, window)
-            if last:
-                total = (total + before[k][tap]).T
-                refs[2 + k][tap] = total.astype(jnp.bfloat16)
-            refs[k][tap] = total
+            if not first:
+                total = total + before_ref[at]
+            out_ref[at] = total.T.astype(jnp.bfloat16) if last else total
 
     one(h_ref, mid, g_ref, out, 1)
     one(x_ref, side, m_ref, mid, 0)
@@ -230,11 +223,13 @@
     peers = per_half * cores
     patches, side, _, channels = tiles.shape
     out_side = cotangent.shape[1]
-    capacity = max(2, (patches + peers - 1) // peers)
-    chunks = capacity // SLOTS
+    slots = max(2, (patches + peers - 1) // peers)
     blocks = side * side // BLOCK
-    message = (side * side + out_side * out_side) * SLOTS
-    wide = peers * SLOTS
+    message = (side * side + out_side * out_side) * slots
+    order = sorted(range(peers), key=lambda mask: (mask >= cores, -(mask // cores).bit_count(), mask % cores, mask))
+    chunks = (order[: peers // 2], order[peers // 2 :])
+    part = peers // 2
+    wide = part * slots
 
     other_one, other_two = (
         lax.ppermute(k[0], ("half", "replica"), SWAP) for k in (conv_first, conv_second)
@@ -247,22 +242,22 @@
     bf16 = functools.partial(jax.ShapeDtypeStruct, dtype=jnp.bfloat16)
     f32 = functools.partial(jax.ShapeDtypeStruct, dtype=jnp.float32)
 
-    def exchange(messages):
-        got = [messages[0]]
-        for mask in range(1, peers):
-            pairs = [(i, i ^ mask) for i in range(peers)]
-            got.append(lax.ppermute(messages[mask], ("owner", "replica"), pairs))
-        return got
-
-    def pack(chunk):
-        return pl.pallas_call(
-            functools.partial(pack_kernel, chunk),
-            out_shape=[bf16((message, channels))] * peers,
-            compiler_params=PARAMS,
-            name="pack",
-        )(key, gate_row, tiles_rows, cotangent)
-
-    arrived = [exchange(pack(chunk)) for chunk in range(chunks)]
+    def exchange(mask, message, after=None):
+        if mask == 0:
+            return message
+        if after is not None:
+            message, _ = lax.optimization_barrier((message, after))
+        return lax.ppermute(message, ("owner", "replica"), [(i, i ^ mask) for i in range(peers)])
+
+    packed = pl.pallas_call(
+        functools.partial(pack_kernel, slots),
+        out_shape=[bf16((message, channels))] * peers,
+        compiler_params=PARAMS,
+        name="pack",
+    )(key, gate_row, tiles_rows, cotangent)
+    arrived = [[exchange(mask, packed[mask]) for mask in chunks[0]]]
+    leading = [None, None] + arrived[0][2:]
+    arrived.append([exchange(mask, packed[mask], leading[i % len(leading)]) for i, mask in enumerate(chunks[1])])
 
     kernel_one = jnp.where(core == 0, conv_first[0], other_one)
     kernel_two = jnp.where(core == 0, conv_second[0], other_two)
@@ -274,6 +269,11 @@
         jnp.swapaxes(kernel_two, 2, 3).reshape(flat),
     )
     mid = side - 2
+
+    def cost(cells):
+        flops = int(cells * wide * TAPS * TAPS * channels * channels * 8)
+        return pl.CostEstimate(flops=flops, bytes_accessed=flops // 500, transcendentals=0)
+
     kept = [
         bf16((side * side * wide, channels)),
         bf16((mid * mid * wide, channels)),
@@ -281,50 +281,52 @@
         bf16((mid * (mid + 4) * wide, channels)),
     ]
 
-    def expert(messages):
+    def expert(messages, after):
+        specs = [pl.BlockSpec()] * (len(messages) + len(weights))
+        specs = specs + [pl.BlockSpec(memory_space=pl.ANY)] * len(after)
         result = pl.pallas_call(
-            functools.partial(expert_kernel, peers, side),
-            out_shape=[bf16((message, channels))] * peers + kept,
+            functools.partial(expert_kernel, part, slots, side),
+            in_specs=specs,
+            out_shape=[bf16((message, channels))] * part + kept,
             scratch_shapes=[
                 pltpu.VMEM((mid * mid * wide, channels), jnp.float32),
                 pltpu.VMEM((side * side * wide, channels), jnp.bfloat16),
             ],
             compiler_params=PARAMS,
+            cost_estimate=cost(2.0 * (2 * mid * mid + out_side * out_side + side * side)),
             name="expert",
-        )(*messages, *weights)
-        return result[:peers], result[peers:]
-
-    def sums(held, before):
-        last = before is not None or chunks == 1
-        shape = (TAPS * TAPS, channels, channels)
+        )(*messages, *weights, *after)
+        return result[:part], result[part:]
+
+    def sums(held, before, after, last):
+        specs = [pl.BlockSpec()] * (len(held) + len(before))
+        specs = specs + [pl.BlockSpec(memory_space=pl.ANY)] * len(after)
+        shape = (2 * TAPS * TAPS, channels, channels)
         return pl.pallas_call(
-            functools.partial(sums_kernel, side, wide, before is not None),
-            out_shape=[f32(shape)] * 2 + ([bf16(shape)] * 2 if before is not None else []),
+            functools.partial(sums_kernel, side, wide, not before, last),
+            in_specs=specs,
+            out_shape=bf16(shape) if last else f32(shape),
             compiler_params=PARAMS,
+            cost_estimate=cost(2.0 * (mid * mid + out_side * out_side)),
             name="sums",
-        )(*held, *(before or []))
-
-    backs, total = [], None
-    for messages in arrived:
-        back, held = expert(messages)
-        backs.append(exchange(back))
-        if total is None:
-            shape = (TAPS * TAPS, channels, channels)
-            total = [jnp.zeros(shape, jnp.float32)] * 2 if chunks == 1 else None
-        total = sums(held, total)
-
-    def combine(local, short):
-        away = lax.ppermute(short, ("half", "replica"), SWAP_HOME)
-        beside = lax.ppermute(local, "replica", [(0, 1)])
-        own = jnp.where(core == 0, local, beside)
-        passed = lax.ppermute(away, "replica", [(0, 1)])
-        total = own + jnp.where(core == 0, away, passed).astype(jnp.float32)
-        return total.reshape((1, TAPS, TAPS) + total.shape[1:])
-
-    first_grad = combine(total[0], total[2])
-    second_grad = combine(total[1], total[3])
+        )(*held, *before, *after)
+
+    backs, total = {}, []
+    for chunk, messages in zip(chunks, arrived):
+        back, held = expert(messages, total)
+        after = [backs[mask] for mask in backs if mask]
+        for mask, returned in zip(chunk, back):
+            backs[mask] = exchange(mask, returned)
+        total = [sums(held, total, after, chunk is chunks[-1])]
+
+    away = lax.ppermute(total[0], ("half", "replica"), SWAP_HOME)
+    away, _ = lax.optimization_barrier((away, [backs[mask] for mask in chunks[1]]))
+    away = jnp.where(core == 0, total[0], away)
+    beside = lax.ppermute(away, "replica", [(0, 1), (1, 0)])
+    grads = away.astype(jnp.float32) + beside.astype(jnp.float32)
+    first_grad, second_grad = grads.reshape((2, 1, TAPS, TAPS, channels, channels))
     output, tiles_out, gate_grad = pl.pallas_call(
-        functools.partial(unpack_kernel, peers),
+        functools.partial(unpack_kernel, slots),
         out_shape=[
             bf16(cotangent.shape),
             bf16(tiles_rows.shape),
@@ -332,7 +334,7 @@
         ],
         compiler_params=PARAMS,
         name="unpack",
-    )(key, gate_row, cotangent, *[m for back in backs for m in back])
+    )(key, gate_row, cotangent, *[backs[mask] for mask in range(peers)])
     tiles_grad = jnp.transpose(tiles_out.reshape(side, side, patches, channels), (2, 0, 1, 3))
     return (output, tiles_grad, first_grad, second_grad, gate_grad[0])
 

time: 98.4 us -> 80.5 us (0.82)
  starting transfers between devices: 44.9 us -> 30 us
  waiting for transfers between devices: 27.8 us -> 24.3 us
  other arithmetic: 2.64 us -> 0.97 us
  Pallas kernels: 18.3 us -> 19.6 us
  local copies, waits for them, and re-layouts: 3.43 us -> 4.52 us
    ppermute x34 -> x16, starting transfers between devices: 37.4 us -> 21.9 us  [the longest x14 20.1 us: exchange(): lax.ppermute(message, ('owner', 'replica'), [(i, i ^ mask) for i in range...]
    ppermute x34 -> x16, waiting for transfers between devices: 27.8 us -> 24.3 us  [the longest x14 24.3 us: exchange(): lax.ppermute(message, ('owner', 'replica'), [(i, i ^ mask) for i in range...]
    add x2 -> x1, other arithmetic: 1.89 us -> 0.14 us  [shards(): grads = away.astype(jnp.float32) + beside.astype(jnp.float32)]
    pallas_call x7 -> x6, Pallas kernels: 18.3 us -> 19.6 us  [the longest x2 11.5 us: expert(): pl.pallas_call(functools.partial(expert_kernel, part, slots, side), in_sp...]
    another operation x0 -> x1, local copies, waits for them, and re-layouts: none -> 1.11 us  [shards(): first_grad, second_grad = grads.reshape((2, 1, TAPS, TAPS, channels, chan...]
  transfers between devices with their start and end apart: 36 -> 18, of which waited for: 12 -> 7; matrix products, arithmetic and copies ran while one was open for 2% -> 1% of each run, Pallas kernels for 19% -> 22%
where the time goes in v3:
time: 80.5 us; the launch traced here: 80.2 us
  starting transfers between devices  30 us (37%)
  waiting for transfers between devices  24.3 us (30%)
  Pallas kernels  19.6 us (24%)
  local copies, waits for them, and re-layouts  4.52 us (6%)
  other arithmetic  0.97 us (1%)
    ppermute x14, waiting for transfers between devices, exchange(): lax.ppermute(message, ('owner', 'replica'), [(i, i ^ mask) for i in range...  24.3 us
    ppermute x14, starting transfers between devices, exchange(): lax.ppermute(message, ('owner', 'replica'), [(i, i ^ mask) for i in range...  20.1 us
    pallas_call x2, Pallas kernels, expert(): pl.pallas_call(functools.partial(expert_kernel, part, slots, side), in_sp...  11.5 us
    ppermute x2, starting transfers between devices, shards(): lax.ppermute(k[0], ('half', 'replica'), SWAP)  8.1 us
    pallas_call x2, Pallas kernels, sums(): pl.pallas_call(functools.partial(sums_kernel, side, wide, not before, las...  3.76 us
    unnamed x14, local copies, waits for them, and re-layouts  2.98 us
    pallas_call x1, Pallas kernels, shards(): pl.pallas_call(functools.partial(unpack_kernel, slots), out_shape=[bf16(c...  2.47 us
    pallas_call x1, Pallas kernels, shards(): pl.pallas_call(functools.partial(pack_kernel, slots), out_shape=[bf16((me...  1.87 us
  transfers between devices with their start and end apart: 18, of which 7 were waited for; matrix products, arithmetic and copies ran while one was open for 1% of the time, Pallas kernels for 22%

profile of v3, /device:TPU:0, one launch (start us, length us, event | category | flops | bytes accessed | tf_op | source)
XLA Modules:
  0.0 80.2 jit_solution(15701554704762060220)
XLA Ops:
  0.6 5.4 %collective-permute-start.4 = (bf16[3,3,128,128]{3,2,1,0:T(8,128)(2,1)}, bf16[3,3,128,128]{3,2,1,0:T(8,128)(2,1)S(1)}, u32[]{:S(2)}, u32[]{:S(2)}) collective-permute-start(bf16[3,3,128,128]{3,2,1,0:T(8,128)(2,1)} %bitcast.37), channel_id=1, source_target_pairs={{0,9},{8,1},{2,11},{10,3},{4,13},{12,5},{6,15},{14,7},{16,25},{24,... | collective-permute-start | bytes 884744 | tf_op jit(solution)/shard_map/ppermute | solution.py:235
  6.0 0.7 convert_bitcast_fusion.key_ref
  6.7 1.0 %copy-done = bf16[32,8,8,128]{3,2,1,0:T(8,128)(2,1)S(1)} copy-done((bf16[32,8,8,128]{3,2,1,0:T(8,128)(2,1)S(1)}, bf16[32,8,8,128]{3,2,1,0:T(8,128)(2,1)}, u32[]{:S(2)}) %copy-start) | copy-done | bytes 524312
  7.8 1.3 %copy-done.2 = bf16[32,12,12,128]{3,0,2,1:T(8,128)(2,1)S(1)} copy-done((bf16[32,12,12,128]{3,0,2,1:T(8,128)(2,1)S(1)}, bf16[32,12,12,128]{3,0,2,1:T(8,128)(2,1)}, u32[]{:S(2)}) %copy-start.2) | copy-done | bytes 1179672
  9.0 0.7 copy-done.3
  9.7 1.9 %pack.1 = (bf16[832,128]{1,0:T(8,128)(2,1)S(1)}, bf16[832,128]{1,0:T(8,128)(2,1)}, bf16[832,128]{1,0:T(8,128)(2,1)S(1)}, bf16[832,128]{1,0:T(8,128)(2,1)S(1)}, b...) custom-call(f32[1,32]{1,0:T(1,128)S(1)} %convert_bitcast_fusion.key_, ...), custom_call_target="tpu_custom_call" | custom-call | tf_op jit(solution)/shard_map/pack/pallas_call | solution.py:252
  11.6 2.5 %collective-permute-start.1 = (bf16[832,128]{1,0:T(8,128)(2,1)S(1)}, bf16[832,128]{1,0:T(8,128)(2,1)S(1)}, u32[]{:S(2)}, u32[]{:S(2)}) collective-permute-start(bf16[832,128]{1,0:T(8,128)(2,1)S(1)} %get-tuple-element.37), channel_id=1, source_target_pairs={{0,6},{1,7},{2,4},{3,5},{4,2},{5,3},{6,0},{7,1},{8,14},{9,15},{10,... | collective-permute-start | bytes 638984 | tf_op jit(solution)/shard_map/ppermute | solution.py:250
  14.1 0.0 collective-permute-start.2
  14.1 2.7 %collective-permute-start.3 = (bf16[3,3,128,128]{3,2,1,0:T(8,128)(2,1)S(1)}, bf16[3,3,128,128]{3,2,1,0:T(8,128)(2,1)}, u32[]{:S(2)}, u32[]{:S(2)}) collective-permute-start(bf16[3,3,128,128]{3,2,1,0:T(8,128)(2,1)S(1)} %bitcast.38), channel_id=1, source_target_pairs={{0,9},{8,1},{2,11},{10,3},{4,13},{12,5},{6,15},{14,7},{16,25},{24,... | collective-permute-start | bytes 884744 | tf_op jit(solution)/shard_map/ppermute | solution.py:235
  16.8 0.0 collective-permute-start
  16.8 2.8 %collective-permute-done.1.refs_2_ = bf16[832,128]{1,0:T(8,128)(2,1)S(1)} collective-permute-done((bf16[832,128]{1,0:T(8,128)(2,1)S(1)}, bf16[832,128]{1,0:T(8,128)(2,1)S(1)}, u32[]{:S(2)}, u32[]{:S(2)}) %collective-permute-start.1) | collective-permute-done | bytes 213024 | tf_op jit(solution)/shard_map/ppermute | solution.py:250
  19.6 1.9 %collective-permute-start.6 = (bf16[832,128]{1,0:T(8,128)(2,1)S(1)}, bf16[832,128]{1,0:T(8,128)(2,1)S(1)}, u32[]{:S(2)}, u32[]{:S(2)}) collective-permute-start(bf16[832,128]{1,0:T(8,128)(2,1)S(1)} %get-tuple-element.41), channel_id=1, source_target_pairs={{0,2},{1,3},{2,0},{3,1},{4,6},{5,7},{6,4},{7,5},{8,10},{9,11},{10,... | collective-permute-start | bytes 638984 | tf_op jit(solution)/shard_map/ppermute | solution.py:250
  21.5 3.2 %collective-permute-done.2.refs_3_ = bf16[832,128]{1,0:T(8,128)(2,1)S(1)} collective-permute-done((bf16[832,128]{1,0:T(8,128)(2,1)S(1)}, bf16[832,128]{1,0:T(8,128)(2,1)S(1)}, u32[]{:S(2)}, u32[]{:S(2)}) %collective-permute-start.2) | collective-permute-done | bytes 213024 | tf_op jit(solution)/shard_map/ppermute | solution.py:250
  24.6 1.0 %collective-permute-start.7 = (bf16[832,128]{1,0:T(8,128)(2,1)S(1)}, bf16[832,128]{1,0:T(8,128)(2,1)S(1)}, u32[]{:S(2)}, u32[]{:S(2)}) collective-permute-start(bf16[832,128]{1,0:T(8,128)(2,1)S(1)} %get-tuple-element.42), channel_id=1, source_target_pairs={{0,4},{1,5},{2,6},{3,7},{4,0},{5,1},{6,2},{7,3},{8,12},{9,13},{10,... | collective-permute-start | bytes 638984 | tf_op jit(solution)/shard_map/ppermute | solution.py:250
  25.6 0.0 collective-permute-done.4
  25.6 1.4 %collective-permute-start.8 = (bf16[832,128]{1,0:T(8,128)(2,1)S(1)}, bf16[832,128]{1,0:T(8,128)(2,1)S(1)}, u32[]{:S(2)}, u32[]{:S(2)}) collective-permute-start(bf16[832,128]{1,0:T(8,128)(2,1)S(1)} %get-tuple-element.44), channel_id=1, source_target_pairs={{0,3},{1,2},{2,1},{3,0},{4,7},{5,6},{6,5},{7,4},{8,11},{9,10},{10,... | collective-permute-start | bytes 638984 | tf_op jit(solution)/shard_map/ppermute | solution.py:250
  27.1 0.2 copy.12
  27.3 0.0 collective-permute-done.3
  27.3 0.9 %collective-permute-start.9 = (bf16[832,128]{1,0:T(8,128)(2,1)S(1)}, bf16[832,128]{1,0:T(8,128)(2,1)S(1)}, u32[]{:S(2)}, u32[]{:S(2)}) collective-permute-start(bf16[832,128]{1,0:T(8,128)(2,1)S(1)} %get-tuple-element.46), channel_id=1, source_target_pairs={{0,5},{1,4},{2,7},{3,6},{4,1},{5,0},{6,3},{7,2},{8,13},{9,12},{10,... | collective-permute-start | bytes 638984 | tf_op jit(solution)/shard_map/ppermute | solution.py:250
  28.2 0.2 copy.11
  28.4 0.0 collective-permute-done.refs_1_
  28.4 6.1 %expert.2 = (bf16[832,128]{1,0:T(8,128)(2,1)S(1)}, bf16[832,128]{1,0:T(8,128)(2,1)S(1)}, bf16[832,128]{1,0:T(8,128)(2,1)S(1)}, bf16[832,128]{1,0:T(8,128)(2,1)S(...) custom-call(bf16[832,128]{1,0:T(8,128)(2,1)S(1)} %get-tuple-element., ...), custom_call_target="tpu_custom_call" | custom-call | flops 15401484288 | bytes 30802968 | tf_op jit(solution)/shard_map/expert/pallas_call | solution.py:287
  34.6 2.1 %collective-permute-start.5 = (bf16[832,128]{1,0:T(8,128)(2,1)S(1)}, bf16[832,128]{1,0:T(8,128)(2,1)S(1)}, u32[]{:S(2)}, u32[]{:S(2)}) collective-permute-start(bf16[832,128]{1,0:T(8,128)(2,1)S(1)} %get-tuple-element.40), channel_id=1, source_target_pairs={{0,1},{1,0},{2,3},{3,2},{4,5},{5,4},{6,7},{7,6},{8,9},{9,8},{10,11... | collective-permute-start | bytes 638984 | tf_op jit(solution)/shard_map/ppermute | solution.py:250
  36.6 1.8 %sums.2.refs_8_.refs_4_ = f32[18,128,128]{2,1,0:T(8,128)S(1)} custom-call(bf16[2304,128]{1,0:T(8,128)(2,1)S(1)} %get-tuple-element.47.refs_0_, bf16[1600,128]{1,0:T(8,128)(2,1)S(1)} %get-tuple-element.48.refs_1_, bf16[1536,128]{1,0:T(8,128)(2,1)S(1)} %get-tuple-element.49.refs_2_, bf16[2240,128]{1,0:T(8,128)(2,1)S(1)} %get-tuple-element.50.refs_3_), custom_call_target="tpu_custom_call" | custom-call | flops 6190792704 | bytes 12381585 | tf_op jit(solution)/shard_map/sums/pallas_call | solution.py:305
  38.4 0.0 collective-permute-done.6.refs_0_
  38.5 0.1 collective-permute-start.14
  38.5 0.0 collective-permute-done.7.refs_1_
  38.5 2.3 %collective-permute-start.15 = (bf16[832,128]{1,0:T(8,128)(2,1)S(1)}, bf16[832,128]{1,0:T(8,128)(2,1)S(1)}, u32[]{:S(2)}, u32[]{:S(2)}) collective-permute-start(bf16[832,128]{1,0:T(8,128)(2,1)S(1)} %get-tuple-element.56), channel_id=1, source_target_pairs={{0,7},{1,6},{2,5},{3,4},{4,3},{5,2},{6,1},{7,0},{8,15},{9,14},{10,... | collective-permute-start | bytes 638984 | tf_op jit(solution)/shard_map/ppermute | solution.py:250
  40.8 5.4 %expert.3 = (bf16[832,128]{1,0:T(8,128)(2,1)S(1)}, bf16[832,128]{1,0:T(8,128)(2,1)S(1)}, bf16[832,128]{1,0:T(8,128)(2,1)S(1)}, bf16[832,128]{1,0:T(8,128)(2,1)S(...) custom-call(bf16[832,128]{1,0:T(8,128)(2,1)S(1)} %collective-permute, ...), custom_call_target="tpu_custom_call" | custom-call | flops 15401484288 | bytes 30802968 | tf_op jit(solution)/shard_map/expert/pallas_call | solution.py:287
  46.2 0.0 collective-permute-done.5.refs_1_.refs_5_
  46.2 1.3 %collective-permute-done.14.refs_6_ = bf16[832,128]{1,0:T(8,128)(2,1)S(1)} collective-permute-done((bf16[832,128]{1,0:T(8,128)(2,1)S(1)}, bf16[832,128]{1,0:T(8,128)(2,1)S(1)}, u32[]{:S(2)}, u32[]{:S(2)}) %collective-permute-start.14) | collective-permute-done | bytes 213024 | tf_op jit(solution)/shard_map/ppermute | solution.py:250
  47.5 2.7 %collective-permute-done.15.refs_7_ = bf16[832,128]{1,0:T(8,128)(2,1)S(1)} collective-permute-done((bf16[832,128]{1,0:T(8,128)(2,1)S(1)}, bf16[832,128]{1,0:T(8,128)(2,1)S(1)}, u32[]{:S(2)}, u32[]{:S(2)}) %collective-permute-start.15) | collective-permute-done | bytes 213024 | tf_op jit(solution)/shard_map/ppermute | solution.py:250
  50.2 1.9 %sums.3 = bf16[18,128,128]{2,1,0:T(8,128)(2,1)S(1)} custom-call(bf16[2304,128]{1,0:T(8,128)(2,1)S(1)} %get-tuple-element.59.refs_0_, bf16[1600,128]{1,0:T(8,128)(2,1)S(1)} %get-tuple-element.60.refs_1_, bf16[1536,128]{1,0:T(8,128)(2,1)S(1)} %get-tuple-element.61.refs_2_, bf16[2240,128]{1,0:T(8,128)(2,1)S(1)} %get-tuple-element.62.refs_3_, ...), custom_call_target="tpu_custom_call" | custom-call | flops 6190792704 | bytes 12381585 | tf_op jit(solution)/shard_map/sums/pallas_call | solution.py:305
  52.2 0.0 copy-start.1
  52.2 0.0 copy-start.4
  52.2 0.8 %collective-permute-start.16 = (bf16[18,128,128]{2,1,0:T(8,128)(2,1)S(1)}, bf16[18,128,128]{2,1,0:T(8,128)(2,1)S(1)}, u32[]{:S(2)}, u32[]{:S(2)}) collective-permute-start(bf16[18,128,128]{2,1,0:T(8,128)(2,1)S(1)} %sums.3), channel_id=1, source_target_pairs={{1,9},{9,1},{3,11},{11,3},{5,13},{13,5},{7,15},{15,7},{17,25},{25,... | collective-permute-start | bytes 1769480 | tf_op jit(solution)/shard_map/ppermute | solution.py:322
  53.0 0.1 collective-permute-start.10
  53.1 6.5 %collective-permute-start.11 = (bf16[832,128]{1,0:T(8,128)(2,1)S(1)}, bf16[832,128]{1,0:T(8,128)(2,1)S(1)}, u32[]{:S(2)}, u32[]{:S(2)}) collective-permute-start(bf16[832,128]{1,0:T(8,128)(2,1)S(1)} %get-tuple-element.52), channel_id=1, source_target_pairs={{0,3},{1,2},{2,1},{3,0},{4,7},{5,6},{6,5},{7,4},{8,11},{9,10},{10,... | collective-permute-start | bytes 638984 | tf_op jit(solution)/shard_map/ppermute | solution.py:250
  59.6 1.5 %collective-permute-start.12 = (bf16[832,128]{1,0:T(8,128)(2,1)S(1)}, bf16[832,128]{1,0:T(8,128)(2,1)S(1)}, u32[]{:S(2)}, u32[]{:S(2)}) collective-permute-start(bf16[832,128]{1,0:T(8,128)(2,1)S(1)} %get-tuple-element.53), channel_id=1, source_target_pairs={{0,4},{1,5},{2,6},{3,7},{4,0},{5,1},{6,2},{7,3},{8,12},{9,13},{10,... | collective-permute-start | bytes 638984 | tf_op jit(solution)/shard_map/ppermute | solution.py:250
  61.1 6.6 %collective-permute-done.11.refs_3_ = bf16[832,128]{1,0:T(8,128)(2,1)S(1)} collective-permute-done((bf16[832,128]{1,0:T(8,128)(2,1)S(1)}, bf16[832,128]{1,0:T(8,128)(2,1)S(1)}, u32[]{:S(2)}, u32[]{:S(2)}) %collective-permute-start.11) | collective-permute-done | bytes 213024 | tf_op jit(solution)/shard_map/ppermute | solution.py:250
  67.7 5.3 %collective-permute-done.12.refs_4_ = bf16[832,128]{1,0:T(8,128)(2,1)S(1)} collective-permute-done((bf16[832,128]{1,0:T(8,128)(2,1)S(1)}, bf16[832,128]{1,0:T(8,128)(2,1)S(1)}, u32[]{:S(2)}, u32[]{:S(2)}) %collective-permute-start.12) | collective-permute-done | bytes 213024 | tf_op jit(solution)/shard_map/ppermute | solution.py:250
  73.0 2.5 %collective-permute-done.13.refs_5_ = bf16[832,128]{1,0:T(8,128)(2,1)S(1)} collective-permute-done((bf16[832,128]{1,0:T(8,128)(2,1)S(1)}, bf16[832,128]{1,0:T(8,128)(2,1)S(1)}, u32[]{:S(2)}, u32[]{:S(2)}) %collective-permute-start.13) | collective-permute-done | bytes 213024 | tf_op jit(solution)/shard_map/ppermute | solution.py:250
  75.5 0.0 collective-permute-done.16
  75.5 0.1 broadcast_select_fusion
  75.5 0.9 %collective-permute-start.17 = (bf16[18,128,128]{2,1,0:T(8,128)(2,1)S(1)}, bf16[18,128,128]{2,1,0:T(8,128)(2,1)S(1)}, u32[]{:S(2)}, u32[]{:S(2)}) collective-permute-start(bf16[18,128,128]{2,1,0:T(8,128)(2,1)S(1)} %broadcast_select_fusion), channel_id=1, source_target_pairs={{0,1},{1,0},{2,3},{3,2},{4,5},{5,4},{6,7},{7,6},{8,9},{9,8},{10,11... | collective-permute-start | bytes 1769480 | tf_op jit(solution)/shard_map/ppermute | solution.py:325
  76.5 2.5 %unpack.1 = (bf16[32,8,8,128]{3,2,1,0:T(8,128)(2,1)}, bf16[18,256,128]{2,1,0:T(8,128)(2,1)}, f32[1,32]{1,0:T(1,128)}) custom-call(f32[1,32]{1,0:T(1,128)S(1)} %convert_bitcast_fusion.key_ref, f32[1,32]{1,0:T(1,128)S(1)} %bitcast.34, bf16[32,8,8,128]{3,2,1,0:T(8,128)(2,1)S(1)} %copy-done.1, bf16[832,128]{1,0:T(8,128)(2,1)S(1)} %get-tuple-element.39.refs_0_, ...), custom_call_target="tpu_custom_call" | custom-call | tf_op jit(solution)/shard_map/unpack/pallas_call | solution.py:328
  79.0 0.1 convert_add_fusion
  79.1 1.1 %fusion.3 = (f32[9,128,128]{2,1,0:T(8,128)}, f32[9,128,128]{2,1,0:T(8,128)}) fusion(f32[18,128,128]{2,1,0:T(8,128)S(1)} %convert_add_fusion), kind=kLoop, calls=%fused_computation.16 | loop fusion | bytes 2359296 | tf_op jit(solution)/shard_map/unstack | solution.py:327
  (16 shorter events, 0.1 us)
Async XLA Ops:
  0.6 25.0 %collective-permute-start.4 = (bf16[3,3,128,128]{3,2,1,0:T(8,128)(2,1)}, bf16[3,3,128,128]{3,2,1,0:T(8,128)(2,1)S(1)}, u32[]{:S(2)}, u32[]{:S(2)}) collective-permute-start(bf16[3,3,128,128]{3,2,1,0:T(8,128)(2,1)} %bitcast.37), channel_id=1, source_target_pairs={{0,9},{8,1},{2,11},{10,3},{4,13},{12,5},{6,15},{14,7},{16,25},{24,... | collective-permute-start | bytes 884744 | tf_op jit(solution)/shard_map/ppermute | solution.py:235
  6.7 1.0 %copy-start = (bf16[32,8,8,128]{3,2,1,0:T(8,128)(2,1)S(1)}, bf16[32,8,8,128]{3,2,1,0:T(8,128)(2,1)}, u32[]{:S(2)}) copy-start(bf16[32,8,8,128]{3,2,1,0:T(8,128)(2,1)} %cot_ref.3) | copy-start | bytes 1572868
  7.8 1.3 %copy-start.2 = (bf16[32,12,12,128]{3,0,2,1:T(8,128)(2,1)S(1)}, bf16[32,12,12,128]{3,0,2,1:T(8,128)(2,1)}, u32[]{:S(2)}) copy-start(bf16[32,12,12,128]{3,0,2,1:T(8,128)(2,1)} %param.6) | copy-start | bytes 3538948
  9.0 0.7 copy-start.3
  9.7 4.4 %copy-start.6 = (bf16[1,3,3,128,128]{4,3,2,1,0:T(8,128)(2,1)S(1)}, bf16[1,3,3,128,128]{4,3,2,1,0:T(8,128)(2,1)}, u32[]{:S(2)}) copy-start(bf16[1,3,3,128,128]{4,3,2,1,0:T(8,128)(2,1)} %param.9) | copy-start | bytes 884740
  9.7 17.3 %copy-start.5 = (bf16[1,3,3,128,128]{4,3,2,1,0:T(8,128)(2,1)S(1)}, bf16[1,3,3,128,128]{4,3,2,1,0:T(8,128)(2,1)}, u32[]{:S(2)}) copy-start(bf16[1,3,3,128,128]{4,3,2,1,0:T(8,128)(2,1)} %param.10) | copy-start | bytes 884740
  11.6 8.0 %collective-permute-start.1 = (bf16[832,128]{1,0:T(8,128)(2,1)S(1)}, bf16[832,128]{1,0:T(8,128)(2,1)S(1)}, u32[]{:S(2)}, u32[]{:S(2)}) collective-permute-start(bf16[832,128]{1,0:T(8,128)(2,1)S(1)} %get-tuple-element.37), channel_id=1, source_target_pairs={{0,6},{1,7},{2,4},{3,5},{4,2},{5,3},{6,0},{7,1},{8,14},{9,15},{10,... | collective-permute-start | bytes 638984 | tf_op jit(solution)/shard_map/ppermute | solution.py:250
  14.1 10.5 %collective-permute-start.2 = (bf16[832,128]{1,0:T(8,128)(2,1)S(1)}, bf16[832,128]{1,0:T(8,128)(2,1)S(1)}, u32[]{:S(2)}, u32[]{:S(2)}) collective-permute-start(bf16[832,128]{1,0:T(8,128)(2,1)S(1)} %get-tuple-element.38), channel_id=1, source_target_pairs={{0,7},{1,6},{2,5},{3,4},{4,3},{5,2},{6,1},{7,0},{8,15},{9,14},{10,... | collective-permute-start | bytes 638984 | tf_op jit(solution)/shard_map/ppermute | solution.py:250
  14.1 13.2 %collective-permute-start.3 = (bf16[3,3,128,128]{3,2,1,0:T(8,128)(2,1)S(1)}, bf16[3,3,128,128]{3,2,1,0:T(8,128)(2,1)}, u32[]{:S(2)}, u32[]{:S(2)}) collective-permute-start(bf16[3,3,128,128]{3,2,1,0:T(8,128)(2,1)S(1)} %bitcast.38), channel_id=1, source_target_pairs={{0,9},{8,1},{2,11},{10,3},{4,13},{12,5},{6,15},{14,7},{16,25},{24,... | collective-permute-start | bytes 884744 | tf_op jit(solution)/shard_map/ppermute | solution.py:235
  16.8 11.6 %collective-permute-start = (bf16[832,128]{1,0:T(8,128)(2,1)}, bf16[832,128]{1,0:T(8,128)(2,1)}, u32[]{:S(2)}, u32[]{:S(2)}) collective-permute-start(bf16[832,128]{1,0:T(8,128)(2,1)} %get-tuple-element.36), channel_id=1, source_target_pairs={{0,1},{1,0},{2,3},{3,2},{4,5},{5,4},{6,7},{7,6},{8,9},{9,8},{10,11... | collective-permute-start | bytes 638984 | tf_op jit(solution)/shard_map/ppermute | solution.py:250
  19.6 18.9 %collective-permute-start.6 = (bf16[832,128]{1,0:T(8,128)(2,1)S(1)}, bf16[832,128]{1,0:T(8,128)(2,1)S(1)}, u32[]{:S(2)}, u32[]{:S(2)}) collective-permute-start(bf16[832,128]{1,0:T(8,128)(2,1)S(1)} %get-tuple-element.41), channel_id=1, source_target_pairs={{0,2},{1,3},{2,0},{3,1},{4,6},{5,7},{6,4},{7,5},{8,10},{9,11},{10,... | collective-permute-start | bytes 638984 | tf_op jit(solution)/shard_map/ppermute | solution.py:250
  24.6 13.9 %collective-permute-start.7 = (bf16[832,128]{1,0:T(8,128)(2,1)S(1)}, bf16[832,128]{1,0:T(8,128)(2,1)S(1)}, u32[]{:S(2)}, u32[]{:S(2)}) collective-permute-start(bf16[832,128]{1,0:T(8,128)(2,1)S(1)} %get-tuple-element.42), channel_id=1, source_target_pairs={{0,4},{1,5},{2,6},{3,7},{4,0},{5,1},{6,2},{7,3},{8,12},{9,13},{10,... | collective-permute-start | bytes 638984 | tf_op jit(solution)/shard_map/ppermute | solution.py:250
  25.6 15.2 %collective-permute-start.8 = (bf16[832,128]{1,0:T(8,128)(2,1)S(1)}, bf16[832,128]{1,0:T(8,128)(2,1)S(1)}, u32[]{:S(2)}, u32[]{:S(2)}) collective-permute-start(bf16[832,128]{1,0:T(8,128)(2,1)S(1)} %get-tuple-element.44), channel_id=1, source_target_pairs={{0,3},{1,2},{2,1},{3,0},{4,7},{5,6},{6,5},{7,4},{8,11},{9,10},{10,... | collective-permute-start | bytes 638984 | tf_op jit(solution)/shard_map/ppermute | solution.py:250
  27.3 13.5 %collective-permute-start.9 = (bf16[832,128]{1,0:T(8,128)(2,1)S(1)}, bf16[832,128]{1,0:T(8,128)(2,1)S(1)}, u32[]{:S(2)}, u32[]{:S(2)}) collective-permute-start(bf16[832,128]{1,0:T(8,128)(2,1)S(1)} %get-tuple-element.46), channel_id=1, source_target_pairs={{0,5},{1,4},{2,7},{3,6},{4,1},{5,0},{6,3},{7,2},{8,13},{9,12},{10,... | collective-permute-start | bytes 638984 | tf_op jit(solution)/shard_map/ppermute | solution.py:250
  34.6 11.6 %collective-permute-start.5 = (bf16[832,128]{1,0:T(8,128)(2,1)S(1)}, bf16[832,128]{1,0:T(8,128)(2,1)S(1)}, u32[]{:S(2)}, u32[]{:S(2)}) collective-permute-start(bf16[832,128]{1,0:T(8,128)(2,1)S(1)} %get-tuple-element.40), channel_id=1, source_target_pairs={{0,1},{1,0},{2,3},{3,2},{4,5},{5,4},{6,7},{7,6},{8,9},{9,8},{10,11... | collective-permute-start | bytes 638984 | tf_op jit(solution)/shard_map/ppermute | solution.py:250
  38.5 9.1 %collective-permute-start.14 = (bf16[832,128]{1,0:T(8,128)(2,1)S(1)}, bf16[832,128]{1,0:T(8,128)(2,1)S(1)}, u32[]{:S(2)}, u32[]{:S(2)}) collective-permute-start(bf16[832,128]{1,0:T(8,128)(2,1)S(1)} %get-tuple-element.55), channel_id=1, source_target_pairs={{0,6},{1,7},{2,4},{3,5},{4,2},{5,3},{6,0},{7,1},{8,14},{9,15},{10,... | collective-permute-start | bytes 638984 | tf_op jit(solution)/shard_map/ppermute | solution.py:250
  38.5 11.7 %collective-permute-start.15 = (bf16[832,128]{1,0:T(8,128)(2,1)S(1)}, bf16[832,128]{1,0:T(8,128)(2,1)S(1)}, u32[]{:S(2)}, u32[]{:S(2)}) collective-permute-start(bf16[832,128]{1,0:T(8,128)(2,1)S(1)} %get-tuple-element.56), channel_id=1, source_target_pairs={{0,7},{1,6},{2,5},{3,4},{4,3},{5,2},{6,1},{7,0},{8,15},{9,14},{10,... | collective-permute-start | bytes 638984 | tf_op jit(solution)/shard_map/ppermute | solution.py:250
  52.2 24.3 %copy-start.1 = (bf16[32,8,8,128]{3,2,1,0:T(8,128)(2,1)S(1)}, bf16[32,8,8,128]{3,2,1,0:T(8,128)(2,1)}, u32[]{:S(2)}) copy-start(bf16[32,8,8,128]{3,2,1,0:T(8,128)(2,1)} %cot_ref.3) | copy-start | bytes 1572868
  52.2 24.3 %copy-start.4 = (f32[32]{0:T(128)S(1)}, f32[32]{0:T(128)}, u32[]{:S(2)}) copy-start(f32[32]{0:T(128)} %param.8) | copy-start | bytes 388
  52.2 23.3 %collective-permute-start.16 = (bf16[18,128,128]{2,1,0:T(8,128)(2,1)S(1)}, bf16[18,128,128]{2,1,0:T(8,128)(2,1)S(1)}, u32[]{:S(2)}, u32[]{:S(2)}) collective-permute-start(bf16[18,128,128]{2,1,0:T(8,128)(2,1)S(1)} %sums.3), channel_id=1, source_target_pairs={{1,9},{9,1},{3,11},{11,3},{5,13},{13,5},{7,15},{15,7},{17,25},{25,... | collective-permute-start | bytes 1769480 | tf_op jit(solution)/shard_map/ppermute | solution.py:322
  53.0 8.1 %collective-permute-start.10 = (bf16[832,128]{1,0:T(8,128)(2,1)S(1)}, bf16[832,128]{1,0:T(8,128)(2,1)S(1)}, u32[]{:S(2)}, u32[]{:S(2)}) collective-permute-start(bf16[832,128]{1,0:T(8,128)(2,1)S(1)} %get-tuple-element.51), channel_id=1, source_target_pairs={{0,2},{1,3},{2,0},{3,1},{4,6},{5,7},{6,4},{7,5},{8,10},{9,11},{10,... | collective-permute-start | bytes 638984 | tf_op jit(solution)/shard_map/ppermute | solution.py:250
  53.1 14.6 %collective-permute-start.11 = (bf16[832,128]{1,0:T(8,128)(2,1)S(1)}, bf16[832,128]{1,0:T(8,128)(2,1)S(1)}, u32[]{:S(2)}, u32[]{:S(2)}) collective-permute-start(bf16[832,128]{1,0:T(8,128)(2,1)S(1)} %get-tuple-element.52), channel_id=1, source_target_pairs={{0,3},{1,2},{2,1},{3,0},{4,7},{5,6},{6,5},{7,4},{8,11},{9,10},{10,... | collective-permute-start | bytes 638984 | tf_op jit(solution)/shard_map/ppermute | solution.py:250
  59.6 13.4 %collective-permute-start.12 = (bf16[832,128]{1,0:T(8,128)(2,1)S(1)}, bf16[832,128]{1,0:T(8,128)(2,1)S(1)}, u32[]{:S(2)}, u32[]{:S(2)}) collective-permute-start(bf16[832,128]{1,0:T(8,128)(2,1)S(1)} %get-tuple-element.53), channel_id=1, source_target_pairs={{0,4},{1,5},{2,6},{3,7},{4,0},{5,1},{6,2},{7,3},{8,12},{9,13},{10,... | collective-permute-start | bytes 638984 | tf_op jit(solution)/shard_map/ppermute | solution.py:250
  61.1 14.3 %collective-permute-start.13 = (bf16[832,128]{1,0:T(8,128)(2,1)S(1)}, bf16[832,128]{1,0:T(8,128)(2,1)S(1)}, u32[]{:S(2)}, u32[]{:S(2)}) collective-permute-start(bf16[832,128]{1,0:T(8,128)(2,1)S(1)} %get-tuple-element.54), channel_id=1, source_target_pairs={{0,5},{1,4},{2,7},{3,6},{4,1},{5,0},{6,3},{7,2},{8,13},{9,12},{10,... | collective-permute-start | bytes 638984 | tf_op jit(solution)/shard_map/ppermute | solution.py:250
  75.5 3.4 %collective-permute-start.17 = (bf16[18,128,128]{2,1,0:T(8,128)(2,1)S(1)}, bf16[18,128,128]{2,1,0:T(8,128)(2,1)S(1)}, u32[]{:S(2)}, u32[]{:S(2)}) collective-permute-start(bf16[18,128,128]{2,1,0:T(8,128)(2,1)S(1)} %broadcast_select_fusion), channel_id=1, source_target_pairs={{0,1},{1,0},{2,3},{3,2},{4,5},{5,4},{6,7},{7,6},{8,9},{9,8},{10,11... | collective-permute-start | bytes 1769480 | tf_op jit(solution)/shard_map/ppermute | solution.py:325

commit v4 on v3

--- a/solution.py
+++ b/solution.py
@@ -74,8 +74,9 @@
         put((blocks + i) * step, dot(pick, scaled))
 
 
-def unpack_kernel(slots, key_ref, gate_ref, cot_ref, *refs):
+def unpack_kernel(slots, queue, key_ref, gate_ref, cot_ref, *refs):
     msgs, (out_ref, tiles_ref, gate_grad_ref) = refs[:-3], refs[-3:]
+    msgs = [msgs[queue.index(peer)] for peer in range(len(msgs))]
     peers = len(msgs)
     step = BLOCK * slots
     key = key_ref[...]
@@ -110,11 +111,14 @@
     return jnp.where(from_b == b, 1.0, 0.0).astype(jnp.bfloat16)
 
 
-def expert_kernel(peers, slots, side, *refs):
+def expert_kernel(peers, slots, side, earlier, last, *refs):
     msgs = refs[:peers]
     one_ref, two_ref, one_t_ref, two_t_ref = refs[peers : peers + 4]
-    backs = refs[-peers - 6 : -6]
-    x_ref, h_ref, g_ref, m_ref, slope_ref, t_ref = refs[-6:]
+    held = [refs[peers + 4 + 4 * k : peers + 8 + 4 * k] for k in range(earlier)]
+    outs = refs[peers + 4 + 4 * earlier :]
+    backs = outs[:peers]
+    sums_ref = outs[peers] if last else None
+    x_ref, h_ref, g_ref, m_ref, slope_ref, t_ref = outs[-6:]
     step = BLOCK * slots
     wide = peers * slots
     mid, out = side - 2, side - 4
@@ -183,34 +187,33 @@
         put(block, t_ref[block * size : (block + 1) * size, :])
 
 
-def sums_kernel(side, wide, first, last, *refs):
-    x_ref, h_ref, g_ref, m_ref = refs[:4]
-    before_ref = None if first else refs[4]
-    out_ref = refs[-1]
-    mid, out = side - 2, side - 4
-
-    def one(in_ref, cols, grad_ref, rows, k):
-        grads = [
-            grad_ref[(i * (rows + 4) + 2) * wide : (i * (rows + 4) + 2 + rows) * wide, :] for i in range(rows)
-        ]
-        grad_t = jnp.concatenate(grads, axis=0).T
-        for tap in range(TAPS * TAPS):
-            a, b = divmod(tap, TAPS)
-            window = jnp.concatenate(
-                [
-                    in_ref[((i + a) * cols + b) * wide : ((i + a) * cols + b + rows) * wide, :]
-                    for i in range(rows)
-                ],
-                axis=0,
-            )
-            at = k * TAPS * TAPS + tap
-            total = dot(grad_t, window)
-            if not first:
-                total = total + before_ref[at]
-            out_ref[at] = total.T.astype(jnp.bfloat16) if last else total
-
-    one(h_ref, mid, g_ref, out, 1)
-    one(x_ref, side, m_ref, mid, 0)
+    if last:
+        held = held + [(x_ref, h_ref, g_ref, m_ref)]
+        kernel_sums([k[0] for k in held], side, [k[3] for k in held], mid, wide, sums_ref, 0)
+        kernel_sums([k[1] for k in held], mid, [k[2] for k in held], out, wide, sums_ref, 1)
+
+
+def kernel_sums(in_refs, cols, grad_refs, rows, wide, sums_ref, k):
+    taps = TAPS * TAPS
+
+    def window(ref, tap):
+        a, b = divmod(tap, TAPS)
+        starts = [((i + a) * cols + b) * wide for i in range(rows)]
+        return [ref[at : at + rows * wide, :] for at in starts]
+
+    grads = []
+    for ref in grad_refs:
+        starts = [(i * (rows + 4) + 2) * wide for i in range(rows)]
+        grads = grads + [ref[at : at + rows * wide, :] for at in starts]
+    grad_t = jnp.concatenate(grads, axis=0).T
+    for first in range(0, taps, 2):
+        pair = range(first, min(first + 2, taps))
+        windows = [jnp.concatenate([w for ref in in_refs for w in window(ref, tap)], axis=0) for tap in pair]
+        total = dot(grad_t, jnp.concatenate(windows, axis=1))
+        channels = windows[0].shape[1]
+        for j, tap in enumerate(pair):
+            part = total[:, j * channels : (j + 1) * channels]
+            sums_ref[k * taps + tap] = part.T.astype(jnp.bfloat16)
 
 
 def shards(tiles, route, gate, conv_first, conv_second, cotangent):
@@ -255,9 +258,12 @@
         compiler_params=PARAMS,
         name="pack",
     )(key, gate_row, tiles_rows, cotangent)
-    arrived = [[exchange(mask, packed[mask]) for mask in chunks[0]]]
-    leading = [None, None] + arrived[0][2:]
-    arrived.append([exchange(mask, packed[mask], leading[i % len(leading)]) for i, mask in enumerate(chunks[1])])
+    nearer = sorted(chunks[1], key=lambda mask: (mask % cores, -mask))
+    queue = [mask for mask in chunks[0] if mask >= cores] + order[1:cores] + nearer
+    got = {0: packed[0]}
+    for i, mask in enumerate(queue):
+        got[mask] = exchange(mask, packed[mask], got[queue[i - 4]] if i >= 4 else None)
+    arrived = [[got[mask] for mask in chunk] for chunk in chunks]
 
     kernel_one = jnp.where(core == 0, conv_first[0], other_one)
     kernel_two = jnp.where(core == 0, conv_second[0], other_two)
@@ -281,52 +287,45 @@
         bf16((mid * (mid + 4) * wide, channels)),
     ]
 
-    def expert(messages, after):
-        specs = [pl.BlockSpec()] * (len(messages) + len(weights))
-        specs = specs + [pl.BlockSpec(memory_space=pl.ANY)] * len(after)
+    def expert(messages, held, last):
+        sums = [bf16((2 * TAPS * TAPS, channels, channels))]
+        scratch = [
+            pltpu.VMEM((mid * mid * wide, channels), jnp.float32),
+            pltpu.VMEM((side * side * wide, channels), jnp.bfloat16),
+        ]
+        if last:
+            scratch = [pltpu.VMEM(k.shape, k.dtype) for k in kept] + scratch
         result = pl.pallas_call(
-            functools.partial(expert_kernel, part, slots, side),
-            in_specs=specs,
-            out_shape=[bf16((message, channels))] * part + kept,
-            scratch_shapes=[
-                pltpu.VMEM((mid * mid * wide, channels), jnp.float32),
-                pltpu.VMEM((side * side * wide, channels), jnp.bfloat16),
-            ],
+            functools.partial(expert_kernel, part, slots, side, len(held) // 4, last),
+            out_shape=[bf16((message, channels))] * part + (sums if last else kept),
+            scratch_shapes=scratch,
             compiler_params=PARAMS,
             cost_estimate=cost(2.0 * (2 * mid * mid + out_side * out_side + side * side)),
             name="expert",
-        )(*messages, *weights, *after)
-        return result[:part], result[part:]
-
-    def sums(held, before, after, last):
-        specs = [pl.BlockSpec()] * (len(held) + len(before))
-        specs = specs + [pl.BlockSpec(memory_space=pl.ANY)] * len(after)
-        shape = (2 * TAPS * TAPS, channels, channels)
-        return pl.pallas_call(
-            functools.partial(sums_kernel, side, wide, not before, last),
-            in_specs=specs,
-            out_shape=bf16(shape) if last else f32(shape),
-            compiler_params=PARAMS,
-            cost_estimate=cost(2.0 * (mid * mid + out_side * out_side)),
-            name="sums",
-        )(*held, *before, *after)
-
-    backs, total = {}, []
+        )(*messages, *weights, *held)
+        return result[:part], list(result[part:])
+
+    backs, held = {}, []
     for chunk, messages in zip(chunks, arrived):
-        back, held = expert(messages, total)
-        after = [backs[mask] for mask in backs if mask]
-        for mask, returned in zip(chunk, back):
-            backs[mask] = exchange(mask, returned)
-        total = [sums(held, total, after, chunk is chunks[-1])]
-
-    away = lax.ppermute(total[0], ("half", "replica"), SWAP_HOME)
+        last = chunk is chunks[-1]
+        back, rest = expert(messages, held, last)
+        returned = dict(zip(chunk, back))
+        if not last:
+            held = held + rest
+            before = [mask for mask in chunk if mask]
+            for mask in chunk:
+                backs[mask] = exchange(mask, returned[mask])
+    total, _ = lax.optimization_barrier((rest[0], [backs[mask] for mask in before]))
+    for mask in nearer:
+        backs[mask] = exchange(mask, returned[mask], [backs[m] for m in before])
+    away = lax.ppermute(total, ("half", "replica"), SWAP_HOME)
     away, _ = lax.optimization_barrier((away, [backs[mask] for mask in chunks[1]]))
-    away = jnp.where(core == 0, total[0], away)
+    away = jnp.where(core == 0, total, away)
     beside = lax.ppermute(away, "replica", [(0, 1), (1, 0)])
     grads = away.astype(jnp.float32) + beside.astype(jnp.float32)
     first_grad, second_grad = grads.reshape((2, 1, TAPS, TAPS, channels, channels))
     output, tiles_out, gate_grad = pl.pallas_call(
-        functools.partial(unpack_kernel, slots),
+        functools.partial(unpack_kernel, slots, [*chunks[0], *nearer]),
         out_shape=[
             bf16(cotangent.shape),
             bf16(tiles_rows.shape),
@@ -334,7 +333,7 @@
         ],
         compiler_params=PARAMS,
         name="unpack",
-    )(key, gate_row, cotangent, *[backs[mask] for mask in range(peers)])
+    )(key, gate_row, cotangent, *[backs[mask] for mask in [*chunks[0], *nearer]])
     tiles_grad = jnp.transpose(tiles_out.reshape(side, side, patches, channels), (2, 0, 1, 3))
     return (output, tiles_grad, first_grad, second_grad, gate_grad[0])
 

time: 80.5 us -> 72.1 us (0.90)
  waiting for transfers between devices: 24.3 us -> 17.4 us
  Pallas kernels: 19.6 us -> 17.3 us
    ppermute x14, waiting for transfers between devices: 24.3 us -> 17.4 us  [exchange(): lax.ppermute(message, ('owner', 'replica'), [(i, i ^ mask) for i in range...]
    ppermute x14, starting transfers between devices: 20.1 us -> 22.1 us  [exchange(): lax.ppermute(message, ('owner', 'replica'), [(i, i ^ mask) for i in range...]
    pallas_call x5 -> x3, Pallas kernels: 17.8 us -> 16.1 us  [the longest x2 13.6 us: expert(): pl.pallas_call(functools.partial(expert_kernel, part, slots, side, len(he...]
    ppermute x1, starting transfers between devices: 0.93 us -> 0.07 us  [shards(): beside = lax.ppermute(away, 'replica', [(0, 1), (1, 0)])]
  transfers between devices with their start and end apart: 18 -> 18, of which waited for: 7 -> 4; matrix products, arithmetic and copies ran while one was open for 1% -> 2% of each run, Pallas kernels for 22% -> 24%
where the time goes in v4:
time: 72.1 us; the launch traced here: 71.8 us
  starting transfers between devices  30.8 us (43%)
  waiting for transfers between devices  17.4 us (24%)
  Pallas kernels  17.3 us (24%)
  local copies, waits for them, and re-layouts  4.52 us (6%)
  other arithmetic  0.97 us (1%)
  between operations  0.81 us (1%)
    ppermute x14, starting transfers between devices, exchange(): lax.ppermute(message, ('owner', 'replica'), [(i, i ^ mask) for i in range...  22.1 us
    ppermute x14, waiting for transfers between devices, exchange(): lax.ppermute(message, ('owner', 'replica'), [(i, i ^ mask) for i in range...  17.4 us
    pallas_call x2, Pallas kernels, expert(): pl.pallas_call(functools.partial(expert_kernel, part, slots, side, len(he...  13.6 us
    ppermute x2, starting transfers between devices, shards(): lax.ppermute(k[0], ('half', 'replica'), SWAP)  7.96 us
    unnamed x14, local copies, waits for them, and re-layouts  2.98 us
    pallas_call x1, Pallas kernels, shards(): pl.pallas_call(functools.partial(unpack_kernel, slots, [*chunks[0], *near...  2.48 us
  transfers between devices with their start and end apart: 18, of which 4 were waited for; matrix products, arithmetic and copies ran while one was open for 2% of the time, Pallas kernels for 24%

profile of v4, /device:TPU:0, one launch (start us, length us, event | category | flops | bytes accessed | tf_op | source)
XLA Modules:
  0.0 71.8 jit_solution(9767014572899775172)
XLA Ops:
  0.6 5.4 %collective-permute-start.3 = (bf16[3,3,128,128]{3,2,1,0:T(8,128)(2,1)}, bf16[3,3,128,128]{3,2,1,0:T(8,128)(2,1)S(1)}, u32[]{:S(2)}, u32[]{:S(2)}) collective-permute-start(bf16[3,3,128,128]{3,2,1,0:T(8,128)(2,1)} %bitcast.37), channel_id=1, source_target_pairs={{0,9},{8,1},{2,11},{10,3},{4,13},{12,5},{6,15},{14,7},{16,25},{24,... | collective-permute-start | bytes 884744 | tf_op jit(solution)/shard_map/ppermute | solution.py:238
  6.0 0.7 convert_bitcast_fusion.key_ref
  6.7 1.0 %copy-done = bf16[32,8,8,128]{3,2,1,0:T(8,128)(2,1)S(1)} copy-done((bf16[32,8,8,128]{3,2,1,0:T(8,128)(2,1)S(1)}, bf16[32,8,8,128]{3,2,1,0:T(8,128)(2,1)}, u32[]{:S(2)}) %copy-start) | copy-done | bytes 524312
  7.8 1.3 %copy-done.2 = bf16[32,12,12,128]{3,0,2,1:T(8,128)(2,1)S(1)} copy-done((bf16[32,12,12,128]{3,0,2,1:T(8,128)(2,1)S(1)}, bf16[32,12,12,128]{3,0,2,1:T(8,128)(2,1)}, u32[]{:S(2)}) %copy-start.2) | copy-done | bytes 1179672
  9.0 0.7 copy-done.3
  9.7 1.2 %pack.1 = (bf16[832,128]{1,0:T(8,128)(2,1)S(1)}, bf16[832,128]{1,0:T(8,128)(2,1)S(1)}, bf16[832,128]{1,0:T(8,128)(2,1)S(1)}, bf16[832,128]{1,0:T(8,128)(2,1)S(1)...) custom-call(f32[1,32]{1,0:T(1,128)S(1)} %convert_bitcast_fusion.key_, ...), custom_call_target="tpu_custom_call" | custom-call | tf_op jit(solution)/shard_map/pack/pallas_call | solution.py:255
  10.9 2.6 %collective-permute-start.1 = (bf16[832,128]{1,0:T(8,128)(2,1)S(1)}, bf16[832,128]{1,0:T(8,128)(2,1)S(1)}, u32[]{:S(2)}, u32[]{:S(2)}) collective-permute-start(bf16[832,128]{1,0:T(8,128)(2,1)S(1)} %get-tuple-element.40), channel_id=1, source_target_pairs={{0,6},{1,7},{2,4},{3,5},{4,2},{5,3},{6,0},{7,1},{8,14},{9,15},{10,... | collective-permute-start | bytes 638984 | tf_op jit(solution)/shard_map/ppermute | solution.py:253
  13.5 0.0 collective-permute-start
  13.5 0.5 collective-permute-start.2
  14.0 2.6 %collective-permute-start.4 = (bf16[3,3,128,128]{3,2,1,0:T(8,128)(2,1)S(1)}, bf16[3,3,128,128]{3,2,1,0:T(8,128)(2,1)}, u32[]{:S(2)}, u32[]{:S(2)}) collective-permute-start(bf16[3,3,128,128]{3,2,1,0:T(8,128)(2,1)S(1)} %bitcast.38), channel_id=1, source_target_pairs={{0,9},{8,1},{2,11},{10,3},{4,13},{12,5},{6,15},{14,7},{16,25},{24,... | collective-permute-start | bytes 884744 | tf_op jit(solution)/shard_map/ppermute | solution.py:238
  16.6 2.6 %collective-permute-done.1.refs_2_ = bf16[832,128]{1,0:T(8,128)(2,1)S(1)} collective-permute-done((bf16[832,128]{1,0:T(8,128)(2,1)S(1)}, bf16[832,128]{1,0:T(8,128)(2,1)S(1)}, u32[]{:S(2)}, u32[]{:S(2)}) %collective-permute-start.1) | collective-permute-done | bytes 213024 | tf_op jit(solution)/shard_map/ppermute | solution.py:253
  19.2 1.6 %collective-permute-start.9 = (bf16[832,128]{1,0:T(8,128)(2,1)S(1)}, bf16[832,128]{1,0:T(8,128)(2,1)S(1)}, u32[]{:S(2)}, u32[]{:S(2)}) collective-permute-start(bf16[832,128]{1,0:T(8,128)(2,1)S(1)} %get-tuple-element.48), channel_id=1, source_target_pairs={{0,4},{1,5},{2,6},{3,7},{4,0},{5,1},{6,2},{7,3},{8,12},{9,13},{10,... | collective-permute-start | bytes 638984 | tf_op jit(solution)/shard_map/ppermute | solution.py:253
  20.8 0.0 collective-permute-done.refs_1_
  20.8 2.3 %collective-permute-start.8 = (bf16[832,128]{1,0:T(8,128)(2,1)S(1)}, bf16[832,128]{1,0:T(8,128)(2,1)S(1)}, u32[]{:S(2)}, u32[]{:S(2)}) collective-permute-start(bf16[832,128]{1,0:T(8,128)(2,1)S(1)} %get-tuple-element.47), channel_id=1, source_target_pairs={{0,2},{1,3},{2,0},{3,1},{4,6},{5,7},{6,4},{7,5},{8,10},{9,11},{10,... | collective-permute-start | bytes 638984 | tf_op jit(solution)/shard_map/ppermute | solution.py:253
  23.1 1.0 %collective-permute-done.2.refs_3_ = bf16[832,128]{1,0:T(8,128)(2,1)S(1)} collective-permute-done((bf16[832,128]{1,0:T(8,128)(2,1)S(1)}, bf16[832,128]{1,0:T(8,128)(2,1)S(1)}, u32[]{:S(2)}, u32[]{:S(2)}) %collective-permute-start.2) | collective-permute-done | bytes 213024 | tf_op jit(solution)/shard_map/ppermute | solution.py:253
  24.1 4.0 %collective-permute-start.10 = (bf16[832,128]{1,0:T(8,128)(2,1)S(1)}, bf16[832,128]{1,0:T(8,128)(2,1)S(1)}, u32[]{:S(2)}, u32[]{:S(2)}) collective-permute-start(bf16[832,128]{1,0:T(8,128)(2,1)S(1)} %get-tuple-element.50), channel_id=1, source_target_pairs={{0,3},{1,2},{2,1},{3,0},{4,7},{5,6},{6,5},{7,4},{8,11},{9,10},{10,... | collective-permute-start | bytes 638984 | tf_op jit(solution)/shard_map/ppermute | solution.py:253
  28.0 0.0 collective-permute-done.3
  28.0 0.0 collective-permute-start.11
  28.1 0.2 copy.11
  28.3 0.0 collective-permute-done.4
  28.4 0.2 copy.12
  28.6 5.2 %expert.2 = (bf16[832,128]{1,0:T(8,128)(2,1)S(1)}, bf16[832,128]{1,0:T(8,128)(2,1)S(1)}, bf16[832,128]{1,0:T(8,128)(2,1)S(1)}, bf16[832,128]{1,0:T(8,128)(2,1)S(...) custom-call(bf16[832,128]{1,0:T(8,128)(2,1)S(1)} %get-tuple-element., ...), custom_call_target="tpu_custom_call" | custom-call | flops 15401484288 | bytes 30802968 | tf_op jit(solution)/shard_map/expert/pallas_call | solution.py:298
  33.8 0.1 collective-permute-start.5
  33.9 0.0 collective-permute-done.9.refs_1_
  33.9 1.5 %collective-permute-start.6 = (bf16[832,128]{1,0:T(8,128)(2,1)S(1)}, bf16[832,128]{1,0:T(8,128)(2,1)S(1)}, u32[]{:S(2)}, u32[]{:S(2)}) collective-permute-start(bf16[832,128]{1,0:T(8,128)(2,1)S(1)} %get-tuple-element.44), channel_id=1, source_target_pairs={{0,6},{1,7},{2,4},{3,5},{4,2},{5,3},{6,0},{7,1},{8,14},{9,15},{10,... | collective-permute-start | bytes 638984 | tf_op jit(solution)/shard_map/ppermute | solution.py:253
  35.5 0.0 collective-permute-done.8.refs_0_
  35.5 1.2 %collective-permute-start.7 = (bf16[832,128]{1,0:T(8,128)(2,1)S(1)}, bf16[832,128]{1,0:T(8,128)(2,1)S(1)}, u32[]{:S(2)}, u32[]{:S(2)}) collective-permute-start(bf16[832,128]{1,0:T(8,128)(2,1)S(1)} %get-tuple-element.45), channel_id=1, source_target_pairs={{0,7},{1,6},{2,5},{3,4},{4,3},{5,2},{6,1},{7,0},{8,15},{9,14},{10,... | collective-permute-start | bytes 638984 | tf_op jit(solution)/shard_map/ppermute | solution.py:253
  36.7 0.0 collective-permute-done.10.refs_2_
  36.7 0.0 collective-permute-done.11.refs_3_
  36.7 8.3 %expert.3 = (bf16[832,128]{1,0:T(8,128)(2,1)S(1)}, bf16[832,128]{1,0:T(8,128)(2,1)S(1)}, bf16[832,128]{1,0:T(8,128)(2,1)S(1)}, bf16[832,128]{1,0:T(8,128)(2,1)S(1)}, bf16[18,128,128]{2,1,0:T(8,128)(2,1)S(1)}) custom-call(bf16[832,128]{1,0:T(8,128)(2,1)S(1)} %collective-permute-done.8.refs_0_, bf16[832,128]{1,0:T(8,128)(2,1)S(1)} %collective-permute-done.9.refs_1_, ...), custom_call_target="tpu_custom_call" | custom-call | flops 15401484288 | bytes 30802968 | tf_op jit(solution)/shard_map/expert/pallas_call | solution.py:298
  45.0 0.0 copy-start.1
  45.0 0.0 copy-start.4
  45.1 0.0 collective-permute-done.5.refs_1_
  45.1 1.5 %collective-permute-done.7.refs_3_ = bf16[832,128]{1,0:T(8,128)(2,1)S(1)} collective-permute-done((bf16[832,128]{1,0:T(8,128)(2,1)S(1)}, bf16[832,128]{1,0:T(8,128)(2,1)S(1)}, u32[]{:S(2)}, u32[]{:S(2)}) %collective-permute-start.7) | collective-permute-done | bytes 213024 | tf_op jit(solution)/shard_map/ppermute | solution.py:253
  46.6 0.7 collective-permute-start.16
  47.3 2.3 %collective-permute-start.12 = (bf16[832,128]{1,0:T(8,128)(2,1)S(1)}, bf16[832,128]{1,0:T(8,128)(2,1)S(1)}, u32[]{:S(2)}, u32[]{:S(2)}) collective-permute-start(bf16[832,128]{1,0:T(8,128)(2,1)S(1)} %get-tuple-element.58), channel_id=1, source_target_pairs={{0,4},{1,5},{2,6},{3,7},{4,0},{5,1},{6,2},{7,3},{8,12},{9,13},{10,... | collective-permute-start | bytes 638984 | tf_op jit(solution)/shard_map/ppermute | solution.py:253
  49.6 6.0 %collective-permute-start.14 = (bf16[832,128]{1,0:T(8,128)(2,1)S(1)}, bf16[832,128]{1,0:T(8,128)(2,1)S(1)}, u32[]{:S(2)}, u32[]{:S(2)}) collective-permute-start(bf16[832,128]{1,0:T(8,128)(2,1)S(1)} %get-tuple-element.62), channel_id=1, source_target_pairs={{0,5},{1,4},{2,7},{3,6},{4,1},{5,0},{6,3},{7,2},{8,13},{9,12},{10,... | collective-permute-start | bytes 638984 | tf_op jit(solution)/shard_map/ppermute | solution.py:253
  55.6 0.0 collective-permute-start.15
  55.6 0.0 collective-permute-done.12.refs_4_
  55.6 0.0 collective-permute-done.13.refs_5_
  55.6 12.3 %collective-permute-done.14.refs_6_ = bf16[832,128]{1,0:T(8,128)(2,1)S(1)} collective-permute-done((bf16[832,128]{1,0:T(8,128)(2,1)S(1)}, bf16[832,128]{1,0:T(8,128)(2,1)S(1)}, u32[]{:S(2)}, u32[]{:S(2)}) %collective-permute-start.14) | collective-permute-done | bytes 213024 | tf_op jit(solution)/shard_map/ppermute | solution.py:253
  67.9 0.0 collective-permute-done.16
  67.9 0.1 broadcast_select_fusion
  68.0 0.1 collective-permute-start.17
  68.1 2.5 %unpack.1 = (bf16[32,8,8,128]{3,2,1,0:T(8,128)(2,1)}, bf16[18,256,128]{2,1,0:T(8,128)(2,1)}, f32[1,32]{1,0:T(1,128)}) custom-call(f32[1,32]{1,0:T(1,128)S(1)} %convert_bitcast_fusion.key_ref, f32[1,32]{1,0:T(1,128)S(1)} %bitcast.34, bf16[32,8,8,128]{3,2,1,0:T(8,128)(2,1)S(1)} %copy-done.1, bf16[832,128]{1,0:T(8,128)(2,1)S(1)} %get-tuple-element.42.refs_0_, ...), custom_call_target="tpu_custom_call" | custom-call | tf_op jit(solution)/shard_map/unpack/pallas_call | solution.py:327
  70.5 0.0 collective-permute-done.17
  70.5 0.1 convert_add_fusion
  70.7 1.1 %fusion.3 = (f32[9,128,128]{2,1,0:T(8,128)}, f32[9,128,128]{2,1,0:T(8,128)}) fusion(f32[18,128,128]{2,1,0:T(8,128)S(1)} %convert_add_fusion), kind=kLoop, calls=%fused_computation.16 | loop fusion | bytes 2359296 | tf_op jit(solution)/shard_map/unstack | solution.py:326
  (14 shorter events, 0.1 us)
Async XLA Ops:
  0.6 27.4 %collective-permute-start.3 = (bf16[3,3,128,128]{3,2,1,0:T(8,128)(2,1)}, bf16[3,3,128,128]{3,2,1,0:T(8,128)(2,1)S(1)}, u32[]{:S(2)}, u32[]{:S(2)}) collective-permute-start(bf16[3,3,128,128]{3,2,1,0:T(8,128)(2,1)} %bitcast.37), channel_id=1, source_target_pairs={{0,9},{8,1},{2,11},{10,3},{4,13},{12,5},{6,15},{14,7},{16,25},{24,... | collective-permute-start | bytes 884744 | tf_op jit(solution)/shard_map/ppermute | solution.py:238
  6.7 1.0 %copy-start = (bf16[32,8,8,128]{3,2,1,0:T(8,128)(2,1)S(1)}, bf16[32,8,8,128]{3,2,1,0:T(8,128)(2,1)}, u32[]{:S(2)}) copy-start(bf16[32,8,8,128]{3,2,1,0:T(8,128)(2,1)} %cot_ref.3) | copy-start | bytes 1572868
  7.8 1.3 %copy-start.2 = (bf16[32,12,12,128]{3,0,2,1:T(8,128)(2,1)S(1)}, bf16[32,12,12,128]{3,0,2,1:T(8,128)(2,1)}, u32[]{:S(2)}) copy-start(bf16[32,12,12,128]{3,0,2,1:T(8,128)(2,1)} %param.6) | copy-start | bytes 3538948
  9.0 0.7 copy-start.3
  9.7 4.3 %copy-start.6 = (bf16[1,3,3,128,128]{4,3,2,1,0:T(8,128)(2,1)S(1)}, bf16[1,3,3,128,128]{4,3,2,1,0:T(8,128)(2,1)}, u32[]{:S(2)}) copy-start(bf16[1,3,3,128,128]{4,3,2,1,0:T(8,128)(2,1)} %param.10) | copy-start | bytes 884740
  9.7 18.4 %copy-start.5 = (bf16[1,3,3,128,128]{4,3,2,1,0:T(8,128)(2,1)S(1)}, bf16[1,3,3,128,128]{4,3,2,1,0:T(8,128)(2,1)}, u32[]{:S(2)}) copy-start(bf16[1,3,3,128,128]{4,3,2,1,0:T(8,128)(2,1)} %param.9) | copy-start | bytes 884740
  10.9 8.2 %collective-permute-start.1 = (bf16[832,128]{1,0:T(8,128)(2,1)S(1)}, bf16[832,128]{1,0:T(8,128)(2,1)S(1)}, u32[]{:S(2)}, u32[]{:S(2)}) collective-permute-start(bf16[832,128]{1,0:T(8,128)(2,1)S(1)} %get-tuple-element.40), channel_id=1, source_target_pairs={{0,6},{1,7},{2,4},{3,5},{4,2},{5,3},{6,0},{7,1},{8,14},{9,15},{10,... | collective-permute-start | bytes 638984 | tf_op jit(solution)/shard_map/ppermute | solution.py:253
  13.5 7.3 %collective-permute-start = (bf16[832,128]{1,0:T(8,128)(2,1)S(1)}, bf16[832,128]{1,0:T(8,128)(2,1)S(1)}, u32[]{:S(2)}, u32[]{:S(2)}) collective-permute-start(bf16[832,128]{1,0:T(8,128)(2,1)S(1)} %get-tuple-element.39), channel_id=1, source_target_pairs={{0,1},{1,0},{2,3},{3,2},{4,5},{5,4},{6,7},{7,6},{8,9},{9,8},{10,11... | collective-permute-start | bytes 638984 | tf_op jit(solution)/shard_map/ppermute | solution.py:253
  13.5 10.6 %collective-permute-start.2 = (bf16[832,128]{1,0:T(8,128)(2,1)S(1)}, bf16[832,128]{1,0:T(8,128)(2,1)S(1)}, u32[]{:S(2)}, u32[]{:S(2)}) collective-permute-start(bf16[832,128]{1,0:T(8,128)(2,1)S(1)} %get-tuple-element.41), channel_id=1, source_target_pairs={{0,7},{1,6},{2,5},{3,4},{4,3},{5,2},{6,1},{7,0},{8,15},{9,14},{10,... | collective-permute-start | bytes 638984 | tf_op jit(solution)/shard_map/ppermute | solution.py:253
  14.0 14.3 %collective-permute-start.4 = (bf16[3,3,128,128]{3,2,1,0:T(8,128)(2,1)S(1)}, bf16[3,3,128,128]{3,2,1,0:T(8,128)(2,1)}, u32[]{:S(2)}, u32[]{:S(2)}) collective-permute-start(bf16[3,3,128,128]{3,2,1,0:T(8,128)(2,1)S(1)} %bitcast.38), channel_id=1, source_target_pairs={{0,9},{8,1},{2,11},{10,3},{4,13},{12,5},{6,15},{14,7},{16,25},{24,... | collective-permute-start | bytes 884744 | tf_op jit(solution)/shard_map/ppermute | solution.py:238
  19.2 14.7 %collective-permute-start.9 = (bf16[832,128]{1,0:T(8,128)(2,1)S(1)}, bf16[832,128]{1,0:T(8,128)(2,1)S(1)}, u32[]{:S(2)}, u32[]{:S(2)}) collective-permute-start(bf16[832,128]{1,0:T(8,128)(2,1)S(1)} %get-tuple-element.48), channel_id=1, source_target_pairs={{0,4},{1,5},{2,6},{3,7},{4,0},{5,1},{6,2},{7,3},{8,12},{9,13},{10,... | collective-permute-start | bytes 638984 | tf_op jit(solution)/shard_map/ppermute | solution.py:253
  20.8 14.6 %collective-permute-start.8 = (bf16[832,128]{1,0:T(8,128)(2,1)S(1)}, bf16[832,128]{1,0:T(8,128)(2,1)S(1)}, u32[]{:S(2)}, u32[]{:S(2)}) collective-permute-start(bf16[832,128]{1,0:T(8,128)(2,1)S(1)} %get-tuple-element.47), channel_id=1, source_target_pairs={{0,2},{1,3},{2,0},{3,1},{4,6},{5,7},{6,4},{7,5},{8,10},{9,11},{10,... | collective-permute-start | bytes 638984 | tf_op jit(solution)/shard_map/ppermute | solution.py:253
  24.1 12.6 %collective-permute-start.10 = (bf16[832,128]{1,0:T(8,128)(2,1)S(1)}, bf16[832,128]{1,0:T(8,128)(2,1)S(1)}, u32[]{:S(2)}, u32[]{:S(2)}) collective-permute-start(bf16[832,128]{1,0:T(8,128)(2,1)S(1)} %get-tuple-element.50), channel_id=1, source_target_pairs={{0,3},{1,2},{2,1},{3,0},{4,7},{5,6},{6,5},{7,4},{8,11},{9,10},{10,... | collective-permute-start | bytes 638984 | tf_op jit(solution)/shard_map/ppermute | solution.py:253
  28.0 8.6 %collective-permute-start.11 = (bf16[832,128]{1,0:T(8,128)(2,1)S(1)}, bf16[832,128]{1,0:T(8,128)(2,1)}, u32[]{:S(2)}, u32[]{:S(2)}) collective-permute-start(bf16[832,128]{1,0:T(8,128)(2,1)S(1)} %get-tuple-element.52), channel_id=1, source_target_pairs={{0,5},{1,4},{2,7},{3,6},{4,1},{5,0},{6,3},{7,2},{8,13},{9,12},{10,... | collective-permute-start | bytes 638984 | tf_op jit(solution)/shard_map/ppermute | solution.py:253
  33.8 11.2 %collective-permute-start.5 = (bf16[832,128]{1,0:T(8,128)(2,1)S(1)}, bf16[832,128]{1,0:T(8,128)(2,1)S(1)}, u32[]{:S(2)}, u32[]{:S(2)}) collective-permute-start(bf16[832,128]{1,0:T(8,128)(2,1)S(1)} %get-tuple-element.43), channel_id=1, source_target_pairs={{0,1},{1,0},{2,3},{3,2},{4,5},{5,4},{6,7},{7,6},{8,9},{9,8},{10,11... | collective-permute-start | bytes 638984 | tf_op jit(solution)/shard_map/ppermute | solution.py:253
  33.9 11.1 %collective-permute-start.6 = (bf16[832,128]{1,0:T(8,128)(2,1)S(1)}, bf16[832,128]{1,0:T(8,128)(2,1)S(1)}, u32[]{:S(2)}, u32[]{:S(2)}) collective-permute-start(bf16[832,128]{1,0:T(8,128)(2,1)S(1)} %get-tuple-element.44), channel_id=1, source_target_pairs={{0,6},{1,7},{2,4},{3,5},{4,2},{5,3},{6,0},{7,1},{8,14},{9,15},{10,... | collective-permute-start | bytes 638984 | tf_op jit(solution)/shard_map/ppermute | solution.py:253
  35.5 11.1 %collective-permute-start.7 = (bf16[832,128]{1,0:T(8,128)(2,1)S(1)}, bf16[832,128]{1,0:T(8,128)(2,1)S(1)}, u32[]{:S(2)}, u32[]{:S(2)}) collective-permute-start(bf16[832,128]{1,0:T(8,128)(2,1)S(1)} %get-tuple-element.45), channel_id=1, source_target_pairs={{0,7},{1,6},{2,5},{3,4},{4,3},{5,2},{6,1},{7,0},{8,15},{9,14},{10,... | collective-permute-start | bytes 638984 | tf_op jit(solution)/shard_map/ppermute | solution.py:253
  45.0 23.0 %copy-start.1 = (bf16[32,8,8,128]{3,2,1,0:T(8,128)(2,1)S(1)}, bf16[32,8,8,128]{3,2,1,0:T(8,128)(2,1)}, u32[]{:S(2)}) copy-start(bf16[32,8,8,128]{3,2,1,0:T(8,128)(2,1)} %cot_ref.3) | copy-start | bytes 1572868
  45.0 23.0 %copy-start.4 = (f32[32]{0:T(128)S(1)}, f32[32]{0:T(128)}, u32[]{:S(2)}) copy-start(f32[32]{0:T(128)} %param.8) | copy-start | bytes 388
  46.6 21.3 %collective-permute-start.16 = (bf16[18,128,128]{2,1,0:T(8,128)(2,1)S(1)}, bf16[18,128,128]{2,1,0:T(8,128)(2,1)S(1)}, u32[]{:S(2)}, u32[]{:S(2)}) collective-permute-start(bf16[18,128,128]{2,1,0:T(8,128)(2,1)S(1)} %get-tuple-element.68), channel_id=1, source_target_pairs={{1,9},{9,1},{3,11},{11,3},{5,13},{13,5},{7,15},{15,7},{17,25},{25,... | collective-permute-start | bytes 1769480 | tf_op jit(solution)/shard_map/ppermute | solution.py:321
  47.3 8.3 %collective-permute-start.12 = (bf16[832,128]{1,0:T(8,128)(2,1)S(1)}, bf16[832,128]{1,0:T(8,128)(2,1)S(1)}, u32[]{:S(2)}, u32[]{:S(2)}) collective-permute-start(bf16[832,128]{1,0:T(8,128)(2,1)S(1)} %get-tuple-element.58), channel_id=1, source_target_pairs={{0,4},{1,5},{2,6},{3,7},{4,0},{5,1},{6,2},{7,3},{8,12},{9,13},{10,... | collective-permute-start | bytes 638984 | tf_op jit(solution)/shard_map/ppermute | solution.py:253
  49.6 6.0 %collective-permute-start.13 = (bf16[832,128]{1,0:T(8,128)(2,1)S(1)}, bf16[832,128]{1,0:T(8,128)(2,1)S(1)}, u32[]{:S(2)}, u32[]{:S(2)}) collective-permute-start(bf16[832,128]{1,0:T(8,128)(2,1)S(1)} %get-tuple-element.60), channel_id=1, source_target_pairs={{0,2},{1,3},{2,0},{3,1},{4,6},{5,7},{6,4},{7,5},{8,10},{9,11},{10,... | collective-permute-start | bytes 638984 | tf_op jit(solution)/shard_map/ppermute | solution.py:253
  49.6 18.3 %collective-permute-start.14 = (bf16[832,128]{1,0:T(8,128)(2,1)S(1)}, bf16[832,128]{1,0:T(8,128)(2,1)S(1)}, u32[]{:S(2)}, u32[]{:S(2)}) collective-permute-start(bf16[832,128]{1,0:T(8,128)(2,1)S(1)} %get-tuple-element.62), channel_id=1, source_target_pairs={{0,5},{1,4},{2,7},{3,6},{4,1},{5,0},{6,3},{7,2},{8,13},{9,12},{10,... | collective-permute-start | bytes 638984 | tf_op jit(solution)/shard_map/ppermute | solution.py:253
  55.6 12.3 %collective-permute-start.15 = (bf16[832,128]{1,0:T(8,128)(2,1)S(1)}, bf16[832,128]{1,0:T(8,128)(2,1)S(1)}, u32[]{:S(2)}, u32[]{:S(2)}) collective-permute-start(bf16[832,128]{1,0:T(8,128)(2,1)S(1)} %get-tuple-element.64), channel_id=1, source_target_pairs={{0,3},{1,2},{2,1},{3,0},{4,7},{5,6},{6,5},{7,4},{8,11},{9,10},{10,... | collective-permute-start | bytes 638984 | tf_op jit(solution)/shard_map/ppermute | solution.py:253
  68.0 2.6 %collective-permute-start.17 = (bf16[18,128,128]{2,1,0:T(8,128)(2,1)S(1)}, bf16[18,128,128]{2,1,0:T(8,128)(2,1)S(1)}, u32[]{:S(2)}, u32[]{:S(2)}) collective-permute-start(bf16[18,128,128]{2,1,0:T(8,128)(2,1)S(1)} %broadcast_select_fusion), channel_id=1, source_target_pairs={{0,1},{1,0},{2,3},{3,2},{4,5},{5,4},{6,7},{7,6},{8,9},{9,8},{10,11... | collective-permute-start | bytes 1769480 | tf_op jit(solution)/shard_map/ppermute | solution.py:324

commit v5 on v4

--- a/solution.py
+++ b/solution.py
@@ -12,6 +12,8 @@
 SWAP_HOME = [(1, 3), (3, 1)]
 TAPS = 3
 BLOCK = 8
+PLACED = pl.BlockSpec(memory_space=pl.ANY)
+PACK_PARAMS = pltpu.CompilerParams(vmem_limit_bytes=56 * 1024 * 1024)
 PARAMS = pltpu.CompilerParams(vmem_limit_bytes=40 * 1024 * 1024)
 
 
@@ -51,11 +53,23 @@
     return jnp.where(match, 1.0, 0.0).astype(jnp.bfloat16)
 
 
-def pack_kernel(slots, key_ref, gate_ref, tiles_ref, cot_ref, *out_refs):
+def pack_kernel(slots, place, route_at, gate_at, tiles_at, cot_at, *refs):
+    route_ref, gate_ref, tiles_ref, cot_ref, sems = refs[-5:]
+    *out_refs, pick_ref, cot_pick_ref = refs[:-5]
     peers = len(out_refs)
     step = BLOCK * slots
-    key = key_ref[...]
+    pairs = ((route_at, route_ref), (gate_at, gate_ref), (tiles_at, tiles_ref), (cot_at, cot_ref))
+    made = [pltpu.make_async_copy(a, b, sems.at[k]) for k, (a, b) in enumerate(pairs)]
+    for copy in made:
+        copy.start()
+    made[0].wait()
+    key = place(route_ref[...]).astype(jnp.float32)
     pick = slot_matrix(key, slots, peers, True)
+    cot_pick = slot_matrix(key, slots, peers, False)
+    pick_ref[...] = pick.T
+    cot_pick_ref[...] = cot_pick.T
+    made[1].wait()
+    gate = onto_rows(gate_ref[...])[:, :, None]
     blocks = tiles_ref.shape[0]
 
     def put(at, values):
@@ -63,37 +77,33 @@
         for peer in range(peers):
             out_refs[peer][at : at + step, :] = values[peer * step : (peer + 1) * step, :]
 
+    made[2].wait()
     for block in range(blocks):
         put(block * step, dot(pick, tiles_ref[block]))
-    pick = slot_matrix(key, slots, peers, False)
-    gate = onto_rows(gate_ref[...])[:, :, None]
+    made[3].wait()
     patches, rows, cols, channels = cot_ref.shape
     for i in range(rows):
         scaled = cot_ref[:, i, :, :].astype(jnp.float32) * gate
         scaled = scaled.reshape(patches * cols, channels).astype(jnp.bfloat16)
-        put((blocks + i) * step, dot(pick, scaled))
-
-
-def unpack_kernel(slots, queue, key_ref, gate_ref, cot_ref, *refs):
+        put((blocks + i) * step, dot(cot_pick, scaled))
+
+
+def unpack_kernel(slots, queue, pick_ref, cot_pick_ref, gate_ref, cot_ref, *refs):
     msgs, (out_ref, tiles_ref, gate_grad_ref) = refs[:-3], refs[-3:]
     msgs = [msgs[queue.index(peer)] for peer in range(len(msgs))]
-    peers = len(msgs)
     step = BLOCK * slots
-    key = key_ref[...]
 
     def gather(block):
         return jnp.concatenate([m[block * step : (block + 1) * step, :] for m in msgs], axis=0)
 
     blocks = tiles_ref.shape[0]
-    pick = slot_matrix(key, slots, peers, True).T
     for block in range(blocks):
-        tiles_ref[block] = dot(pick, gather(block)).astype(jnp.bfloat16)
-    pick = slot_matrix(key, slots, peers, False).T
+        tiles_ref[block] = dot(pick_ref[...], gather(block)).astype(jnp.bfloat16)
     gate = onto_rows(gate_ref[...])[:, :, None]
     patches, rows, cols, channels = cot_ref.shape
     total = jnp.zeros((patches, cols, channels), jnp.float32)
     for i in range(rows):
-        result = dot(pick, gather(blocks + i)).reshape(patches, cols, channels)
+        result = dot(cot_pick_ref[...], gather(blocks + i)).reshape(patches, cols, channels)
         out_ref[:, i, :, :] = (result * gate).astype(jnp.bfloat16)
         total = total + result * cot_ref[:, i, :, :].astype(jnp.float32)
     sums = jnp.sum(jnp.sum(total, axis=1), axis=1, keepdims=True)
@@ -220,9 +230,7 @@
     halves = lax.axis_size("half")
     per_half = lax.axis_size("owner")
     cores = lax.axis_size("replica")
-    half = lax.axis_index("half")
     core = lax.axis_index("replica")
-    me = lax.axis_index("owner") * cores + core
     peers = per_half * cores
     patches, side, _, channels = tiles.shape
     out_side = cotangent.shape[1]
@@ -237,8 +245,11 @@
     other_one, other_two = (
         lax.ppermute(k[0], ("half", "replica"), SWAP) for k in (conv_first, conv_second)
     )
-    route_core = (route // per_half - half + halves) % halves
-    key = ((((route % per_half) * cores + route_core) ^ me).astype(jnp.float32))[None, :]
+    def place(route):
+        home, owner = route // per_half, route % per_half
+        here = lax.axis_index("owner") * cores + lax.axis_index("replica")
+        return (owner * cores + (home + halves - lax.axis_index("half")) % halves) ^ here
+
     gate_row = gate[None, :]
     tiles_rows = jnp.transpose(tiles, (1, 2, 0, 3)).reshape(blocks, BLOCK * patches, channels)
 
@@ -252,17 +263,27 @@
             message, _ = lax.optimization_barrier((message, after))
         return lax.ppermute(message, ("owner", "replica"), [(i, i ^ mask) for i in range(peers)])
 
-    packed = pl.pallas_call(
-        functools.partial(pack_kernel, slots),
-        out_shape=[bf16((message, channels))] * peers,
-        compiler_params=PARAMS,
+    picks = [bf16((BLOCK * patches, peers * BLOCK * slots))] * 2
+    *packed, pick, cot_pick = pl.pallas_call(
+        functools.partial(pack_kernel, slots, place),
+        in_specs=[PLACED] * 4,
+        out_shape=[bf16((message, channels))] * peers + picks,
+        scratch_shapes=[
+            pltpu.VMEM((1, patches), jnp.int32),
+            pltpu.VMEM((1, patches), jnp.float32),
+            pltpu.VMEM(tiles_rows.shape, jnp.bfloat16),
+            pltpu.VMEM(cotangent.shape, jnp.bfloat16),
+            pltpu.SemaphoreType.DMA((4,)),
+        ],
+        compiler_params=PACK_PARAMS,
         name="pack",
-    )(key, gate_row, tiles_rows, cotangent)
+    )(route[None, :], gate_row, tiles_rows, cotangent)
+
     nearer = sorted(chunks[1], key=lambda mask: (mask % cores, -mask))
     queue = [mask for mask in chunks[0] if mask >= cores] + order[1:cores] + nearer
     got = {0: packed[0]}
     for i, mask in enumerate(queue):
-        got[mask] = exchange(mask, packed[mask], got[queue[i - 4]] if i >= 4 else None)
+        got[mask] = exchange(mask, packed[mask], got[queue[0]] if i >= 4 else None)
     arrived = [[got[mask] for mask in chunk] for chunk in chunks]
 
     kernel_one = jnp.where(core == 0, conv_first[0], other_one)
@@ -333,7 +354,7 @@
         ],
         compiler_params=PARAMS,
         name="unpack",
-    )(key, gate_row, cotangent, *[backs[mask] for mask in [*chunks[0], *nearer]])
+    )(pick, cot_pick, gate_row, cotangent, *[backs[mask] for mask in [*chunks[0], *nearer]])
     tiles_grad = jnp.transpose(tiles_out.reshape(side, side, patches, channels), (2, 0, 1, 3))
     return (output, tiles_grad, first_grad, second_grad, gate_grad[0])
 

time: 72.1 us -> 69.4 us (0.963)
  starting transfers between devices: 30.8 us -> 22.9 us
  waiting for transfers between devices: 17.4 us -> 24.6 us
  local copies, waits for them, and re-layouts: 4.52 us -> 1.92 us
  Pallas kernels: 17.3 us -> 18.6 us
    ppermute x14, waiting for transfers between devices: 17.4 us -> 24.6 us  [exchange(): lax.ppermute(message, ('owner', 'replica'), [(i, i ^ mask) for i in range...]
    ppermute x14, starting transfers between devices: 22.1 us -> 15.4 us  [exchange(): lax.ppermute(message, ('owner', 'replica'), [(i, i ^ mask) for i in range...]
    unnamed x14 -> x18, local copies, waits for them, and re-layouts: 2.98 us -> 0.37 us
    pallas_call x1, Pallas kernels: 1.23 us -> 3.71 us  [shards(): pl.pallas_call(functools.partial(pack_kernel, slots, place), in_specs=[PL...]
    ppermute x2, starting transfers between devices: 7.96 us -> 6.83 us  [shards(): lax.ppermute(k[0], ('half', 'replica'), SWAP)]
    pallas_call x2, Pallas kernels: 13.6 us -> 12.6 us  [expert(): pl.pallas_call(functools.partial(expert_kernel, part, slots, side, len(he...]
  transfers between devices with their start and end apart: 18 -> 18, of which waited for: 4 -> 4; matrix products, arithmetic and copies ran while one was open for 2% -> 1% of each run, Pallas kernels for 24% -> 27%
where the time goes in v5:
time: 69.4 us; the launch traced here: 69.2 us
  waiting for transfers between devices  24.6 us (35%)
  starting transfers between devices  22.9 us (33%)
  Pallas kernels  18.6 us (27%)
  local copies, waits for them, and re-layouts  1.92 us (3%)
  between operations  0.9 us (1%)
    ppermute x14, waiting for transfers between devices, exchange(): lax.ppermute(message, ('owner', 'replica'), [(i, i ^ mask) for i in range...  24.6 us
    ppermute x14, starting transfers between devices, exchange(): lax.ppermute(message, ('owner', 'replica'), [(i, i ^ mask) for i in range...  15.4 us
    pallas_call x2, Pallas kernels, expert(): pl.pallas_call(functools.partial(expert_kernel, part, slots, side, len(he...  12.6 us
    ppermute x2, starting transfers between devices, shards(): lax.ppermute(k[0], ('half', 'replica'), SWAP)  6.83 us
    pallas_call x1, Pallas kernels, shards(): pl.pallas_call(functools.partial(pack_kernel, slots, place), in_specs=[PL...  3.71 us
    pallas_call x1, Pallas kernels, shards(): pl.pallas_call(functools.partial(unpack_kernel, slots, [*chunks[0], *near...  2.26 us
  transfers between devices with their start and end apart: 18, of which 4 were waited for; matrix products, arithmetic and copies ran while one was open for 1% of the time, Pallas kernels for 27%

profile of v5, /device:TPU:0, one launch (start us, length us, event | category | flops | bytes accessed | tf_op | source)
XLA Modules:
  0.0 69.2 jit_solution(8845676528266673741)
XLA Ops:
  0.7 5.5 %collective-permute-start.3 = (bf16[3,3,128,128]{3,2,1,0:T(8,128)(2,1)}, bf16[3,3,128,128]{3,2,1,0:T(8,128)(2,1)S(1)}, u32[]{:S(2)}, u32[]{:S(2)}) collective-permute-start(bf16[3,3,128,128]{3,2,1,0:T(8,128)(2,1)} %bitcast.36), channel_id=1, source_target_pairs={{0,9},{8,1},{2,11},{10,3},{4,13},{12,5},{6,15},{14,7},{16,25},{24,... | collective-permute-start | bytes 884744 | tf_op jit(solution)/shard_map/ppermute | solution.py:246
  6.2 3.7 %pack.1 = (bf16[832,128]{1,0:T(8,128)(2,1)}, bf16[832,128]{1,0:T(8,128)(2,1)}, bf16[832,128]{1,0:T(8,128)(2,1)}, bf16[832,128]{1,0:T(8,128)(2,1)}, bf16[832,128]...) custom-call(s32[1,32]{1,0:T(1,128)} %bitcast.38, ...), custom_call_target="tpu_custom_call" | custom-call | tf_op jit(solution)/shard_map/pack/pallas_call | solution.py:267
  9.9 0.0 copy-start.8
  9.9 2.6 %collective-permute-start.1 = (bf16[832,128]{1,0:T(8,128)(2,1)}, bf16[832,128]{1,0:T(8,128)(2,1)S(1)}, u32[]{:S(2)}, u32[]{:S(2)}) collective-permute-start(bf16[832,128]{1,0:T(8,128)(2,1)} %get-tuple-element.44), channel_id=1, source_target_pairs={{0,6},{1,7},{2,4},{3,5},{4,2},{5,3},{6,0},{7,1},{8,14},{9,15},{10,... | collective-permute-start | bytes 638984 | tf_op jit(solution)/shard_map/ppermute | solution.py:264
  12.5 1.3 %collective-permute-start.4 = (bf16[3,3,128,128]{3,2,1,0:T(8,128)(2,1)S(1)}, bf16[3,3,128,128]{3,2,1,0:T(8,128)(2,1)S(1)}, u32[]{:S(2)}, u32[]{:S(2)}) collective-permute-start(bf16[3,3,128,128]{3,2,1,0:T(8,128)(2,1)S(1)} %bitcast.37), channel_id=1, source_target_pairs={{0,9},{8,1},{2,11},{10,3},{4,13},{12,5},{6,15},{14,7},{16,25},{24,... | collective-permute-start | bytes 884744 | tf_op jit(solution)/shard_map/ppermute | solution.py:246
  13.8 0.1 collective-permute-start
  13.9 0.5 collective-permute-start.2
  14.4 8.8 %collective-permute-done.1.refs_2_ = bf16[832,128]{1,0:T(8,128)(2,1)S(1)} collective-permute-done((bf16[832,128]{1,0:T(8,128)(2,1)}, bf16[832,128]{1,0:T(8,128)(2,1)S(1)}, u32[]{:S(2)}, u32[]{:S(2)}) %collective-permute-start.1) | collective-permute-done | bytes 213024 | tf_op jit(solution)/shard_map/ppermute | solution.py:264
  23.2 0.0 collective-permute-start.9
  23.2 0.0 collective-permute-done.3
  23.2 0.2 collective-permute-start.8
  23.5 0.0 copy-start.4
  23.5 0.2 copy.11
  23.7 0.0 collective-permute-done.4
  23.7 0.1 collective-permute-start.10
  23.8 0.2 copy.12
  24.0 0.0 collective-permute-done.refs_1_
  24.0 0.3 copy-done.7
  24.4 3.3 %collective-permute-start.11 = (bf16[832,128]{1,0:T(8,128)(2,1)S(1)}, bf16[832,128]{1,0:T(8,128)(2,1)S(1)}, u32[]{:S(2)}, u32[]{:S(2)}) collective-permute-start(bf16[832,128]{1,0:T(8,128)(2,1)S(1)} %copy-done.7), channel_id=1, source_target_pairs={{0,5},{1,4},{2,7},{3,6},{4,1},{5,0},{6,3},{7,2},{8,13},{9,12},{10,... | collective-permute-start | bytes 638984 | tf_op jit(solution)/shard_map/ppermute | solution.py:264
  27.7 0.0 collective-permute-done.2.refs_3_
  27.7 5.2 %expert.2 = (bf16[832,128]{1,0:T(8,128)(2,1)S(1)}, bf16[832,128]{1,0:T(8,128)(2,1)S(1)}, bf16[832,128]{1,0:T(8,128)(2,1)S(1)}, bf16[832,128]{1,0:T(8,128)(2,1)S(...) custom-call(bf16[832,128]{1,0:T(8,128)(2,1)S(1)} %copy-done.4, ...), custom_call_target="tpu_custom_call" | custom-call | flops 15401484288 | bytes 30802968 | tf_op jit(solution)/shard_map/expert/pallas_call | solution.py:319
  32.9 0.1 collective-permute-start.5
  33.0 0.0 collective-permute-done.9.refs_1_
  33.0 1.7 %collective-permute-start.6 = (bf16[832,128]{1,0:T(8,128)(2,1)S(1)}, bf16[832,128]{1,0:T(8,128)(2,1)S(1)}, u32[]{:S(2)}, u32[]{:S(2)}) collective-permute-start(bf16[832,128]{1,0:T(8,128)(2,1)S(1)} %get-tuple-element.48), channel_id=1, source_target_pairs={{0,6},{1,7},{2,4},{3,5},{4,2},{5,3},{6,0},{7,1},{8,14},{9,15},{10,... | collective-permute-start | bytes 638984 | tf_op jit(solution)/shard_map/ppermute | solution.py:264
  34.7 0.0 collective-permute-done.8.refs_0_
  34.7 1.1 %collective-permute-start.7 = (bf16[832,128]{1,0:T(8,128)(2,1)S(1)}, bf16[832,128]{1,0:T(8,128)(2,1)S(1)}, u32[]{:S(2)}, u32[]{:S(2)}) collective-permute-start(bf16[832,128]{1,0:T(8,128)(2,1)S(1)} %get-tuple-element.49), channel_id=1, source_target_pairs={{0,7},{1,6},{2,5},{3,4},{4,3},{5,2},{6,1},{7,0},{8,15},{9,14},{10,... | collective-permute-start | bytes 638984 | tf_op jit(solution)/shard_map/ppermute | solution.py:264
  35.8 0.0 collective-permute-done.10.refs_2_
  35.8 0.0 collective-permute-done.11.refs_3_
  35.8 7.4 %expert.3 = (bf16[832,128]{1,0:T(8,128)(2,1)S(1)}, bf16[832,128]{1,0:T(8,128)(2,1)S(1)}, bf16[832,128]{1,0:T(8,128)(2,1)S(1)}, bf16[832,128]{1,0:T(8,128)(2,1)S(1)}, bf16[18,128,128]{2,1,0:T(8,128)(2,1)S(1)}) custom-call(bf16[832,128]{1,0:T(8,128)(2,1)S(1)} %collective-permute-done.8.refs_0_, bf16[832,128]{1,0:T(8,128)(2,1)S(1)} %collective-permute-done.9.refs_1_, ...), custom_call_target="tpu_custom_call" | custom-call | flops 15401484288 | bytes 30802968 | tf_op jit(solution)/shard_map/expert/pallas_call | solution.py:319
  43.2 0.0 copy-start
  43.2 0.0 copy-start.3
  43.2 0.0 collective-permute-done.5.refs_1_
  43.2 0.0 collective-permute-done.6.refs_2_
  43.3 2.4 %collective-permute-done.7.refs_3_ = bf16[832,128]{1,0:T(8,128)(2,1)S(1)} collective-permute-done((bf16[832,128]{1,0:T(8,128)(2,1)S(1)}, bf16[832,128]{1,0:T(8,128)(2,1)S(1)}, u32[]{:S(2)}, u32[]{:S(2)}) %collective-permute-start.7) | collective-permute-done | bytes 213024 | tf_op jit(solution)/shard_map/ppermute | solution.py:264
  45.7 0.7 collective-permute-start.16
  46.4 0.1 collective-permute-start.12
  46.5 1.4 %collective-permute-start.13 = (bf16[832,128]{1,0:T(8,128)(2,1)S(1)}, bf16[832,128]{1,0:T(8,128)(2,1)S(1)}, u32[]{:S(2)}, u32[]{:S(2)}) collective-permute-start(bf16[832,128]{1,0:T(8,128)(2,1)S(1)} %get-tuple-element.64), channel_id=1, source_target_pairs={{0,2},{1,3},{2,0},{3,1},{4,6},{5,7},{6,4},{7,5},{8,10},{9,11},{10,... | collective-permute-start | bytes 638984 | tf_op jit(solution)/shard_map/ppermute | solution.py:264
  47.9 4.0 %collective-permute-start.14 = (bf16[832,128]{1,0:T(8,128)(2,1)S(1)}, bf16[832,128]{1,0:T(8,128)(2,1)S(1)}, u32[]{:S(2)}, u32[]{:S(2)}) collective-permute-start(bf16[832,128]{1,0:T(8,128)(2,1)S(1)} %get-tuple-element.66), channel_id=1, source_target_pairs={{0,5},{1,4},{2,7},{3,6},{4,1},{5,0},{6,3},{7,2},{8,13},{9,12},{10,... | collective-permute-start | bytes 638984 | tf_op jit(solution)/shard_map/ppermute | solution.py:264
  51.8 0.4 collective-permute-start.15
  52.2 2.6 %collective-permute-done.12.refs_4_ = bf16[832,128]{1,0:T(8,128)(2,1)S(1)} collective-permute-done((bf16[832,128]{1,0:T(8,128)(2,1)S(1)}, bf16[832,128]{1,0:T(8,128)(2,1)S(1)}, u32[]{:S(2)}, u32[]{:S(2)}) %collective-permute-start.12) | collective-permute-done | bytes 213024 | tf_op jit(solution)/shard_map/ppermute | solution.py:264
  54.8 0.0 collective-permute-done.13.refs_5_
  54.8 10.7 %collective-permute-done.14.refs_6_ = bf16[832,128]{1,0:T(8,128)(2,1)S(1)} collective-permute-done((bf16[832,128]{1,0:T(8,128)(2,1)S(1)}, bf16[832,128]{1,0:T(8,128)(2,1)S(1)}, u32[]{:S(2)}, u32[]{:S(2)}) %collective-permute-start.14) | collective-permute-done | bytes 213024 | tf_op jit(solution)/shard_map/ppermute | solution.py:264
  65.5 0.1 broadcast_select_fusion
  65.6 0.1 collective-permute-start.17
  65.7 2.3 %unpack.1 = (bf16[32,8,8,128]{3,2,1,0:T(8,128)(2,1)}, bf16[18,256,128]{2,1,0:T(8,128)(2,1)}, f32[1,32]{1,0:T(1,128)}) custom-call(bf16[256,256]{1,0:T(8,128)(2,1)S(1)} %copy-done.1, bf16[256,256]{1,0:T(8,128)(2,1)S(1)} %copy-done.2, f32[1,32]{1,0:T(1,128)S(1)} %bitcast.32, bf16[32,8,8,128]{3,2,1,0:T(8,128)(2,1)S(1)} %copy-done, ...), custom_call_target="tpu_custom_call" | custom-call | tf_op jit(solution)/shard_map/unpack/pallas_call | solution.py:348
  67.9 0.0 collective-permute-done.17
  67.9 0.1 convert_add_fusion
  68.1 1.1 %fusion = (f32[9,128,128]{2,1,0:T(8,128)}, f32[9,128,128]{2,1,0:T(8,128)}) fusion(f32[18,128,128]{2,1,0:T(8,128)S(1)} %convert_add_fusion), kind=kLoop, calls=%fused_computation.4 | loop fusion | bytes 2359296 | tf_op jit(solution)/shard_map/unstack | solution.py:347
  (17 shorter events, 0.1 us)
Async XLA Ops:
  0.6 22.8 %copy-start.5 = (bf16[1,3,3,128,128]{4,3,2,1,0:T(8,128)(2,1)S(1)}, bf16[1,3,3,128,128]{4,3,2,1,0:T(8,128)(2,1)}, u32[]{:S(2)}) copy-start(bf16[1,3,3,128,128]{4,3,2,1,0:T(8,128)(2,1)} %param.9) | copy-start | bytes 884740
  0.6 11.9 %copy-start.6 = (bf16[1,3,3,128,128]{4,3,2,1,0:T(8,128)(2,1)S(1)}, bf16[1,3,3,128,128]{4,3,2,1,0:T(8,128)(2,1)}, u32[]{:S(2)}) copy-start(bf16[1,3,3,128,128]{4,3,2,1,0:T(8,128)(2,1)} %param.10) | copy-start | bytes 884740
  0.7 22.6 %collective-permute-start.3 = (bf16[3,3,128,128]{3,2,1,0:T(8,128)(2,1)}, bf16[3,3,128,128]{3,2,1,0:T(8,128)(2,1)S(1)}, u32[]{:S(2)}, u32[]{:S(2)}) collective-permute-start(bf16[3,3,128,128]{3,2,1,0:T(8,128)(2,1)} %bitcast.36), channel_id=1, source_target_pairs={{0,9},{8,1},{2,11},{10,3},{4,13},{12,5},{6,15},{14,7},{16,25},{24,... | collective-permute-start | bytes 884744 | tf_op jit(solution)/shard_map/ppermute | solution.py:246
  9.9 13.8 %copy-start.8 = (bf16[832,128]{1,0:T(8,128)(2,1)S(1)}, bf16[832,128]{1,0:T(8,128)(2,1)}, u32[]{:S(2)}) copy-start(bf16[832,128]{1,0:T(8,128)(2,1)} %get-tuple-element.54) | copy-start | bytes 638980
  9.9 13.3 %collective-permute-start.1 = (bf16[832,128]{1,0:T(8,128)(2,1)}, bf16[832,128]{1,0:T(8,128)(2,1)S(1)}, u32[]{:S(2)}, u32[]{:S(2)}) collective-permute-start(bf16[832,128]{1,0:T(8,128)(2,1)} %get-tuple-element.44), channel_id=1, source_target_pairs={{0,6},{1,7},{2,4},{3,5},{4,2},{5,3},{6,0},{7,1},{8,14},{9,15},{10,... | collective-permute-start | bytes 638984 | tf_op jit(solution)/shard_map/ppermute | solution.py:264
  12.5 11.2 %collective-permute-start.4 = (bf16[3,3,128,128]{3,2,1,0:T(8,128)(2,1)S(1)}, bf16[3,3,128,128]{3,2,1,0:T(8,128)(2,1)S(1)}, u32[]{:S(2)}, u32[]{:S(2)}) collective-permute-start(bf16[3,3,128,128]{3,2,1,0:T(8,128)(2,1)S(1)} %bitcast.37), channel_id=1, source_target_pairs={{0,9},{8,1},{2,11},{10,3},{4,13},{12,5},{6,15},{14,7},{16,25},{24,... | collective-permute-start | bytes 884744 | tf_op jit(solution)/shard_map/ppermute | solution.py:246
  13.8 10.2 %collective-permute-start = (bf16[832,128]{1,0:T(8,128)(2,1)}, bf16[832,128]{1,0:T(8,128)(2,1)S(1)}, u32[]{:S(2)}, u32[]{:S(2)}) collective-permute-start(bf16[832,128]{1,0:T(8,128)(2,1)} %get-tuple-element.43), channel_id=1, source_target_pairs={{0,1},{1,0},{2,3},{3,2},{4,5},{5,4},{6,7},{7,6},{8,9},{9,8},{10,11... | collective-permute-start | bytes 638984 | tf_op jit(solution)/shard_map/ppermute | solution.py:264
  13.9 13.8 %collective-permute-start.2 = (bf16[832,128]{1,0:T(8,128)(2,1)}, bf16[832,128]{1,0:T(8,128)(2,1)S(1)}, u32[]{:S(2)}, u32[]{:S(2)}) collective-permute-start(bf16[832,128]{1,0:T(8,128)(2,1)} %get-tuple-element.45), channel_id=1, source_target_pairs={{0,7},{1,6},{2,5},{3,4},{4,3},{5,2},{6,1},{7,0},{8,15},{9,14},{10,... | collective-permute-start | bytes 638984 | tf_op jit(solution)/shard_map/ppermute | solution.py:264
  23.2 9.8 %collective-permute-start.9 = (bf16[832,128]{1,0:T(8,128)(2,1)}, bf16[832,128]{1,0:T(8,128)(2,1)S(1)}, u32[]{:S(2)}, u32[]{:S(2)}) collective-permute-start(bf16[832,128]{1,0:T(8,128)(2,1)} %get-tuple-element.52), channel_id=1, source_target_pairs={{0,4},{1,5},{2,6},{3,7},{4,0},{5,1},{6,2},{7,3},{8,12},{9,13},{10,... | collective-permute-start | bytes 638984 | tf_op jit(solution)/shard_map/ppermute | solution.py:264
  23.2 11.5 %collective-permute-start.8 = (bf16[832,128]{1,0:T(8,128)(2,1)}, bf16[832,128]{1,0:T(8,128)(2,1)S(1)}, u32[]{:S(2)}, u32[]{:S(2)}) collective-permute-start(bf16[832,128]{1,0:T(8,128)(2,1)} %get-tuple-element.51), channel_id=1, source_target_pairs={{0,2},{1,3},{2,0},{3,1},{4,6},{5,7},{6,4},{7,5},{8,10},{9,11},{10,... | collective-permute-start | bytes 638984 | tf_op jit(solution)/shard_map/ppermute | solution.py:264
  23.4 0.9 %copy-start.7 = (bf16[832,128]{1,0:T(8,128)(2,1)S(1)}, bf16[832,128]{1,0:T(8,128)(2,1)}, u32[]{:S(2)}) copy-start(bf16[832,128]{1,0:T(8,128)(2,1)} %get-tuple-element.56) | copy-start | bytes 638980
  23.5 4.3 %copy-start.4 = (bf16[832,128]{1,0:T(8,128)(2,1)S(1)}, bf16[832,128]{1,0:T(8,128)(2,1)}, u32[]{:S(2)}) copy-start(bf16[832,128]{1,0:T(8,128)(2,1)} %get-tuple-element.42.refs_0_) | copy-start | bytes 638980
  23.7 12.1 %collective-permute-start.10 = (bf16[832,128]{1,0:T(8,128)(2,1)S(1)}, bf16[832,128]{1,0:T(8,128)(2,1)S(1)}, u32[]{:S(2)}, u32[]{:S(2)}) collective-permute-start(bf16[832,128]{1,0:T(8,128)(2,1)S(1)} %copy-done.8), channel_id=1, source_target_pairs={{0,3},{1,2},{2,1},{3,0},{4,7},{5,6},{6,5},{7,4},{8,11},{9,10},{10,... | collective-permute-start | bytes 638984 | tf_op jit(solution)/shard_map/ppermute | solution.py:264
  24.4 11.4 %collective-permute-start.11 = (bf16[832,128]{1,0:T(8,128)(2,1)S(1)}, bf16[832,128]{1,0:T(8,128)(2,1)S(1)}, u32[]{:S(2)}, u32[]{:S(2)}) collective-permute-start(bf16[832,128]{1,0:T(8,128)(2,1)S(1)} %copy-done.7), channel_id=1, source_target_pairs={{0,5},{1,4},{2,7},{3,6},{4,1},{5,0},{6,3},{7,2},{8,13},{9,12},{10,... | collective-permute-start | bytes 638984 | tf_op jit(solution)/shard_map/ppermute | solution.py:264
  32.9 10.3 %collective-permute-start.5 = (bf16[832,128]{1,0:T(8,128)(2,1)S(1)}, bf16[832,128]{1,0:T(8,128)(2,1)S(1)}, u32[]{:S(2)}, u32[]{:S(2)}) collective-permute-start(bf16[832,128]{1,0:T(8,128)(2,1)S(1)} %get-tuple-element.47), channel_id=1, source_target_pairs={{0,1},{1,0},{2,3},{3,2},{4,5},{5,4},{6,7},{7,6},{8,9},{9,8},{10,11... | collective-permute-start | bytes 638984 | tf_op jit(solution)/shard_map/ppermute | solution.py:264
  33.0 10.2 %collective-permute-start.6 = (bf16[832,128]{1,0:T(8,128)(2,1)S(1)}, bf16[832,128]{1,0:T(8,128)(2,1)S(1)}, u32[]{:S(2)}, u32[]{:S(2)}) collective-permute-start(bf16[832,128]{1,0:T(8,128)(2,1)S(1)} %get-tuple-element.48), channel_id=1, source_target_pairs={{0,6},{1,7},{2,4},{3,5},{4,2},{5,3},{6,0},{7,1},{8,14},{9,15},{10,... | collective-permute-start | bytes 638984 | tf_op jit(solution)/shard_map/ppermute | solution.py:264
  34.7 11.0 %collective-permute-start.7 = (bf16[832,128]{1,0:T(8,128)(2,1)S(1)}, bf16[832,128]{1,0:T(8,128)(2,1)S(1)}, u32[]{:S(2)}, u32[]{:S(2)}) collective-permute-start(bf16[832,128]{1,0:T(8,128)(2,1)S(1)} %get-tuple-element.49), channel_id=1, source_target_pairs={{0,7},{1,6},{2,5},{3,4},{4,3},{5,2},{6,1},{7,0},{8,15},{9,14},{10,... | collective-permute-start | bytes 638984 | tf_op jit(solution)/shard_map/ppermute | solution.py:264
  43.2 22.5 %copy-start = (bf16[32,8,8,128]{3,2,1,0:T(8,128)(2,1)S(1)}, bf16[32,8,8,128]{3,2,1,0:T(8,128)(2,1)}, u32[]{:S(2)}) copy-start(bf16[32,8,8,128]{3,2,1,0:T(8,128)(2,1)} %cot_ref.1) | copy-start | bytes 1572868
  43.2 22.5 %copy-start.1 = (bf16[256,256]{1,0:T(8,128)(2,1)S(1)}, bf16[256,256]{1,0:T(8,128)(2,1)}, u32[]{:S(2)}) copy-start(bf16[256,256]{1,0:T(8,128)(2,1)} %get-tuple-element.40.pick_ref) | copy-start | bytes 393220
  43.2 22.5 %copy-start.2 = (bf16[256,256]{1,0:T(8,128)(2,1)S(1)}, bf16[256,256]{1,0:T(8,128)(2,1)}, u32[]{:S(2)}) copy-start(bf16[256,256]{1,0:T(8,128)(2,1)} %get-tuple-element.41.cot_pick_ref) | copy-start | bytes 393220
  43.2 22.5 %copy-start.3 = (f32[32]{0:T(128)S(1)}, f32[32]{0:T(128)}, u32[]{:S(2)}) copy-start(f32[32]{0:T(128)} %param.8) | copy-start | bytes 388
  45.7 19.8 %collective-permute-start.16 = (bf16[18,128,128]{2,1,0:T(8,128)(2,1)S(1)}, bf16[18,128,128]{2,1,0:T(8,128)(2,1)S(1)}, u32[]{:S(2)}, u32[]{:S(2)}) collective-permute-start(bf16[18,128,128]{2,1,0:T(8,128)(2,1)S(1)} %get-tuple-element.72), channel_id=1, source_target_pairs={{1,9},{9,1},{3,11},{11,3},{5,13},{13,5},{7,15},{15,7},{17,25},{25,... | collective-permute-start | bytes 1769480 | tf_op jit(solution)/shard_map/ppermute | solution.py:342
  46.4 8.4 %collective-permute-start.12 = (bf16[832,128]{1,0:T(8,128)(2,1)S(1)}, bf16[832,128]{1,0:T(8,128)(2,1)S(1)}, u32[]{:S(2)}, u32[]{:S(2)}) collective-permute-start(bf16[832,128]{1,0:T(8,128)(2,1)S(1)} %get-tuple-element.62), channel_id=1, source_target_pairs={{0,4},{1,5},{2,6},{3,7},{4,0},{5,1},{6,2},{7,3},{8,12},{9,13},{10,... | collective-permute-start | bytes 638984 | tf_op jit(solution)/shard_map/ppermute | solution.py:264
  46.5 8.3 %collective-permute-start.13 = (bf16[832,128]{1,0:T(8,128)(2,1)S(1)}, bf16[832,128]{1,0:T(8,128)(2,1)S(1)}, u32[]{:S(2)}, u32[]{:S(2)}) collective-permute-start(bf16[832,128]{1,0:T(8,128)(2,1)S(1)} %get-tuple-element.64), channel_id=1, source_target_pairs={{0,2},{1,3},{2,0},{3,1},{4,6},{5,7},{6,4},{7,5},{8,10},{9,11},{10,... | collective-permute-start | bytes 638984 | tf_op jit(solution)/shard_map/ppermute | solution.py:264
  47.9 17.6 %collective-permute-start.14 = (bf16[832,128]{1,0:T(8,128)(2,1)S(1)}, bf16[832,128]{1,0:T(8,128)(2,1)S(1)}, u32[]{:S(2)}, u32[]{:S(2)}) collective-permute-start(bf16[832,128]{1,0:T(8,128)(2,1)S(1)} %get-tuple-element.66), channel_id=1, source_target_pairs={{0,5},{1,4},{2,7},{3,6},{4,1},{5,0},{6,3},{7,2},{8,13},{9,12},{10,... | collective-permute-start | bytes 638984 | tf_op jit(solution)/shard_map/ppermute | solution.py:264
  51.8 13.6 %collective-permute-start.15 = (bf16[832,128]{1,0:T(8,128)(2,1)S(1)}, bf16[832,128]{1,0:T(8,128)(2,1)S(1)}, u32[]{:S(2)}, u32[]{:S(2)}) collective-permute-start(bf16[832,128]{1,0:T(8,128)(2,1)S(1)} %get-tuple-element.68), channel_id=1, source_target_pairs={{0,3},{1,2},{2,1},{3,0},{4,7},{5,6},{6,5},{7,4},{8,11},{9,10},{10,... | collective-permute-start | bytes 638984 | tf_op jit(solution)/shard_map/ppermute | solution.py:264
  65.6 2.4 %collective-permute-start.17 = (bf16[18,128,128]{2,1,0:T(8,128)(2,1)S(1)}, bf16[18,128,128]{2,1,0:T(8,128)(2,1)S(1)}, u32[]{:S(2)}, u32[]{:S(2)}) collective-permute-start(bf16[18,128,128]{2,1,0:T(8,128)(2,1)S(1)} %broadcast_select_fusion), channel_id=1, source_target_pairs={{0,1},{1,0},{2,3},{3,2},{4,5},{5,4},{6,7},{7,6},{8,9},{9,8},{10,11... | collective-permute-start | bytes 1769480 | tf_op jit(solution)/shard_map/ppermute | solution.py:345

commit v6 on v5

--- a/solution.py
+++ b/solution.py
@@ -11,6 +11,7 @@
 SWAP = [(0, 3), (2, 1)]
 SWAP_HOME = [(1, 3), (3, 1)]
 TAPS = 3
+ROWS = 5
 BLOCK = 8
 PLACED = pl.BlockSpec(memory_space=pl.ANY)
 PACK_PARAMS = pltpu.CompilerParams(vmem_limit_bytes=56 * 1024 * 1024)
@@ -54,9 +55,9 @@
 
 
 def pack_kernel(slots, place, route_at, gate_at, tiles_at, cot_at, *refs):
-    route_ref, gate_ref, tiles_ref, cot_ref, sems = refs[-5:]
-    *out_refs, pick_ref, cot_pick_ref = refs[:-5]
-    peers = len(out_refs)
+    route_ref, gate_ref, tiles_ref, cot_ref, msg_ref, sems, out_sems = refs[-7:]
+    *outs_at, pick_ref, cot_pick_ref = refs[:-7]
+    peers = len(outs_at)
     step = BLOCK * slots
     pairs = ((route_at, route_ref), (gate_at, gate_ref), (tiles_at, tiles_ref), (cot_at, cot_ref))
     made = [pltpu.make_async_copy(a, b, sems.at[k]) for k, (a, b) in enumerate(pairs)]
@@ -75,17 +76,30 @@
     def put(at, values):
         values = values.astype(jnp.bfloat16)
         for peer in range(peers):
-            out_refs[peer][at : at + step, :] = values[peer * step : (peer + 1) * step, :]
+            msg_ref[peer, at : at + step, :] = values[peer * step : (peer + 1) * step, :]
+
+    def leave(part, start, count):
+        rows = pl.ds(start * step, count * step)
+        sent = [
+            pltpu.make_async_copy(msg_ref.at[peer, rows], outs_at[peer].at[rows], out_sems.at[part, peer])
+            for peer in range(peers)
+        ]
+        for copy in sent:
+            copy.start()
+        return sent
 
     made[2].wait()
     for block in range(blocks):
         put(block * step, dot(pick, tiles_ref[block]))
+    sent = leave(0, 0, blocks)
     made[3].wait()
     patches, rows, cols, channels = cot_ref.shape
     for i in range(rows):
         scaled = cot_ref[:, i, :, :].astype(jnp.float32) * gate
         scaled = scaled.reshape(patches * cols, channels).astype(jnp.bfloat16)
         put((blocks + i) * step, dot(cot_pick, scaled))
+    for copy in sent + leave(1, blocks, rows):
+        copy.wait()
 
 
 def unpack_kernel(slots, queue, pick_ref, cot_pick_ref, gate_ref, cot_ref, *refs):
@@ -138,6 +152,9 @@
     def gather(block):
         return jnp.concatenate([m[block * step : (block + 1) * step, :] for m in msgs], axis=0)
 
+    def groups(first, end):
+        return [range(i, min(i + ROWS, end)) for i in range(first, end, ROWS)]
+
     def window(ref, cols, row, col, count):
         at = (row * cols + col) * wide
         return ref[at : at + count * wide, :]
@@ -145,13 +162,17 @@
     mix = mix_matrix(peers, slots, False)
     for block in range(blocks):
         x_ref[block * size : (block + 1) * size, :] = dot(mix, gather(block)).astype(jnp.bfloat16)
-    for i in range(mid):
-        lhs = jnp.concatenate(
-            [window(x_ref, side, i + a, b, mid) for a in range(TAPS) for b in range(TAPS)], axis=1
-        )
-        pre = dot(lhs, one_ref[...])
+    def lined(ref, cols, rows, count):
+        taps = [(a, b) for a in range(TAPS) for b in range(TAPS)]
+        lines = [
+            jnp.concatenate([window(ref, cols, i + a, b, count) for a, b in taps], axis=1) for i in rows
+        ]
+        return jnp.concatenate(lines, axis=0)
+
+    for group in groups(0, mid):
+        pre = dot(lined(x_ref, side, group, mid), one_ref[...])
         sigma = jax.nn.sigmoid(pre)
-        rows = slice(i * mid * wide, (i + 1) * mid * wide)
+        rows = slice(group[0] * mid * wide, (group[-1] + 1) * mid * wide)
         h_ref[rows, :] = (pre * sigma).astype(jnp.bfloat16)
         slope_ref[rows, :] = sigma * (1.0 + pre * (1.0 - sigma))
 
@@ -162,11 +183,10 @@
         for peer in range(peers):
             backs[peer][block * step : (block + 1) * step, :] = values[peer * step : (peer + 1) * step, :]
 
-    for i in range(out):
-        lhs = jnp.concatenate(
-            [window(h_ref, mid, i + a, b, out) for a in range(TAPS) for b in range(TAPS)], axis=1
-        )
-        put(blocks + i, dot(lhs, two_ref[...]).astype(jnp.bfloat16))
+    for group in groups(0, out):
+        result = dot(lined(h_ref, mid, group, out), two_ref[...]).astype(jnp.bfloat16)
+        for k, i in enumerate(group):
+            put(blocks + i, result[k * size : (k + 1) * size, :])
 
     blank = jnp.zeros((2 * wide, x_ref.shape[1]), jnp.bfloat16)
     for i in range(out):
@@ -175,24 +195,32 @@
         g_ref[at + 2 * wide : at + 2 * wide + size, :] = dot(mix, gather(blocks + i)).astype(jnp.bfloat16)
         g_ref[at + 2 * wide + size : at + 4 * wide + size, :] = blank
 
-    def transposed(ref, kernel_ref, rows, i):
-        taps = [a for a in range(TAPS) if 0 <= i - a < rows]
-        lhs = jnp.concatenate(
-            [window(ref, rows + 4, i - a, 2 - b, rows + 2) for a in taps for b in range(TAPS)], axis=1
-        )
+    def transposed(ref, kernel_ref, rows, group):
+        taps = [a for a in range(TAPS) if 0 <= group[0] - a < rows]
+        lines = [
+            jnp.concatenate(
+                [window(ref, rows + 4, i - a, 2 - b, rows + 2) for a in taps for b in range(TAPS)], axis=1
+            )
+            for i in group
+        ]
         per = TAPS * x_ref.shape[1]
+        lhs = jnp.concatenate(lines, axis=0)
         return dot(lhs, kernel_ref[taps[0] * per : (taps[-1] + 1) * per, :])
 
-    for i in range(mid):
-        at = i * (mid + 4) * wide
-        grad_mid = transposed(g_ref, two_t_ref, out, i) * slope_ref[i * mid * wide : (i + 1) * mid * wide, :]
-        m_ref[at : at + 2 * wide, :] = blank
-        m_ref[at + 2 * wide : at + (mid + 2) * wide, :] = grad_mid.astype(jnp.bfloat16)
-        m_ref[at + (mid + 2) * wide : at + (mid + 4) * wide, :] = blank
-    for i in range(side):
-        t_ref[i * side * wide : (i + 1) * side * wide, :] = transposed(m_ref, one_t_ref, mid, i).astype(
-            jnp.bfloat16
-        )
+    def edged(rows):
+        return [range(i, i + 1) for i in (0, 1)] + groups(2, rows) + [range(i, i + 1) for i in (rows, rows + 1)]
+
+    for group in edged(out):
+        rows = slice(group[0] * mid * wide, (group[-1] + 1) * mid * wide)
+        grad_mid = (transposed(g_ref, two_t_ref, out, group) * slope_ref[rows, :]).astype(jnp.bfloat16)
+        for k, i in enumerate(group):
+            at = i * (mid + 4) * wide
+            m_ref[at : at + 2 * wide, :] = blank
+            m_ref[at + 2 * wide : at + (mid + 2) * wide, :] = grad_mid[k * mid * wide : (k + 1) * mid * wide, :]
+            m_ref[at + (mid + 2) * wide : at + (mid + 4) * wide, :] = blank
+    for group in edged(mid):
+        rows = slice(group[0] * side * wide, (group[-1] + 1) * side * wide)
+        t_ref[rows, :] = transposed(m_ref, one_t_ref, mid, group).astype(jnp.bfloat16)
     for block in range(blocks):
         put(block, t_ref[block * size : (block + 1) * size, :])
 
@@ -267,13 +295,16 @@
     *packed, pick, cot_pick = pl.pallas_call(
         functools.partial(pack_kernel, slots, place),
         in_specs=[PLACED] * 4,
+        out_specs=[PLACED] * peers + [pl.BlockSpec()] * 2,
         out_shape=[bf16((message, channels))] * peers + picks,
         scratch_shapes=[
             pltpu.VMEM((1, patches), jnp.int32),
             pltpu.VMEM((1, patches), jnp.float32),
             pltpu.VMEM(tiles_rows.shape, jnp.bfloat16),
             pltpu.VMEM(cotangent.shape, jnp.bfloat16),
+            pltpu.VMEM((peers, message, channels), jnp.bfloat16),
             pltpu.SemaphoreType.DMA((4,)),
+            pltpu.SemaphoreType.DMA((2, peers)),
         ],
         compiler_params=PACK_PARAMS,
         name="pack",

time: 69.4 us -> 68.2 us (0.983)
  waiting for transfers between devices: 24.6 us -> 21.7 us
  starting transfers between devices: 22.9 us -> 24.7 us
    ppermute x14, waiting for transfers between devices: 24.6 us -> 21.7 us  [exchange(): lax.ppermute(message, ('owner', 'replica'), [(i, i ^ mask) for i in range...]
    ppermute x14, starting transfers between devices: 15.4 us -> 17.1 us  [exchange(): lax.ppermute(message, ('owner', 'replica'), [(i, i ^ mask) for i in range...]
where the time goes in v6:
time: 68.2 us; the launch traced here: 68 us
  starting transfers between devices  24.7 us (36%)
  waiting for transfers between devices  21.7 us (32%)
  Pallas kernels  18.5 us (27%)
  local copies, waits for them, and re-layouts  1.92 us (3%)
  between operations  0.9 us (1%)
    ppermute x14, waiting for transfers between devices, exchange(): lax.ppermute(message, ('owner', 'replica'), [(i, i ^ mask) for i in range...  21.7 us
    ppermute x14, starting transfers between devices, exchange(): lax.ppermute(message, ('owner', 'replica'), [(i, i ^ mask) for i in range...  17.1 us
    pallas_call x2, Pallas kernels, expert(): pl.pallas_call(functools.partial(expert_kernel, part, slots, side, len(he...  12.1 us
    ppermute x2, starting transfers between devices, shards(): lax.ppermute(k[0], ('half', 'replica'), SWAP)  6.83 us
    pallas_call x1, Pallas kernels, shards(): pl.pallas_call(functools.partial(pack_kernel, slots, place), in_specs=[PL...  4.17 us
    pallas_call x1, Pallas kernels, shards(): pl.pallas_call(functools.partial(unpack_kernel, slots, [*chunks[0], *near...  2.26 us
  transfers between devices with their start and end apart: 18, of which 4 were waited for; matrix products, arithmetic and copies ran while one was open for 1% of the time, Pallas kernels for 27%

profile of v6, /device:TPU:0, one launch (start us, length us, event | category | flops | bytes accessed | tf_op | source)
XLA Modules:
  0.0 68.0 jit_solution(13178231168586519884)
XLA Ops:
  0.7 5.5 %collective-permute-start.3 = (bf16[3,3,128,128]{3,2,1,0:T(8,128)(2,1)}, bf16[3,3,128,128]{3,2,1,0:T(8,128)(2,1)S(1)}, u32[]{:S(2)}, u32[]{:S(2)}) collective-permute-start(bf16[3,3,128,128]{3,2,1,0:T(8,128)(2,1)} %bitcast.36), channel_id=1, source_target_pairs={{0,9},{8,1},{2,11},{10,3},{4,13},{12,5},{6,15},{14,7},{16,25},{24,... | collective-permute-start | bytes 884744 | tf_op jit(solution)/shard_map/ppermute | solution.py:274
  6.2 4.2 %pack.1 = (bf16[832,128]{1,0:T(8,128)(2,1)}, bf16[832,128]{1,0:T(8,128)(2,1)}, bf16[832,128]{1,0:T(8,128)(2,1)}, bf16[832,128]{1,0:T(8,128)(2,1)}, bf16[832,128]...) custom-call(s32[1,32]{1,0:T(1,128)} %bitcast.38, ...), custom_call_target="tpu_custom_call" | custom-call | tf_op jit(solution)/shard_map/pack/pallas_call | solution.py:295
  10.4 0.0 copy-start.8
  10.4 2.6 %collective-permute-start.1 = (bf16[832,128]{1,0:T(8,128)(2,1)}, bf16[832,128]{1,0:T(8,128)(2,1)S(1)}, u32[]{:S(2)}, u32[]{:S(2)}) collective-permute-start(bf16[832,128]{1,0:T(8,128)(2,1)} %get-tuple-element.44), channel_id=1, source_target_pairs={{0,6},{1,7},{2,4},{3,5},{4,2},{5,3},{6,0},{7,1},{8,14},{9,15},{10,... | collective-permute-start | bytes 638984 | tf_op jit(solution)/shard_map/ppermute | solution.py:292
  13.0 1.3 %collective-permute-start.4 = (bf16[3,3,128,128]{3,2,1,0:T(8,128)(2,1)S(1)}, bf16[3,3,128,128]{3,2,1,0:T(8,128)(2,1)S(1)}, u32[]{:S(2)}, u32[]{:S(2)}) collective-permute-start(bf16[3,3,128,128]{3,2,1,0:T(8,128)(2,1)S(1)} %bitcast.37), channel_id=1, source_target_pairs={{0,9},{8,1},{2,11},{10,3},{4,13},{12,5},{6,15},{14,7},{16,25},{24,... | collective-permute-start | bytes 884744 | tf_op jit(solution)/shard_map/ppermute | solution.py:274
  14.3 0.1 collective-permute-start
  14.4 0.5 collective-permute-start.2
  14.9 7.4 %collective-permute-done.1.refs_2_ = bf16[832,128]{1,0:T(8,128)(2,1)S(1)} collective-permute-done((bf16[832,128]{1,0:T(8,128)(2,1)}, bf16[832,128]{1,0:T(8,128)(2,1)S(1)}, u32[]{:S(2)}, u32[]{:S(2)}) %collective-permute-start.1) | collective-permute-done | bytes 213024 | tf_op jit(solution)/shard_map/ppermute | solution.py:292
  22.3 0.0 collective-permute-start.9
  22.3 0.0 collective-permute-done.3
  22.3 1.4 %collective-permute-start.8 = (bf16[832,128]{1,0:T(8,128)(2,1)}, bf16[832,128]{1,0:T(8,128)(2,1)S(1)}, u32[]{:S(2)}, u32[]{:S(2)}) collective-permute-start(bf16[832,128]{1,0:T(8,128)(2,1)} %get-tuple-element.51), channel_id=1, source_target_pairs={{0,2},{1,3},{2,0},{3,1},{4,6},{5,7},{6,4},{7,5},{8,10},{9,11},{10,... | collective-permute-start | bytes 638984 | tf_op jit(solution)/shard_map/ppermute | solution.py:292
  23.7 0.0 copy-start.4
  23.7 0.2 copy.11
  23.9 0.0 collective-permute-done.4
  23.9 0.1 collective-permute-start.10
  24.1 0.2 copy.12
  24.3 0.0 collective-permute-done.refs_1_
  24.3 0.3 copy-done.7
  24.6 2.1 %collective-permute-start.11 = (bf16[832,128]{1,0:T(8,128)(2,1)S(1)}, bf16[832,128]{1,0:T(8,128)(2,1)S(1)}, u32[]{:S(2)}, u32[]{:S(2)}) collective-permute-start(bf16[832,128]{1,0:T(8,128)(2,1)S(1)} %copy-done.7), channel_id=1, source_target_pairs={{0,5},{1,4},{2,7},{3,6},{4,1},{5,0},{6,3},{7,2},{8,13},{9,12},{10,... | collective-permute-start | bytes 638984 | tf_op jit(solution)/shard_map/ppermute | solution.py:292
  26.8 0.0 collective-permute-done.2.refs_3_
  26.8 5.0 %expert.2 = (bf16[832,128]{1,0:T(8,128)(2,1)S(1)}, bf16[832,128]{1,0:T(8,128)(2,1)S(1)}, bf16[832,128]{1,0:T(8,128)(2,1)S(1)}, bf16[832,128]{1,0:T(8,128)(2,1)S(...) custom-call(bf16[832,128]{1,0:T(8,128)(2,1)S(1)} %copy-done.4, ...), custom_call_target="tpu_custom_call" | custom-call | flops 15401484288 | bytes 30802968 | tf_op jit(solution)/shard_map/expert/pallas_call | solution.py:350
  31.8 0.1 collective-permute-start.5
  31.9 0.0 collective-permute-done.9.refs_1_
  31.9 3.1 %collective-permute-start.6 = (bf16[832,128]{1,0:T(8,128)(2,1)S(1)}, bf16[832,128]{1,0:T(8,128)(2,1)S(1)}, u32[]{:S(2)}, u32[]{:S(2)}) collective-permute-start(bf16[832,128]{1,0:T(8,128)(2,1)S(1)} %get-tuple-element.48), channel_id=1, source_target_pairs={{0,6},{1,7},{2,4},{3,5},{4,2},{5,3},{6,0},{7,1},{8,14},{9,15},{10,... | collective-permute-start | bytes 638984 | tf_op jit(solution)/shard_map/ppermute | solution.py:292
  35.0 0.0 collective-permute-done.8.refs_0_
  35.0 0.0 collective-permute-start.7
  35.0 0.0 collective-permute-done.10.refs_2_
  35.0 7.0 %expert.3 = (bf16[832,128]{1,0:T(8,128)(2,1)S(1)}, bf16[832,128]{1,0:T(8,128)(2,1)S(1)}, bf16[832,128]{1,0:T(8,128)(2,1)S(1)}, bf16[832,128]{1,0:T(8,128)(2,1)S(1)}, bf16[18,128,128]{2,1,0:T(8,128)(2,1)S(1)}) custom-call(bf16[832,128]{1,0:T(8,128)(2,1)S(1)} %collective-permute-done.8.refs_0_, bf16[832,128]{1,0:T(8,128)(2,1)S(1)} %collective-permute-done.9.refs_1_, ...), custom_call_target="tpu_custom_call" | custom-call | flops 15401484288 | bytes 30802968 | tf_op jit(solution)/shard_map/expert/pallas_call | solution.py:350
  42.0 0.0 copy-start
  42.1 0.0 copy-start.3
  42.1 0.0 collective-permute-done.5.refs_1_
  42.1 0.0 collective-permute-done.6.refs_2_
  42.1 2.4 %collective-permute-done.7.refs_3_ = bf16[832,128]{1,0:T(8,128)(2,1)S(1)} collective-permute-done((bf16[832,128]{1,0:T(8,128)(2,1)S(1)}, bf16[832,128]{1,0:T(8,128)(2,1)S(1)}, u32[]{:S(2)}, u32[]{:S(2)}) %collective-permute-start.7) | collective-permute-done | bytes 213024 | tf_op jit(solution)/shard_map/ppermute | solution.py:292
  44.5 0.7 %collective-permute-start.16 = (bf16[18,128,128]{2,1,0:T(8,128)(2,1)S(1)}, bf16[18,128,128]{2,1,0:T(8,128)(2,1)S(1)}, u32[]{:S(2)}, u32[]{:S(2)}) collective-permute-start(bf16[18,128,128]{2,1,0:T(8,128)(2,1)S(1)} %get-tuple-element.72), channel_id=1, source_target_pairs={{1,9},{9,1},{3,11},{11,3},{5,13},{13,5},{7,15},{15,7},{17,25},{25,... | collective-permute-start | bytes 1769480 | tf_op jit(solution)/shard_map/ppermute | solution.py:373
  45.2 1.4 %collective-permute-start.12 = (bf16[832,128]{1,0:T(8,128)(2,1)S(1)}, bf16[832,128]{1,0:T(8,128)(2,1)S(1)}, u32[]{:S(2)}, u32[]{:S(2)}) collective-permute-start(bf16[832,128]{1,0:T(8,128)(2,1)S(1)} %get-tuple-element.62), channel_id=1, source_target_pairs={{0,4},{1,5},{2,6},{3,7},{4,0},{5,1},{6,2},{7,3},{8,12},{9,13},{10,... | collective-permute-start | bytes 638984 | tf_op jit(solution)/shard_map/ppermute | solution.py:292
  46.6 1.5 %collective-permute-start.13 = (bf16[832,128]{1,0:T(8,128)(2,1)S(1)}, bf16[832,128]{1,0:T(8,128)(2,1)S(1)}, u32[]{:S(2)}, u32[]{:S(2)}) collective-permute-start(bf16[832,128]{1,0:T(8,128)(2,1)S(1)} %get-tuple-element.64), channel_id=1, source_target_pairs={{0,2},{1,3},{2,0},{3,1},{4,6},{5,7},{6,4},{7,5},{8,10},{9,11},{10,... | collective-permute-start | bytes 638984 | tf_op jit(solution)/shard_map/ppermute | solution.py:292
  48.1 3.4 %collective-permute-start.14 = (bf16[832,128]{1,0:T(8,128)(2,1)S(1)}, bf16[832,128]{1,0:T(8,128)(2,1)S(1)}, u32[]{:S(2)}, u32[]{:S(2)}) collective-permute-start(bf16[832,128]{1,0:T(8,128)(2,1)S(1)} %get-tuple-element.66), channel_id=1, source_target_pairs={{0,5},{1,4},{2,7},{3,6},{4,1},{5,0},{6,3},{7,2},{8,13},{9,12},{10,... | collective-permute-start | bytes 638984 | tf_op jit(solution)/shard_map/ppermute | solution.py:292
  51.5 0.9 %collective-permute-start.15 = (bf16[832,128]{1,0:T(8,128)(2,1)S(1)}, bf16[832,128]{1,0:T(8,128)(2,1)S(1)}, u32[]{:S(2)}, u32[]{:S(2)}) collective-permute-start(bf16[832,128]{1,0:T(8,128)(2,1)S(1)} %get-tuple-element.68), channel_id=1, source_target_pairs={{0,3},{1,2},{2,1},{3,0},{4,7},{5,6},{6,5},{7,4},{8,11},{9,10},{10,... | collective-permute-start | bytes 638984 | tf_op jit(solution)/shard_map/ppermute | solution.py:292
  52.4 1.7 %collective-permute-done.12.refs_4_ = bf16[832,128]{1,0:T(8,128)(2,1)S(1)} collective-permute-done((bf16[832,128]{1,0:T(8,128)(2,1)S(1)}, bf16[832,128]{1,0:T(8,128)(2,1)S(1)}, u32[]{:S(2)}, u32[]{:S(2)}) %collective-permute-start.12) | collective-permute-done | bytes 213024 | tf_op jit(solution)/shard_map/ppermute | solution.py:292
  54.1 0.0 collective-permute-done.13.refs_5_
  54.1 10.2 %collective-permute-done.14.refs_6_ = bf16[832,128]{1,0:T(8,128)(2,1)S(1)} collective-permute-done((bf16[832,128]{1,0:T(8,128)(2,1)S(1)}, bf16[832,128]{1,0:T(8,128)(2,1)S(1)}, u32[]{:S(2)}, u32[]{:S(2)}) %collective-permute-start.14) | collective-permute-done | bytes 213024 | tf_op jit(solution)/shard_map/ppermute | solution.py:292
  64.3 0.0 collective-permute-done.15.refs_7_
  64.3 0.0 collective-permute-done.16
  64.3 0.1 broadcast_select_fusion
  64.4 0.1 collective-permute-start.17
  64.5 2.3 %unpack.1 = (bf16[32,8,8,128]{3,2,1,0:T(8,128)(2,1)}, bf16[18,256,128]{2,1,0:T(8,128)(2,1)}, f32[1,32]{1,0:T(1,128)}) custom-call(bf16[256,256]{1,0:T(8,128)(2,1)S(1)} %copy-done.1, bf16[256,256]{1,0:T(8,128)(2,1)S(1)} %copy-done.2, f32[1,32]{1,0:T(1,128)S(1)} %bitcast.32, bf16[32,8,8,128]{3,2,1,0:T(8,128)(2,1)S(1)} %copy-done, ...), custom_call_target="tpu_custom_call" | custom-call | tf_op jit(solution)/shard_map/unpack/pallas_call | solution.py:379
  66.7 0.1 convert_add_fusion
  66.9 1.1 %fusion = (f32[9,128,128]{2,1,0:T(8,128)}, f32[9,128,128]{2,1,0:T(8,128)}) fusion(f32[18,128,128]{2,1,0:T(8,128)S(1)} %convert_add_fusion), kind=kLoop, calls=%fused_computation.4 | loop fusion | bytes 2359296 | tf_op jit(solution)/shard_map/unstack | solution.py:378
  (17 shorter events, 0.1 us)
Async XLA Ops:
  0.6 23.0 %copy-start.5 = (bf16[1,3,3,128,128]{4,3,2,1,0:T(8,128)(2,1)S(1)}, bf16[1,3,3,128,128]{4,3,2,1,0:T(8,128)(2,1)}, u32[]{:S(2)}) copy-start(bf16[1,3,3,128,128]{4,3,2,1,0:T(8,128)(2,1)} %param.9) | copy-start | bytes 884740
  0.6 12.3 %copy-start.6 = (bf16[1,3,3,128,128]{4,3,2,1,0:T(8,128)(2,1)S(1)}, bf16[1,3,3,128,128]{4,3,2,1,0:T(8,128)(2,1)}, u32[]{:S(2)}) copy-start(bf16[1,3,3,128,128]{4,3,2,1,0:T(8,128)(2,1)} %param.10) | copy-start | bytes 884740
  0.7 21.6 %collective-permute-start.3 = (bf16[3,3,128,128]{3,2,1,0:T(8,128)(2,1)}, bf16[3,3,128,128]{3,2,1,0:T(8,128)(2,1)S(1)}, u32[]{:S(2)}, u32[]{:S(2)}) collective-permute-start(bf16[3,3,128,128]{3,2,1,0:T(8,128)(2,1)} %bitcast.36), channel_id=1, source_target_pairs={{0,9},{8,1},{2,11},{10,3},{4,13},{12,5},{6,15},{14,7},{16,25},{24,... | collective-permute-start | bytes 884744 | tf_op jit(solution)/shard_map/ppermute | solution.py:274
  10.4 13.6 %copy-start.8 = (bf16[832,128]{1,0:T(8,128)(2,1)S(1)}, bf16[832,128]{1,0:T(8,128)(2,1)}, u32[]{:S(2)}) copy-start(bf16[832,128]{1,0:T(8,128)(2,1)} %get-tuple-element.54) | copy-start | bytes 638980
  10.4 11.9 %collective-permute-start.1 = (bf16[832,128]{1,0:T(8,128)(2,1)}, bf16[832,128]{1,0:T(8,128)(2,1)S(1)}, u32[]{:S(2)}, u32[]{:S(2)}) collective-permute-start(bf16[832,128]{1,0:T(8,128)(2,1)} %get-tuple-element.44), channel_id=1, source_target_pairs={{0,6},{1,7},{2,4},{3,5},{4,2},{5,3},{6,0},{7,1},{8,14},{9,15},{10,... | collective-permute-start | bytes 638984 | tf_op jit(solution)/shard_map/ppermute | solution.py:292
  13.0 10.9 %collective-permute-start.4 = (bf16[3,3,128,128]{3,2,1,0:T(8,128)(2,1)S(1)}, bf16[3,3,128,128]{3,2,1,0:T(8,128)(2,1)S(1)}, u32[]{:S(2)}, u32[]{:S(2)}) collective-permute-start(bf16[3,3,128,128]{3,2,1,0:T(8,128)(2,1)S(1)} %bitcast.37), channel_id=1, source_target_pairs={{0,9},{8,1},{2,11},{10,3},{4,13},{12,5},{6,15},{14,7},{16,25},{24,... | collective-permute-start | bytes 884744 | tf_op jit(solution)/shard_map/ppermute | solution.py:274
  14.3 10.0 %collective-permute-start = (bf16[832,128]{1,0:T(8,128)(2,1)}, bf16[832,128]{1,0:T(8,128)(2,1)S(1)}, u32[]{:S(2)}, u32[]{:S(2)}) collective-permute-start(bf16[832,128]{1,0:T(8,128)(2,1)} %get-tuple-element.43), channel_id=1, source_target_pairs={{0,1},{1,0},{2,3},{3,2},{4,5},{5,4},{6,7},{7,6},{8,9},{9,8},{10,11... | collective-permute-start | bytes 638984 | tf_op jit(solution)/shard_map/ppermute | solution.py:292
  14.4 12.4 %collective-permute-start.2 = (bf16[832,128]{1,0:T(8,128)(2,1)}, bf16[832,128]{1,0:T(8,128)(2,1)S(1)}, u32[]{:S(2)}, u32[]{:S(2)}) collective-permute-start(bf16[832,128]{1,0:T(8,128)(2,1)} %get-tuple-element.45), channel_id=1, source_target_pairs={{0,7},{1,6},{2,5},{3,4},{4,3},{5,2},{6,1},{7,0},{8,15},{9,14},{10,... | collective-permute-start | bytes 638984 | tf_op jit(solution)/shard_map/ppermute | solution.py:292
  22.3 9.6 %collective-permute-start.9 = (bf16[832,128]{1,0:T(8,128)(2,1)}, bf16[832,128]{1,0:T(8,128)(2,1)S(1)}, u32[]{:S(2)}, u32[]{:S(2)}) collective-permute-start(bf16[832,128]{1,0:T(8,128)(2,1)} %get-tuple-element.52), channel_id=1, source_target_pairs={{0,4},{1,5},{2,6},{3,7},{4,0},{5,1},{6,2},{7,3},{8,12},{9,13},{10,... | collective-permute-start | bytes 638984 | tf_op jit(solution)/shard_map/ppermute | solution.py:292
  22.3 12.7 %collective-permute-start.8 = (bf16[832,128]{1,0:T(8,128)(2,1)}, bf16[832,128]{1,0:T(8,128)(2,1)S(1)}, u32[]{:S(2)}, u32[]{:S(2)}) collective-permute-start(bf16[832,128]{1,0:T(8,128)(2,1)} %get-tuple-element.51), channel_id=1, source_target_pairs={{0,2},{1,3},{2,0},{3,1},{4,6},{5,7},{6,4},{7,5},{8,10},{9,11},{10,... | collective-permute-start | bytes 638984 | tf_op jit(solution)/shard_map/ppermute | solution.py:292
  23.7 0.9 %copy-start.7 = (bf16[832,128]{1,0:T(8,128)(2,1)S(1)}, bf16[832,128]{1,0:T(8,128)(2,1)}, u32[]{:S(2)}) copy-start(bf16[832,128]{1,0:T(8,128)(2,1)} %get-tuple-element.56) | copy-start | bytes 638980
  23.7 3.1 %copy-start.4 = (bf16[832,128]{1,0:T(8,128)(2,1)S(1)}, bf16[832,128]{1,0:T(8,128)(2,1)}, u32[]{:S(2)}) copy-start(bf16[832,128]{1,0:T(8,128)(2,1)} %get-tuple-element.42.refs_0_) | copy-start | bytes 638980
  23.9 11.0 %collective-permute-start.10 = (bf16[832,128]{1,0:T(8,128)(2,1)S(1)}, bf16[832,128]{1,0:T(8,128)(2,1)S(1)}, u32[]{:S(2)}, u32[]{:S(2)}) collective-permute-start(bf16[832,128]{1,0:T(8,128)(2,1)S(1)} %copy-done.8), channel_id=1, source_target_pairs={{0,3},{1,2},{2,1},{3,0},{4,7},{5,6},{6,5},{7,4},{8,11},{9,10},{10,... | collective-permute-start | bytes 638984 | tf_op jit(solution)/shard_map/ppermute | solution.py:292
  24.6 10.4 %collective-permute-start.11 = (bf16[832,128]{1,0:T(8,128)(2,1)S(1)}, bf16[832,128]{1,0:T(8,128)(2,1)S(1)}, u32[]{:S(2)}, u32[]{:S(2)}) collective-permute-start(bf16[832,128]{1,0:T(8,128)(2,1)S(1)} %copy-done.7), channel_id=1, source_target_pairs={{0,5},{1,4},{2,7},{3,6},{4,1},{5,0},{6,3},{7,2},{8,13},{9,12},{10,... | collective-permute-start | bytes 638984 | tf_op jit(solution)/shard_map/ppermute | solution.py:292
  31.8 10.3 %collective-permute-start.5 = (bf16[832,128]{1,0:T(8,128)(2,1)S(1)}, bf16[832,128]{1,0:T(8,128)(2,1)S(1)}, u32[]{:S(2)}, u32[]{:S(2)}) collective-permute-start(bf16[832,128]{1,0:T(8,128)(2,1)S(1)} %get-tuple-element.47), channel_id=1, source_target_pairs={{0,1},{1,0},{2,3},{3,2},{4,5},{5,4},{6,7},{7,6},{8,9},{9,8},{10,11... | collective-permute-start | bytes 638984 | tf_op jit(solution)/shard_map/ppermute | solution.py:292
  31.9 10.2 %collective-permute-start.6 = (bf16[832,128]{1,0:T(8,128)(2,1)S(1)}, bf16[832,128]{1,0:T(8,128)(2,1)S(1)}, u32[]{:S(2)}, u32[]{:S(2)}) collective-permute-start(bf16[832,128]{1,0:T(8,128)(2,1)S(1)} %get-tuple-element.48), channel_id=1, source_target_pairs={{0,6},{1,7},{2,4},{3,5},{4,2},{5,3},{6,0},{7,1},{8,14},{9,15},{10,... | collective-permute-start | bytes 638984 | tf_op jit(solution)/shard_map/ppermute | solution.py:292
  35.0 9.5 %collective-permute-start.7 = (bf16[832,128]{1,0:T(8,128)(2,1)S(1)}, bf16[832,128]{1,0:T(8,128)(2,1)S(1)}, u32[]{:S(2)}, u32[]{:S(2)}) collective-permute-start(bf16[832,128]{1,0:T(8,128)(2,1)S(1)} %get-tuple-element.49), channel_id=1, source_target_pairs={{0,7},{1,6},{2,5},{3,4},{4,3},{5,2},{6,1},{7,0},{8,15},{9,14},{10,... | collective-permute-start | bytes 638984 | tf_op jit(solution)/shard_map/ppermute | solution.py:292
  42.0 22.4 %copy-start = (bf16[32,8,8,128]{3,2,1,0:T(8,128)(2,1)S(1)}, bf16[32,8,8,128]{3,2,1,0:T(8,128)(2,1)}, u32[]{:S(2)}) copy-start(bf16[32,8,8,128]{3,2,1,0:T(8,128)(2,1)} %cot_ref.1) | copy-start | bytes 1572868
  42.0 22.4 %copy-start.1 = (bf16[256,256]{1,0:T(8,128)(2,1)S(1)}, bf16[256,256]{1,0:T(8,128)(2,1)}, u32[]{:S(2)}) copy-start(bf16[256,256]{1,0:T(8,128)(2,1)} %get-tuple-element.40.pick_ref) | copy-start | bytes 393220
  42.1 22.4 %copy-start.2 = (bf16[256,256]{1,0:T(8,128)(2,1)S(1)}, bf16[256,256]{1,0:T(8,128)(2,1)}, u32[]{:S(2)}) copy-start(bf16[256,256]{1,0:T(8,128)(2,1)} %get-tuple-element.41.cot_pick_ref) | copy-start | bytes 393220
  42.1 22.4 %copy-start.3 = (f32[32]{0:T(128)S(1)}, f32[32]{0:T(128)}, u32[]{:S(2)}) copy-start(f32[32]{0:T(128)} %param.8) | copy-start | bytes 388
  44.5 19.8 %collective-permute-start.16 = (bf16[18,128,128]{2,1,0:T(8,128)(2,1)S(1)}, bf16[18,128,128]{2,1,0:T(8,128)(2,1)S(1)}, u32[]{:S(2)}, u32[]{:S(2)}) collective-permute-start(bf16[18,128,128]{2,1,0:T(8,128)(2,1)S(1)} %get-tuple-element.72), channel_id=1, source_target_pairs={{1,9},{9,1},{3,11},{11,3},{5,13},{13,5},{7,15},{15,7},{17,25},{25,... | collective-permute-start | bytes 1769480 | tf_op jit(solution)/shard_map/ppermute | solution.py:373
  45.2 8.9 %collective-permute-start.12 = (bf16[832,128]{1,0:T(8,128)(2,1)S(1)}, bf16[832,128]{1,0:T(8,128)(2,1)S(1)}, u32[]{:S(2)}, u32[]{:S(2)}) collective-permute-start(bf16[832,128]{1,0:T(8,128)(2,1)S(1)} %get-tuple-element.62), channel_id=1, source_target_pairs={{0,4},{1,5},{2,6},{3,7},{4,0},{5,1},{6,2},{7,3},{8,12},{9,13},{10,... | collective-permute-start | bytes 638984 | tf_op jit(solution)/shard_map/ppermute | solution.py:292
  46.6 7.5 %collective-permute-start.13 = (bf16[832,128]{1,0:T(8,128)(2,1)S(1)}, bf16[832,128]{1,0:T(8,128)(2,1)S(1)}, u32[]{:S(2)}, u32[]{:S(2)}) collective-permute-start(bf16[832,128]{1,0:T(8,128)(2,1)S(1)} %get-tuple-element.64), channel_id=1, source_target_pairs={{0,2},{1,3},{2,0},{3,1},{4,6},{5,7},{6,4},{7,5},{8,10},{9,11},{10,... | collective-permute-start | bytes 638984 | tf_op jit(solution)/shard_map/ppermute | solution.py:292
  48.1 16.1 %collective-permute-start.14 = (bf16[832,128]{1,0:T(8,128)(2,1)S(1)}, bf16[832,128]{1,0:T(8,128)(2,1)S(1)}, u32[]{:S(2)}, u32[]{:S(2)}) collective-permute-start(bf16[832,128]{1,0:T(8,128)(2,1)S(1)} %get-tuple-element.66), channel_id=1, source_target_pairs={{0,5},{1,4},{2,7},{3,6},{4,1},{5,0},{6,3},{7,2},{8,13},{9,12},{10,... | collective-permute-start | bytes 638984 | tf_op jit(solution)/shard_map/ppermute | solution.py:292
  51.5 12.7 %collective-permute-start.15 = (bf16[832,128]{1,0:T(8,128)(2,1)S(1)}, bf16[832,128]{1,0:T(8,128)(2,1)S(1)}, u32[]{:S(2)}, u32[]{:S(2)}) collective-permute-start(bf16[832,128]{1,0:T(8,128)(2,1)S(1)} %get-tuple-element.68), channel_id=1, source_target_pairs={{0,3},{1,2},{2,1},{3,0},{4,7},{5,6},{6,5},{7,4},{8,11},{9,10},{10,... | collective-permute-start | bytes 638984 | tf_op jit(solution)/shard_map/ppermute | solution.py:292
  64.4 2.4 %collective-permute-start.17 = (bf16[18,128,128]{2,1,0:T(8,128)(2,1)S(1)}, bf16[18,128,128]{2,1,0:T(8,128)(2,1)S(1)}, u32[]{:S(2)}, u32[]{:S(2)}) collective-permute-start(bf16[18,128,128]{2,1,0:T(8,128)(2,1)S(1)} %broadcast_select_fusion), channel_id=1, source_target_pairs={{0,1},{1,0},{2,3},{3,2},{4,5},{5,4},{6,7},{7,6},{8,9},{9,8},{10,11... | collective-permute-start | bytes 1769480 | tf_op jit(solution)/shard_map/ppermute | solution.py:376

commit v7 on v6

--- a/solution.py
+++ b/solution.py
@@ -11,7 +11,7 @@
 SWAP = [(0, 3), (2, 1)]
 SWAP_HOME = [(1, 3), (3, 1)]
 TAPS = 3
-ROWS = 5
+ROWS = 4
 BLOCK = 8
 PLACED = pl.BlockSpec(memory_space=pl.ANY)
 PACK_PARAMS = pltpu.CompilerParams(vmem_limit_bytes=56 * 1024 * 1024)

time: 68.2 us -> 68.1 us (level)
  no operation moved by 1% of the time
where the time goes in v7:
time: 68.1 us; the launch traced here: 67.9 us
  starting transfers between devices  24.7 us (36%)
  waiting for transfers between devices  21.8 us (32%)
  Pallas kernels  18.3 us (27%)
  local copies, waits for them, and re-layouts  1.92 us (3%)
  between operations  0.9 us (1%)
    ppermute x14, waiting for transfers between devices, exchange(): lax.ppermute(message, ('owner', 'replica'), [(i, i ^ mask) for i in range...  21.8 us
    ppermute x14, starting transfers between devices, exchange(): lax.ppermute(message, ('owner', 'replica'), [(i, i ^ mask) for i in range...  17.1 us
    pallas_call x2, Pallas kernels, expert(): pl.pallas_call(functools.partial(expert_kernel, part, slots, side, len(he...  11.8 us
    ppermute x2, starting transfers between devices, shards(): lax.ppermute(k[0], ('half', 'replica'), SWAP)  6.83 us
    pallas_call x1, Pallas kernels, shards(): pl.pallas_call(functools.partial(pack_kernel, slots, place), in_specs=[PL...  4.17 us
    pallas_call x1, Pallas kernels, shards(): pl.pallas_call(functools.partial(unpack_kernel, slots, [*chunks[0], *near...  2.26 us
  transfers between devices with their start and end apart: 18, of which 4 were waited for; matrix products, arithmetic and copies ran while one was open for 1% of the time, Pallas kernels for 27%

profile of v7, /device:TPU:0, one launch (start us, length us, event | category | flops | bytes accessed | tf_op | source)
XLA Modules:
  0.0 67.9 jit_solution(13124349579814320574)
XLA Ops:
  0.7 5.5 %collective-permute-start.3 = (bf16[3,3,128,128]{3,2,1,0:T(8,128)(2,1)}, bf16[3,3,128,128]{3,2,1,0:T(8,128)(2,1)S(1)}, u32[]{:S(2)}, u32[]{:S(2)}) collective-permute-start(bf16[3,3,128,128]{3,2,1,0:T(8,128)(2,1)} %bitcast.36), channel_id=1, source_target_pairs={{0,9},{8,1},{2,11},{10,3},{4,13},{12,5},{6,15},{14,7},{16,25},{24,... | collective-permute-start | bytes 884744 | tf_op jit(solution)/shard_map/ppermute | solution.py:274
  6.2 4.2 %pack.1 = (bf16[832,128]{1,0:T(8,128)(2,1)}, bf16[832,128]{1,0:T(8,128)(2,1)}, bf16[832,128]{1,0:T(8,128)(2,1)}, bf16[832,128]{1,0:T(8,128)(2,1)}, bf16[832,128]...) custom-call(s32[1,32]{1,0:T(1,128)} %bitcast.38, ...), custom_call_target="tpu_custom_call" | custom-call | tf_op jit(solution)/shard_map/pack/pallas_call | solution.py:295
  10.4 0.0 copy-start.8
  10.4 2.6 %collective-permute-start.1 = (bf16[832,128]{1,0:T(8,128)(2,1)}, bf16[832,128]{1,0:T(8,128)(2,1)S(1)}, u32[]{:S(2)}, u32[]{:S(2)}) collective-permute-start(bf16[832,128]{1,0:T(8,128)(2,1)} %get-tuple-element.44), channel_id=1, source_target_pairs={{0,6},{1,7},{2,4},{3,5},{4,2},{5,3},{6,0},{7,1},{8,14},{9,15},{10,... | collective-permute-start | bytes 638984 | tf_op jit(solution)/shard_map/ppermute | solution.py:292
  13.0 1.3 %collective-permute-start.4 = (bf16[3,3,128,128]{3,2,1,0:T(8,128)(2,1)S(1)}, bf16[3,3,128,128]{3,2,1,0:T(8,128)(2,1)S(1)}, u32[]{:S(2)}, u32[]{:S(2)}) collective-permute-start(bf16[3,3,128,128]{3,2,1,0:T(8,128)(2,1)S(1)} %bitcast.37), channel_id=1, source_target_pairs={{0,9},{8,1},{2,11},{10,3},{4,13},{12,5},{6,15},{14,7},{16,25},{24,... | collective-permute-start | bytes 884744 | tf_op jit(solution)/shard_map/ppermute | solution.py:274
  14.3 0.1 collective-permute-start
  14.4 0.5 collective-permute-start.2
  14.9 7.4 %collective-permute-done.1.refs_2_ = bf16[832,128]{1,0:T(8,128)(2,1)S(1)} collective-permute-done((bf16[832,128]{1,0:T(8,128)(2,1)}, bf16[832,128]{1,0:T(8,128)(2,1)S(1)}, u32[]{:S(2)}, u32[]{:S(2)}) %collective-permute-start.1) | collective-permute-done | bytes 213024 | tf_op jit(solution)/shard_map/ppermute | solution.py:292
  22.3 0.0 collective-permute-start.9
  22.3 0.0 collective-permute-done.3
  22.3 1.4 %collective-permute-start.8 = (bf16[832,128]{1,0:T(8,128)(2,1)}, bf16[832,128]{1,0:T(8,128)(2,1)S(1)}, u32[]{:S(2)}, u32[]{:S(2)}) collective-permute-start(bf16[832,128]{1,0:T(8,128)(2,1)} %get-tuple-element.51), channel_id=1, source_target_pairs={{0,2},{1,3},{2,0},{3,1},{4,6},{5,7},{6,4},{7,5},{8,10},{9,11},{10,... | collective-permute-start | bytes 638984 | tf_op jit(solution)/shard_map/ppermute | solution.py:292
  23.7 0.0 copy-start.4
  23.7 0.2 copy.11
  23.9 0.0 collective-permute-done.4
  23.9 0.1 collective-permute-start.10
  24.1 0.2 copy.12
  24.3 0.0 collective-permute-done.refs_1_
  24.3 0.3 copy-done.7
  24.6 2.1 %collective-permute-start.11 = (bf16[832,128]{1,0:T(8,128)(2,1)S(1)}, bf16[832,128]{1,0:T(8,128)(2,1)S(1)}, u32[]{:S(2)}, u32[]{:S(2)}) collective-permute-start(bf16[832,128]{1,0:T(8,128)(2,1)S(1)} %copy-done.7), channel_id=1, source_target_pairs={{0,5},{1,4},{2,7},{3,6},{4,1},{5,0},{6,3},{7,2},{8,13},{9,12},{10,... | collective-permute-start | bytes 638984 | tf_op jit(solution)/shard_map/ppermute | solution.py:292
  26.8 0.0 collective-permute-done.2.refs_3_
  26.8 4.9 %expert.2 = (bf16[832,128]{1,0:T(8,128)(2,1)S(1)}, bf16[832,128]{1,0:T(8,128)(2,1)S(1)}, bf16[832,128]{1,0:T(8,128)(2,1)S(1)}, bf16[832,128]{1,0:T(8,128)(2,1)S(...) custom-call(bf16[832,128]{1,0:T(8,128)(2,1)S(1)} %copy-done.4, ...), custom_call_target="tpu_custom_call" | custom-call | flops 15401484288 | bytes 30802968 | tf_op jit(solution)/shard_map/expert/pallas_call | solution.py:350
  31.7 0.1 collective-permute-start.5
  31.8 0.0 collective-permute-done.9.refs_1_
  31.8 3.1 %collective-permute-start.6 = (bf16[832,128]{1,0:T(8,128)(2,1)S(1)}, bf16[832,128]{1,0:T(8,128)(2,1)S(1)}, u32[]{:S(2)}, u32[]{:S(2)}) collective-permute-start(bf16[832,128]{1,0:T(8,128)(2,1)S(1)} %get-tuple-element.48), channel_id=1, source_target_pairs={{0,6},{1,7},{2,4},{3,5},{4,2},{5,3},{6,0},{7,1},{8,14},{9,15},{10,... | collective-permute-start | bytes 638984 | tf_op jit(solution)/shard_map/ppermute | solution.py:292
  34.9 0.0 collective-permute-done.8.refs_0_
  34.9 0.0 collective-permute-start.7
  34.9 0.0 collective-permute-done.10.refs_2_
  34.9 0.0 collective-permute-done.11.refs_3_
  34.9 6.9 %expert.3 = (bf16[832,128]{1,0:T(8,128)(2,1)S(1)}, bf16[832,128]{1,0:T(8,128)(2,1)S(1)}, bf16[832,128]{1,0:T(8,128)(2,1)S(1)}, bf16[832,128]{1,0:T(8,128)(2,1)S(1)}, bf16[18,128,128]{2,1,0:T(8,128)(2,1)S(1)}) custom-call(bf16[832,128]{1,0:T(8,128)(2,1)S(1)} %collective-permute-done.8.refs_0_, bf16[832,128]{1,0:T(8,128)(2,1)S(1)} %collective-permute-done.9.refs_1_, ...), custom_call_target="tpu_custom_call" | custom-call | flops 15401484288 | bytes 30802968 | tf_op jit(solution)/shard_map/expert/pallas_call | solution.py:350
  41.8 0.0 copy-start
  41.8 0.0 copy-start.3
  41.9 0.0 collective-permute-done.6.refs_2_
  41.9 2.5 %collective-permute-done.7.refs_3_ = bf16[832,128]{1,0:T(8,128)(2,1)S(1)} collective-permute-done((bf16[832,128]{1,0:T(8,128)(2,1)S(1)}, bf16[832,128]{1,0:T(8,128)(2,1)S(1)}, u32[]{:S(2)}, u32[]{:S(2)}) %collective-permute-start.7) | collective-permute-done | bytes 213024 | tf_op jit(solution)/shard_map/ppermute | solution.py:292
  44.4 0.7 %collective-permute-start.16 = (bf16[18,128,128]{2,1,0:T(8,128)(2,1)S(1)}, bf16[18,128,128]{2,1,0:T(8,128)(2,1)S(1)}, u32[]{:S(2)}, u32[]{:S(2)}) collective-permute-start(bf16[18,128,128]{2,1,0:T(8,128)(2,1)S(1)} %get-tuple-element.72), channel_id=1, source_target_pairs={{1,9},{9,1},{3,11},{11,3},{5,13},{13,5},{7,15},{15,7},{17,25},{25,... | collective-permute-start | bytes 1769480 | tf_op jit(solution)/shard_map/ppermute | solution.py:373
  45.1 1.4 %collective-permute-start.12 = (bf16[832,128]{1,0:T(8,128)(2,1)S(1)}, bf16[832,128]{1,0:T(8,128)(2,1)S(1)}, u32[]{:S(2)}, u32[]{:S(2)}) collective-permute-start(bf16[832,128]{1,0:T(8,128)(2,1)S(1)} %get-tuple-element.62), channel_id=1, source_target_pairs={{0,4},{1,5},{2,6},{3,7},{4,0},{5,1},{6,2},{7,3},{8,12},{9,13},{10,... | collective-permute-start | bytes 638984 | tf_op jit(solution)/shard_map/ppermute | solution.py:292
  46.5 1.5 %collective-permute-start.13 = (bf16[832,128]{1,0:T(8,128)(2,1)S(1)}, bf16[832,128]{1,0:T(8,128)(2,1)S(1)}, u32[]{:S(2)}, u32[]{:S(2)}) collective-permute-start(bf16[832,128]{1,0:T(8,128)(2,1)S(1)} %get-tuple-element.64), channel_id=1, source_target_pairs={{0,2},{1,3},{2,0},{3,1},{4,6},{5,7},{6,4},{7,5},{8,10},{9,11},{10,... | collective-permute-start | bytes 638984 | tf_op jit(solution)/shard_map/ppermute | solution.py:292
  48.0 3.5 %collective-permute-start.14 = (bf16[832,128]{1,0:T(8,128)(2,1)S(1)}, bf16[832,128]{1,0:T(8,128)(2,1)S(1)}, u32[]{:S(2)}, u32[]{:S(2)}) collective-permute-start(bf16[832,128]{1,0:T(8,128)(2,1)S(1)} %get-tuple-element.66), channel_id=1, source_target_pairs={{0,5},{1,4},{2,7},{3,6},{4,1},{5,0},{6,3},{7,2},{8,13},{9,12},{10,... | collective-permute-start | bytes 638984 | tf_op jit(solution)/shard_map/ppermute | solution.py:292
  51.5 0.8 %collective-permute-start.15 = (bf16[832,128]{1,0:T(8,128)(2,1)S(1)}, bf16[832,128]{1,0:T(8,128)(2,1)S(1)}, u32[]{:S(2)}, u32[]{:S(2)}) collective-permute-start(bf16[832,128]{1,0:T(8,128)(2,1)S(1)} %get-tuple-element.68), channel_id=1, source_target_pairs={{0,3},{1,2},{2,1},{3,0},{4,7},{5,6},{6,5},{7,4},{8,11},{9,10},{10,... | collective-permute-start | bytes 638984 | tf_op jit(solution)/shard_map/ppermute | solution.py:292
  52.3 1.7 %collective-permute-done.12.refs_4_ = bf16[832,128]{1,0:T(8,128)(2,1)S(1)} collective-permute-done((bf16[832,128]{1,0:T(8,128)(2,1)S(1)}, bf16[832,128]{1,0:T(8,128)(2,1)S(1)}, u32[]{:S(2)}, u32[]{:S(2)}) %collective-permute-start.12) | collective-permute-done | bytes 213024 | tf_op jit(solution)/shard_map/ppermute | solution.py:292
  54.0 0.0 collective-permute-done.13.refs_5_
  54.0 10.2 %collective-permute-done.14.refs_6_ = bf16[832,128]{1,0:T(8,128)(2,1)S(1)} collective-permute-done((bf16[832,128]{1,0:T(8,128)(2,1)S(1)}, bf16[832,128]{1,0:T(8,128)(2,1)S(1)}, u32[]{:S(2)}, u32[]{:S(2)}) %collective-permute-start.14) | collective-permute-done | bytes 213024 | tf_op jit(solution)/shard_map/ppermute | solution.py:292
  64.2 0.0 collective-permute-done.15.refs_7_
  64.2 0.0 collective-permute-done.16
  64.2 0.1 broadcast_select_fusion
  64.3 0.1 collective-permute-start.17
  64.4 2.3 %unpack.1 = (bf16[32,8,8,128]{3,2,1,0:T(8,128)(2,1)}, bf16[18,256,128]{2,1,0:T(8,128)(2,1)}, f32[1,32]{1,0:T(1,128)}) custom-call(bf16[256,256]{1,0:T(8,128)(2,1)S(1)} %copy-done.1, bf16[256,256]{1,0:T(8,128)(2,1)S(1)} %copy-done.2, f32[1,32]{1,0:T(1,128)S(1)} %bitcast.32, bf16[32,8,8,128]{3,2,1,0:T(8,128)(2,1)S(1)} %copy-done, ...), custom_call_target="tpu_custom_call" | custom-call | tf_op jit(solution)/shard_map/unpack/pallas_call | solution.py:379
  66.6 0.1 convert_add_fusion
  66.8 1.1 %fusion = (f32[9,128,128]{2,1,0:T(8,128)}, f32[9,128,128]{2,1,0:T(8,128)}) fusion(f32[18,128,128]{2,1,0:T(8,128)S(1)} %convert_add_fusion), kind=kLoop, calls=%fused_computation.4 | loop fusion | bytes 2359296 | tf_op jit(solution)/shard_map/unstack | solution.py:378
  (17 shorter events, 0.1 us)
Async XLA Ops:
  0.6 23.0 %copy-start.5 = (bf16[1,3,3,128,128]{4,3,2,1,0:T(8,128)(2,1)S(1)}, bf16[1,3,3,128,128]{4,3,2,1,0:T(8,128)(2,1)}, u32[]{:S(2)}) copy-start(bf16[1,3,3,128,128]{4,3,2,1,0:T(8,128)(2,1)} %param.9) | copy-start | bytes 884740
  0.6 12.3 %copy-start.6 = (bf16[1,3,3,128,128]{4,3,2,1,0:T(8,128)(2,1)S(1)}, bf16[1,3,3,128,128]{4,3,2,1,0:T(8,128)(2,1)}, u32[]{:S(2)}) copy-start(bf16[1,3,3,128,128]{4,3,2,1,0:T(8,128)(2,1)} %param.10) | copy-start | bytes 884740
  0.7 21.6 %collective-permute-start.3 = (bf16[3,3,128,128]{3,2,1,0:T(8,128)(2,1)}, bf16[3,3,128,128]{3,2,1,0:T(8,128)(2,1)S(1)}, u32[]{:S(2)}, u32[]{:S(2)}) collective-permute-start(bf16[3,3,128,128]{3,2,1,0:T(8,128)(2,1)} %bitcast.36), channel_id=1, source_target_pairs={{0,9},{8,1},{2,11},{10,3},{4,13},{12,5},{6,15},{14,7},{16,25},{24,... | collective-permute-start | bytes 884744 | tf_op jit(solution)/shard_map/ppermute | solution.py:274
  10.4 13.6 %copy-start.8 = (bf16[832,128]{1,0:T(8,128)(2,1)S(1)}, bf16[832,128]{1,0:T(8,128)(2,1)}, u32[]{:S(2)}) copy-start(bf16[832,128]{1,0:T(8,128)(2,1)} %get-tuple-element.54) | copy-start | bytes 638980
  10.4 11.9 %collective-permute-start.1 = (bf16[832,128]{1,0:T(8,128)(2,1)}, bf16[832,128]{1,0:T(8,128)(2,1)S(1)}, u32[]{:S(2)}, u32[]{:S(2)}) collective-permute-start(bf16[832,128]{1,0:T(8,128)(2,1)} %get-tuple-element.44), channel_id=1, source_target_pairs={{0,6},{1,7},{2,4},{3,5},{4,2},{5,3},{6,0},{7,1},{8,14},{9,15},{10,... | collective-permute-start | bytes 638984 | tf_op jit(solution)/shard_map/ppermute | solution.py:292
  13.0 10.9 %collective-permute-start.4 = (bf16[3,3,128,128]{3,2,1,0:T(8,128)(2,1)S(1)}, bf16[3,3,128,128]{3,2,1,0:T(8,128)(2,1)S(1)}, u32[]{:S(2)}, u32[]{:S(2)}) collective-permute-start(bf16[3,3,128,128]{3,2,1,0:T(8,128)(2,1)S(1)} %bitcast.37), channel_id=1, source_target_pairs={{0,9},{8,1},{2,11},{10,3},{4,13},{12,5},{6,15},{14,7},{16,25},{24,... | collective-permute-start | bytes 884744 | tf_op jit(solution)/shard_map/ppermute | solution.py:274
  14.3 10.0 %collective-permute-start = (bf16[832,128]{1,0:T(8,128)(2,1)}, bf16[832,128]{1,0:T(8,128)(2,1)S(1)}, u32[]{:S(2)}, u32[]{:S(2)}) collective-permute-start(bf16[832,128]{1,0:T(8,128)(2,1)} %get-tuple-element.43), channel_id=1, source_target_pairs={{0,1},{1,0},{2,3},{3,2},{4,5},{5,4},{6,7},{7,6},{8,9},{9,8},{10,11... | collective-permute-start | bytes 638984 | tf_op jit(solution)/shard_map/ppermute | solution.py:292
  14.4 12.4 %collective-permute-start.2 = (bf16[832,128]{1,0:T(8,128)(2,1)}, bf16[832,128]{1,0:T(8,128)(2,1)S(1)}, u32[]{:S(2)}, u32[]{:S(2)}) collective-permute-start(bf16[832,128]{1,0:T(8,128)(2,1)} %get-tuple-element.45), channel_id=1, source_target_pairs={{0,7},{1,6},{2,5},{3,4},{4,3},{5,2},{6,1},{7,0},{8,15},{9,14},{10,... | collective-permute-start | bytes 638984 | tf_op jit(solution)/shard_map/ppermute | solution.py:292
  22.3 9.5 %collective-permute-start.9 = (bf16[832,128]{1,0:T(8,128)(2,1)}, bf16[832,128]{1,0:T(8,128)(2,1)S(1)}, u32[]{:S(2)}, u32[]{:S(2)}) collective-permute-start(bf16[832,128]{1,0:T(8,128)(2,1)} %get-tuple-element.52), channel_id=1, source_target_pairs={{0,4},{1,5},{2,6},{3,7},{4,0},{5,1},{6,2},{7,3},{8,12},{9,13},{10,... | collective-permute-start | bytes 638984 | tf_op jit(solution)/shard_map/ppermute | solution.py:292
  22.3 12.6 %collective-permute-start.8 = (bf16[832,128]{1,0:T(8,128)(2,1)}, bf16[832,128]{1,0:T(8,128)(2,1)S(1)}, u32[]{:S(2)}, u32[]{:S(2)}) collective-permute-start(bf16[832,128]{1,0:T(8,128)(2,1)} %get-tuple-element.51), channel_id=1, source_target_pairs={{0,2},{1,3},{2,0},{3,1},{4,6},{5,7},{6,4},{7,5},{8,10},{9,11},{10,... | collective-permute-start | bytes 638984 | tf_op jit(solution)/shard_map/ppermute | solution.py:292
  23.7 0.9 %copy-start.7 = (bf16[832,128]{1,0:T(8,128)(2,1)S(1)}, bf16[832,128]{1,0:T(8,128)(2,1)}, u32[]{:S(2)}) copy-start(bf16[832,128]{1,0:T(8,128)(2,1)} %get-tuple-element.56) | copy-start | bytes 638980
  23.7 3.1 %copy-start.4 = (bf16[832,128]{1,0:T(8,128)(2,1)S(1)}, bf16[832,128]{1,0:T(8,128)(2,1)}, u32[]{:S(2)}) copy-start(bf16[832,128]{1,0:T(8,128)(2,1)} %get-tuple-element.42.refs_0_) | copy-start | bytes 638980
  23.9 10.9 %collective-permute-start.10 = (bf16[832,128]{1,0:T(8,128)(2,1)S(1)}, bf16[832,128]{1,0:T(8,128)(2,1)S(1)}, u32[]{:S(2)}, u32[]{:S(2)}) collective-permute-start(bf16[832,128]{1,0:T(8,128)(2,1)S(1)} %copy-done.8), channel_id=1, source_target_pairs={{0,3},{1,2},{2,1},{3,0},{4,7},{5,6},{6,5},{7,4},{8,11},{9,10},{10,... | collective-permute-start | bytes 638984 | tf_op jit(solution)/shard_map/ppermute | solution.py:292
  24.6 10.3 %collective-permute-start.11 = (bf16[832,128]{1,0:T(8,128)(2,1)S(1)}, bf16[832,128]{1,0:T(8,128)(2,1)S(1)}, u32[]{:S(2)}, u32[]{:S(2)}) collective-permute-start(bf16[832,128]{1,0:T(8,128)(2,1)S(1)} %copy-done.7), channel_id=1, source_target_pairs={{0,5},{1,4},{2,7},{3,6},{4,1},{5,0},{6,3},{7,2},{8,13},{9,12},{10,... | collective-permute-start | bytes 638984 | tf_op jit(solution)/shard_map/ppermute | solution.py:292
  31.7 10.2 %collective-permute-start.5 = (bf16[832,128]{1,0:T(8,128)(2,1)S(1)}, bf16[832,128]{1,0:T(8,128)(2,1)S(1)}, u32[]{:S(2)}, u32[]{:S(2)}) collective-permute-start(bf16[832,128]{1,0:T(8,128)(2,1)S(1)} %get-tuple-element.47), channel_id=1, source_target_pairs={{0,1},{1,0},{2,3},{3,2},{4,5},{5,4},{6,7},{7,6},{8,9},{9,8},{10,11... | collective-permute-start | bytes 638984 | tf_op jit(solution)/shard_map/ppermute | solution.py:292
  31.8 10.1 %collective-permute-start.6 = (bf16[832,128]{1,0:T(8,128)(2,1)S(1)}, bf16[832,128]{1,0:T(8,128)(2,1)S(1)}, u32[]{:S(2)}, u32[]{:S(2)}) collective-permute-start(bf16[832,128]{1,0:T(8,128)(2,1)S(1)} %get-tuple-element.48), channel_id=1, source_target_pairs={{0,6},{1,7},{2,4},{3,5},{4,2},{5,3},{6,0},{7,1},{8,14},{9,15},{10,... | collective-permute-start | bytes 638984 | tf_op jit(solution)/shard_map/ppermute | solution.py:292
  34.9 9.5 %collective-permute-start.7 = (bf16[832,128]{1,0:T(8,128)(2,1)S(1)}, bf16[832,128]{1,0:T(8,128)(2,1)S(1)}, u32[]{:S(2)}, u32[]{:S(2)}) collective-permute-start(bf16[832,128]{1,0:T(8,128)(2,1)S(1)} %get-tuple-element.49), channel_id=1, source_target_pairs={{0,7},{1,6},{2,5},{3,4},{4,3},{5,2},{6,1},{7,0},{8,15},{9,14},{10,... | collective-permute-start | bytes 638984 | tf_op jit(solution)/shard_map/ppermute | solution.py:292
  41.8 22.5 %copy-start = (bf16[32,8,8,128]{3,2,1,0:T(8,128)(2,1)S(1)}, bf16[32,8,8,128]{3,2,1,0:T(8,128)(2,1)}, u32[]{:S(2)}) copy-start(bf16[32,8,8,128]{3,2,1,0:T(8,128)(2,1)} %cot_ref.1) | copy-start | bytes 1572868
  41.8 22.5 %copy-start.1 = (bf16[256,256]{1,0:T(8,128)(2,1)S(1)}, bf16[256,256]{1,0:T(8,128)(2,1)}, u32[]{:S(2)}) copy-start(bf16[256,256]{1,0:T(8,128)(2,1)} %get-tuple-element.40.pick_ref) | copy-start | bytes 393220
  41.8 22.5 %copy-start.2 = (bf16[256,256]{1,0:T(8,128)(2,1)S(1)}, bf16[256,256]{1,0:T(8,128)(2,1)}, u32[]{:S(2)}) copy-start(bf16[256,256]{1,0:T(8,128)(2,1)} %get-tuple-element.41.cot_pick_ref) | copy-start | bytes 393220
  41.8 22.5 %copy-start.3 = (f32[32]{0:T(128)S(1)}, f32[32]{0:T(128)}, u32[]{:S(2)}) copy-start(f32[32]{0:T(128)} %param.8) | copy-start | bytes 388
  44.4 19.8 %collective-permute-start.16 = (bf16[18,128,128]{2,1,0:T(8,128)(2,1)S(1)}, bf16[18,128,128]{2,1,0:T(8,128)(2,1)S(1)}, u32[]{:S(2)}, u32[]{:S(2)}) collective-permute-start(bf16[18,128,128]{2,1,0:T(8,128)(2,1)S(1)} %get-tuple-element.72), channel_id=1, source_target_pairs={{1,9},{9,1},{3,11},{11,3},{5,13},{13,5},{7,15},{15,7},{17,25},{25,... | collective-permute-start | bytes 1769480 | tf_op jit(solution)/shard_map/ppermute | solution.py:373
  45.1 8.9 %collective-permute-start.12 = (bf16[832,128]{1,0:T(8,128)(2,1)S(1)}, bf16[832,128]{1,0:T(8,128)(2,1)S(1)}, u32[]{:S(2)}, u32[]{:S(2)}) collective-permute-start(bf16[832,128]{1,0:T(8,128)(2,1)S(1)} %get-tuple-element.62), channel_id=1, source_target_pairs={{0,4},{1,5},{2,6},{3,7},{4,0},{5,1},{6,2},{7,3},{8,12},{9,13},{10,... | collective-permute-start | bytes 638984 | tf_op jit(solution)/shard_map/ppermute | solution.py:292
  46.5 7.5 %collective-permute-start.13 = (bf16[832,128]{1,0:T(8,128)(2,1)S(1)}, bf16[832,128]{1,0:T(8,128)(2,1)S(1)}, u32[]{:S(2)}, u32[]{:S(2)}) collective-permute-start(bf16[832,128]{1,0:T(8,128)(2,1)S(1)} %get-tuple-element.64), channel_id=1, source_target_pairs={{0,2},{1,3},{2,0},{3,1},{4,6},{5,7},{6,4},{7,5},{8,10},{9,11},{10,... | collective-permute-start | bytes 638984 | tf_op jit(solution)/shard_map/ppermute | solution.py:292
  48.0 16.1 %collective-permute-start.14 = (bf16[832,128]{1,0:T(8,128)(2,1)S(1)}, bf16[832,128]{1,0:T(8,128)(2,1)S(1)}, u32[]{:S(2)}, u32[]{:S(2)}) collective-permute-start(bf16[832,128]{1,0:T(8,128)(2,1)S(1)} %get-tuple-element.66), channel_id=1, source_target_pairs={{0,5},{1,4},{2,7},{3,6},{4,1},{5,0},{6,3},{7,2},{8,13},{9,12},{10,... | collective-permute-start | bytes 638984 | tf_op jit(solution)/shard_map/ppermute | solution.py:292
  51.5 12.6 %collective-permute-start.15 = (bf16[832,128]{1,0:T(8,128)(2,1)S(1)}, bf16[832,128]{1,0:T(8,128)(2,1)S(1)}, u32[]{:S(2)}, u32[]{:S(2)}) collective-permute-start(bf16[832,128]{1,0:T(8,128)(2,1)S(1)} %get-tuple-element.68), channel_id=1, source_target_pairs={{0,3},{1,2},{2,1},{3,0},{4,7},{5,6},{6,5},{7,4},{8,11},{9,10},{10,... | collective-permute-start | bytes 638984 | tf_op jit(solution)/shard_map/ppermute | solution.py:292
  64.3 2.4 %collective-permute-start.17 = (bf16[18,128,128]{2,1,0:T(8,128)(2,1)S(1)}, bf16[18,128,128]{2,1,0:T(8,128)(2,1)S(1)}, u32[]{:S(2)}, u32[]{:S(2)}) collective-permute-start(bf16[18,128,128]{2,1,0:T(8,128)(2,1)S(1)} %broadcast_select_fusion), channel_id=1, source_target_pairs={{0,1},{1,0},{2,3},{3,2},{4,5},{5,4},{6,7},{7,6},{8,9},{9,8},{10,11... | collective-permute-start | bytes 1769480 | tf_op jit(solution)/shard_map/ppermute | solution.py:376
